TPU v7x, 32 devices: a whole 2x2x4 slice. The times are simulated.
32 devices in a mesh: grp: 8 (over z, y), cand: 4 (over x, core).
Axes of the slice: x: 2, y: 2, z: 4, core: 2. Of those that a mesh axis runs over, the one named last changes fastest.
Arguments:
- history: bfloat16 [32, 1024, 256], P(('grp', 'cand')), may hold values from -9 to 9
- lengths: int32 [32], P(('grp', 'cand')), may hold values from 128 to 1024
- target: bfloat16 [32, 32, 256], P('grp', 'cand'), may hold values from -6 to 6
- bag_ids: int32 [32, 32, 8, 4], P('grp', 'cand'), may hold values from 0 to 32767
- leaf_ids: int32 [32, 32, 64], P('grp', 'cand'), may hold values from 0 to 31
- table_piece: bfloat16 [32, 8192, 128], P(('grp', 'cand')), may hold values from -6 to 6
- leaf_table: bfloat16 [64, 32, 256], replicated, may hold values from -0.75 to 0.75
- w_query: bfloat16 [256, 128], replicated, may hold values from -0.375 to 0.375
- w_key: bfloat16 [256, 128], replicated, may hold values from -0.375 to 0.375
- w_pair: bfloat16 [256, 128], replicated, may hold values from -0.375 to 0.375
- a_out: bfloat16 [128], replicated, may hold values from -1 to 1
- w_first: bfloat16 [1792, 1024], replicated, may hold values from -0.125 to 0.125
- w_second: bfloat16 [1024, 512], replicated, may hold values from -0.25 to 0.25
- w_third: bfloat16 [512, 256], replicated, may hold values from -0.375 to 0.375
- w_out: bfloat16 [256], replicated, may hold values from -0.5 to 0.5
Outputs:
- logits: float32 [32, 32], P('grp', 'cand')
All inputs are finite; a program needn't handle non-finite values.
Results may differ from a plain program's by a relative error of at most 0.0092.
Values may be sent and summed in bfloat16 or wider, within the bound.
No kernel may reach another device: no remote copies, remote signals or barrier semaphores. Data moves between devices by JAX's collectives and lax.ppermute only.
A program may use at most 128 MiB of HBM per device.

v0:
```python
import math

import jax
import jax.numpy as jnp
from jax import lax
from jax.sharding import PartitionSpec as P

SPLIT = 4


def interest_of(queries, history_rows, length, w_query, w_key, w_pair, a_out):
    n_items = queries.shape[0]
    block_size = math.gcd(n_items, 32)
    k_part = jnp.dot(history_rows, w_key, preferred_element_type=jnp.float32).T
    live_mask = jnp.arange(history_rows.shape[0], dtype=jnp.int32) < length
    pair_rows = w_pair.T.astype(jnp.float32)
    a_vector = a_out.astype(jnp.float32)

    def one_block(q_block):
        q_part = jnp.dot(q_block, w_query, preferred_element_type=jnp.float32)
        scaled = (q_block.astype(jnp.float32)[:, None, :] * pair_rows[None]).astype(jnp.bfloat16)
        raw_pair = lax.dot_general(
            scaled.reshape(-1, scaled.shape[2]),
            history_rows,
            (((1,), (1,)), ((), ())),
            preferred_element_type=jnp.float32,
        )
        raw_pair = raw_pair.reshape(q_block.shape[0], pair_rows.shape[0], history_rows.shape[0])
        unit_act = jax.nn.relu(raw_pair + q_part[:, :, None] + k_part[None])
        scores = jnp.einsum("bak,a->bk", unit_act, a_vector, precision=lax.Precision.HIGHEST)
        scores = jnp.where(live_mask[None], scores, 0.0).astype(jnp.bfloat16)
        return jnp.dot(scores, history_rows, preferred_element_type=jnp.float32)

    weighted = lax.map(
        one_block, queries.reshape(n_items // block_size, block_size, queries.shape[1])
    )
    inv_root = 1.0 / jnp.sqrt(length.astype(jnp.float32))
    return (weighted.reshape(n_items, -1) * inv_root).astype(jnp.bfloat16)


def leaf_embed(leaf_rows, leaf_table):
    tree_count, leaf_count, feat_width = leaf_table.shape
    one_hot = (leaf_rows[..., None] == jnp.arange(leaf_count, dtype=jnp.int32)).astype(jnp.bfloat16)
    one_hot = one_hot.reshape(leaf_rows.shape[0], tree_count * leaf_count)
    return jnp.dot(
        one_hot,
        leaf_table.reshape(tree_count * leaf_count, feat_width),
        preferred_element_type=jnp.float32,
    ).astype(jnp.bfloat16)


def pool_piece(offsets, rows_of):
    lookups, bag_size = offsets.shape
    piece_rows, emb_width = rows_of.shape
    block_cols = math.gcd(piece_rows, 1024)
    col_base = jnp.arange(block_cols, dtype=jnp.int32)

    def add_block(block_idx, total):
        start = (block_idx * block_cols).astype(jnp.int32)
        columns = col_base + start
        counts = jnp.zeros((lookups, block_cols), jnp.bfloat16)
        for bag_slot in range(bag_size):
            counts = counts + (offsets[:, bag_slot, None] == columns[None]).astype(jnp.bfloat16)
        block_rows = lax.dynamic_slice_in_dim(rows_of, start, block_cols, 0)
        return total + jnp.dot(counts, block_rows, preferred_element_type=jnp.float32)

    empty = jnp.zeros((lookups, emb_width), jnp.float32)
    return lax.fori_loop(0, piece_rows // block_cols, add_block, empty)


def on_device(
    history,
    lengths,
    target,
    bag_ids,
    leaf_ids,
    table_piece,
    leaf_table,
    w_query,
    w_key,
    w_pair,
    a_out,
    w_first,
    w_second,
    w_third,
    w_out,
):
    req_count, per_req, feat_width = target.shape
    local_rows = req_count * per_req
    history_all, lengths_all = (
        lax.all_gather(history, "cand", axis=0, tiled=True),
        lax.all_gather(lengths, "cand", axis=0, tiled=True),
    )

    def one_request(inputs):
        return interest_of(inputs[0], inputs[1], inputs[2], w_query, w_key, w_pair, a_out)

    interest = lax.map(one_request, (target, history_all, lengths_all))
    devices = lax.axis_size(("grp", "cand"))
    tables = devices // SPLIT
    bag_size = bag_ids.shape[3]
    emb_width = table_piece.shape[2]
    piece_rows = table_piece.shape[1]
    bag_rows = jnp.transpose(bag_ids.reshape(local_rows, tables, bag_size), (1, 2, 0))
    outgoing = jnp.repeat(bag_rows, SPLIT, axis=0)
    incoming = lax.all_to_all(outgoing, ("grp", "cand"), split_axis=0, concat_axis=0, tiled=True)
    quarter = lax.axis_index(("grp", "cand")) % SPLIT
    offsets = incoming - quarter * piece_rows
    flat_offsets = jnp.transpose(offsets, (0, 2, 1)).reshape(devices * local_rows, bag_size)
    running = pool_piece(flat_offsets, table_piece[0])
    partial_value = running.astype(jnp.bfloat16).reshape(devices, local_rows, emb_width)
    returned = lax.all_to_all(
        partial_value, ("grp", "cand"), split_axis=0, concat_axis=0, tiled=True
    )
    pooled = jnp.sum(
        returned.reshape(tables, SPLIT, local_rows, emb_width), axis=1, dtype=jnp.float32
    ).astype(jnp.bfloat16)
    leaf_vec = leaf_embed(leaf_ids.reshape(local_rows, -1), leaf_table)
    table_width = tables * emb_width
    hidden_one = jnp.einsum(
        "tne,teh->nh",
        pooled,
        w_first[:table_width].reshape(tables, emb_width, -1),
        preferred_element_type=jnp.float32,
    )
    tail_feats = jnp.concatenate(
        [
            interest.reshape(local_rows, feat_width),
            target.reshape(local_rows, feat_width),
            leaf_vec,
        ],
        axis=1,
    )
    hidden_one = hidden_one + jnp.dot(
        tail_feats, w_first[table_width:], preferred_element_type=jnp.float32
    )
    hidden_one = jax.nn.relu(hidden_one).astype(jnp.bfloat16)
    hidden_two = jax.nn.relu(
        jnp.dot(hidden_one, w_second, preferred_element_type=jnp.float32)
    ).astype(jnp.bfloat16)
    hidden_three = jax.nn.relu(
        jnp.dot(hidden_two, w_third, preferred_element_type=jnp.float32)
    ).astype(jnp.bfloat16)
    logits = jnp.dot(hidden_three, w_out, preferred_element_type=jnp.float32)
    return logits.reshape(req_count, per_req)


def solution(mesh):
    placed = (
        P(("grp", "cand"), None, None),
        P(("grp", "cand")),
        P("grp", "cand", None),
        P("grp", "cand", None, None),
        P("grp", "cand", None),
        P(("grp", "cand"), None, None),
        P(),
        P(),
        P(),
        P(),
        P(),
        P(),
        P(),
        P(),
        P(),
    )
    return jax.shard_map(
        on_device, mesh=mesh, in_specs=placed, out_specs=P("grp", "cand"), check_vma=False
    )
```

profile of v0, /device:TPU:0, one launch (start us, length us, event | category | flops | bytes accessed | tf_op | source)
XLA Modules:
  0.0 108.2 jit_solution(16766396111825830846)
XLA Ops:
  6.5 1.0 copy.21
  7.6 0.7 reshape.81
  8.3 7.3 %all-to-all-start = ((s32[32,1,128]{2,1,0:T(1,128)}), s32[32,1,128]{2,1,0:T(1,128)S(1)}, u32[]{:S(2)}, u32[]{:S(2)}) async-start(s32[32,1,128]{2,1,0:T(1,128)} %reshape.81), calls=%async_computation | async-start | bytes 32768 | tf_op jit(solution)/shard_map/all_to_all | solution.py:106
  15.6 0.7 all-gather.2.cloned.1.call-update
  16.3 6.4 %all-to-all-done = s32[32,1,128]{2,1,0:T(1,128)S(1)} async-done(((s32[32,1,128]{2,1,0:T(1,128)}), s32[32,1,128]{2,1,0:T(1,128)S(1)}, u32[]{:S(2)}, u32[]{:S(2)}) %all-to-all-start) | async-done | bytes 16416 | tf_op jit(solution)/shard_map/all_to_all | solution.py:106
  22.7 0.5 broadcast.26
  23.2 0.6 reduce.1
  23.8 0.1 reshape.82
  23.9 0.1 reshape.62
  24.1 22.6 %while.29 = (s32[]{:T(128)}, f32[1024,128]{1,0:T(8,128)S(1)}, s32[1024,4]{0,1:T(4,128)S(1)}, bf16[8192,128]{1,0:T(8,128)(2,1)}, s32[]{:T(128)}, /*index=5*/s32[]{:T(128)}, s32[]{:T(128)}, s32[]{:T(128)}) while((s32[]{:T(128)}, f32[1024,128]{1,0:T(8,128)S(1)}, s32[1024,4]{0,1:T(4,128)S(1)}, bf16[8192,128]{1,0:T(8,128)(2,1)}, ...), condition=%wide.region_1.2_spmd.clone, body=%wide.region_0.1_spmd.clone.sunk | while | flops 280232960 | bytes 1368221 | solution.py:68
  24.1 2.8 %fusion.115 = f32[1024,128]{1,0:T(8,128)S(1)} fusion(s32[1024]{0:T(1024)S(1)} %iota_add_fusion.2, s32[1024]{0:T(1024)S(1)} %bitcast.117, s32[1024]{0:T(1024)S(1)} %bitcast.118, s32[1024]{0:T(1024)S(1)} %bitcast.119, s32[1024]{0:T(1024)S(1)} %bitcast.116, f32[1024,128]{1,0:T(8,128)S(1)} %get-tuple-element.358, ...), kind=kOutput, calls=%fused_computation.52.clone.1 | convolution fusion | flops 280231936 | bytes 1331205 | tf_op jit(solution)/shard_map/while/body/eval_jaxpr/dot_general | solution.py:65
  27.0 2.8 %fusion.115 = f32[1024,128]{1,0:T(8,128)S(1)} fusion(s32[1024]{0:T(1024)S(1)} %iota_add_fusion.2, s32[1024]{0:T(1024)S(1)} %bitcast.117, s32[1024]{0:T(1024)S(1)} %bitcast.118, s32[1024]{0:T(1024)S(1)} %bitcast.119, s32[1024]{0:T(1024)S(1)} %bitcast.116, f32[1024,128]{1,0:T(8,128)S(1)} %get-tuple-element.358, ...), kind=kOutput, calls=%fused_computation.52.clone.1 | convolution fusion | flops 280231936 | bytes 1331205 | tf_op jit(solution)/shard_map/while/body/eval_jaxpr/dot_general | solution.py:65
  29.8 2.8 %fusion.115 = f32[1024,128]{1,0:T(8,128)S(1)} fusion(s32[1024]{0:T(1024)S(1)} %iota_add_fusion.2, s32[1024]{0:T(1024)S(1)} %bitcast.117, s32[1024]{0:T(1024)S(1)} %bitcast.118, s32[1024]{0:T(1024)S(1)} %bitcast.119, s32[1024]{0:T(1024)S(1)} %bitcast.116, f32[1024,128]{1,0:T(8,128)S(1)} %get-tuple-element.358, ...), kind=kOutput, calls=%fused_computation.52.clone.1 | convolution fusion | flops 280231936 | bytes 1331205 | tf_op jit(solution)/shard_map/while/body/eval_jaxpr/dot_general | solution.py:65
  32.6 2.8 %fusion.115 = f32[1024,128]{1,0:T(8,128)S(1)} fusion(s32[1024]{0:T(1024)S(1)} %iota_add_fusion.2, s32[1024]{0:T(1024)S(1)} %bitcast.117, s32[1024]{0:T(1024)S(1)} %bitcast.118, s32[1024]{0:T(1024)S(1)} %bitcast.119, s32[1024]{0:T(1024)S(1)} %bitcast.116, f32[1024,128]{1,0:T(8,128)S(1)} %get-tuple-element.358, ...), kind=kOutput, calls=%fused_computation.52.clone.1 | convolution fusion | flops 280231936 | bytes 1331205 | tf_op jit(solution)/shard_map/while/body/eval_jaxpr/dot_general | solution.py:65
  35.4 2.8 %fusion.115 = f32[1024,128]{1,0:T(8,128)S(1)} fusion(s32[1024]{0:T(1024)S(1)} %iota_add_fusion.2, s32[1024]{0:T(1024)S(1)} %bitcast.117, s32[1024]{0:T(1024)S(1)} %bitcast.118, s32[1024]{0:T(1024)S(1)} %bitcast.119, s32[1024]{0:T(1024)S(1)} %bitcast.116, f32[1024,128]{1,0:T(8,128)S(1)} %get-tuple-element.358, ...), kind=kOutput, calls=%fused_computation.52.clone.1 | convolution fusion | flops 280231936 | bytes 1331205 | tf_op jit(solution)/shard_map/while/body/eval_jaxpr/dot_general | solution.py:65
  38.3 2.8 %fusion.115 = f32[1024,128]{1,0:T(8,128)S(1)} fusion(s32[1024]{0:T(1024)S(1)} %iota_add_fusion.2, s32[1024]{0:T(1024)S(1)} %bitcast.117, s32[1024]{0:T(1024)S(1)} %bitcast.118, s32[1024]{0:T(1024)S(1)} %bitcast.119, s32[1024]{0:T(1024)S(1)} %bitcast.116, f32[1024,128]{1,0:T(8,128)S(1)} %get-tuple-element.358, ...), kind=kOutput, calls=%fused_computation.52.clone.1 | convolution fusion | flops 280231936 | bytes 1331205 | tf_op jit(solution)/shard_map/while/body/eval_jaxpr/dot_general | solution.py:65
  41.1 2.8 %fusion.115 = f32[1024,128]{1,0:T(8,128)S(1)} fusion(s32[1024]{0:T(1024)S(1)} %iota_add_fusion.2, s32[1024]{0:T(1024)S(1)} %bitcast.117, s32[1024]{0:T(1024)S(1)} %bitcast.118, s32[1024]{0:T(1024)S(1)} %bitcast.119, s32[1024]{0:T(1024)S(1)} %bitcast.116, f32[1024,128]{1,0:T(8,128)S(1)} %get-tuple-element.358, ...), kind=kOutput, calls=%fused_computation.52.clone.1 | convolution fusion | flops 280231936 | bytes 1331205 | tf_op jit(solution)/shard_map/while/body/eval_jaxpr/dot_general | solution.py:65
  43.9 2.8 %fusion.115 = f32[1024,128]{1,0:T(8,128)S(1)} fusion(s32[1024]{0:T(1024)S(1)} %iota_add_fusion.2, s32[1024]{0:T(1024)S(1)} %bitcast.117, s32[1024]{0:T(1024)S(1)} %bitcast.118, s32[1024]{0:T(1024)S(1)} %bitcast.119, s32[1024]{0:T(1024)S(1)} %bitcast.116, f32[1024,128]{1,0:T(8,128)S(1)} %get-tuple-element.358, ...), kind=kOutput, calls=%fused_computation.52.clone.1 | convolution fusion | flops 280231936 | bytes 1331205 | tf_op jit(solution)/shard_map/while/body/eval_jaxpr/dot_general | solution.py:65
  46.7 0.7 convert_element_type.81
  47.4 2.6 %all-to-all-start.1 = ((bf16[32,32,128]{2,1,0:T(8,128)(2,1)}), bf16[32,32,128]{2,1,0:T(8,128)(2,1)S(1)}, u32[]{:S(2)}, u32[]{:S(2)}) async-start(bf16[32,32,128]{2,1,0:T(8,128)(2,1)} %bitcast.14), calls=%async_computation.1 | async-start | bytes 524288 | tf_op jit(solution)/shard_map/all_to_all | solution.py:112
  50.6 0.6 dynamic-slice
  51.2 0.7 dynamic-update-slice
  51.9 5.0 %all-reduce = s32[4]{0:T(128)S(1)} all-reduce(s32[4]{0:T(128)S(1)} %dynamic-update-slice), channel_id=1, replica_groups=mesh['grp'=8,'cand'=4] {'cand'}, use_global_device_ids=true, to_apply=%add | all-reduce | flops 4 | bytes 32
  56.9 0.1 copy.24
  57.0 0.1 copy.23
  57.2 3.2 %slice.34 = bf16[1024,1024]{1,0:T(8,128)(2,1)} slice(bf16[1792,1024]{1,0:T(8,128)(2,1)} %param.30), slice={[0:1024], [0:1024]} | slice | bytes 4194304 | tf_op jit(solution)/shard_map/slice | solution.py:123
  60.4 0.7 fusion.57
  61.2 35.2 %while.28 = (s32[]{:T(128)}, bf16[4,8,256]{2,1,0:T(8,128)(2,1)S(1)}, s32[4]{0:T(128)S(1)}, bf16[4,8,256]{2,1,0:T(8,128)(2,1)S(1)}, bf16[256,128]{0,1:T(8,128)(2,...) while((s32[]{:T(128)}, ...), condition=%wide.region_4.5_spmd, body=%wide.region_3.4_spmd.sunk | while | flops 624999424 | bytes 12607389 | solution.py:98
  61.2 0.7 dynamic_slice.54
  62.6 0.7 iota_compare_fusion.4
  63.3 0.1 fusion.109
  63.4 1.3 %convolution_bitcast_fusion.4 = f32[128,1024]{0,1:T(8,128)S(1)} fusion(bf16[256,128]{1,0:T(8,128)(2,1)S(1)} %get-tuple-element.346, bf16[4,1024,256]{2,1,0:T(8,128)(2,1)} %get-tuple-element.344, s32[]{:T(128)S(6)} %copy.36), kind=kOutput, calls=%fused_computation.8.clone.1 | convolution fusion | flops 67108864 | bytes 1114116 | tf_op jit(solution)/shard_map/while/body/eval_jaxpr/dot_general | solution.py:14
  64.8 0.2 copy.31
  65.0 1.8 %fusion.108 = f32[8,128,1024]{2,1,0:T(8,128)S(1)} fusion(f32[128,256]{1,0:T(8,128)S(1)} %convert_bitcast_fusion.2, f32[8,256]{1,0:T(8,128)S(1)} %bitcast_convert_fusion.2, bf16[4,1024,256]{2,1,0:T(8,128)(2,1)} %get-tuple-element.344, s32[]{:T(128)S(6)} %copy.36), kind=kOutput, calls=%fused_computation.14.clone.1 | convolution fusion | flops 537395200 | bytes 4857860 | tf_op jit(solution)/shard_map/while/body/eval_jaxpr/while/body/eval_jaxpr/dot_general | solution.py:22
  66.8 2.0 %fusion.110 = bf16[1,8,1024]{2,0,1:T(2,128)(2,1)S(1)} fusion(f32[8,128,1024]{2,1,0:T(8,128)S(1)} %fusion.108, f32[128,1024]{1,0:T(8,128)S(1)} %copy.31, f32[8,128]{1,0:T(8,128)S(1)} %fusion.109, bf16[128]{0:T(256)(128)(2,1)S(1)} %get-tuple-element.347), kind=kOutput, calls=%fused_computation.1.clone.1 | convolution fusion | flops 15728640 | bytes 4739328 | tf_op jit(solution)/shard_map/while/body/eval_jaxpr/while/body/eval_jaxpr/bak,a->bk/dot_general | solution.py:30
  68.7 1.2 %fusion.111 = bf16[4,8,256]{2,1,0:T(8,128)(2,1)S(1)} fusion(bf16[4,8,256]{2,1,0:T(8,128)(2,1)S(1)} %get-tuple-element.330, s32[]{:T(128)S(6)} %copy.36, bf16[4,1024,256]{2,1,0:T(8,128)(2,1)} %get-tuple-element.344, bf16[1,8,1024]{2,0,1:T(2,128)(2,1)S(1)} %fusion.110, pred[1024]{0:T(1024)(128)(4,1)S(1)} %iota_compare_fusion.4, f32[]{:T(128)S(6)} %sqrt.4), kind=kOutput, calls=%fused_computation.12.clone.1 | convolution fusion | flops 4206592 | bytes 563712 | tf_op jit(solution)/shard_map/while/body/eval_jaxpr/while/body/eval_jaxpr/dot_general | solution.py:32
  70.0 0.7 dynamic_slice.54
  71.4 0.7 iota_compare_fusion.4
  72.1 0.1 fusion.109
  72.2 1.3 %convolution_bitcast_fusion.4 = f32[128,1024]{0,1:T(8,128)S(1)} fusion(bf16[256,128]{1,0:T(8,128)(2,1)S(1)} %get-tuple-element.346, bf16[4,1024,256]{2,1,0:T(8,128)(2,1)} %get-tuple-element.344, s32[]{:T(128)S(6)} %copy.36), kind=kOutput, calls=%fused_computation.8.clone.1 | convolution fusion | flops 67108864 | bytes 1114116 | tf_op jit(solution)/shard_map/while/body/eval_jaxpr/dot_general | solution.py:14
  73.6 0.2 copy.31
  73.8 1.8 %fusion.108 = f32[8,128,1024]{2,1,0:T(8,128)S(1)} fusion(f32[128,256]{1,0:T(8,128)S(1)} %convert_bitcast_fusion.2, f32[8,256]{1,0:T(8,128)S(1)} %bitcast_convert_fusion.2, bf16[4,1024,256]{2,1,0:T(8,128)(2,1)} %get-tuple-element.344, s32[]{:T(128)S(6)} %copy.36), kind=kOutput, calls=%fused_computation.14.clone.1 | convolution fusion | flops 537395200 | bytes 4857860 | tf_op jit(solution)/shard_map/while/body/eval_jaxpr/while/body/eval_jaxpr/dot_general | solution.py:22
  75.6 2.0 %fusion.110 = bf16[1,8,1024]{2,0,1:T(2,128)(2,1)S(1)} fusion(f32[8,128,1024]{2,1,0:T(8,128)S(1)} %fusion.108, f32[128,1024]{1,0:T(8,128)S(1)} %copy.31, f32[8,128]{1,0:T(8,128)S(1)} %fusion.109, bf16[128]{0:T(256)(128)(2,1)S(1)} %get-tuple-element.347), kind=kOutput, calls=%fused_computation.1.clone.1 | convolution fusion | flops 15728640 | bytes 4739328 | tf_op jit(solution)/shard_map/while/body/eval_jaxpr/while/body/eval_jaxpr/bak,a->bk/dot_general | solution.py:30
  77.5 1.2 %fusion.111 = bf16[4,8,256]{2,1,0:T(8,128)(2,1)S(1)} fusion(bf16[4,8,256]{2,1,0:T(8,128)(2,1)S(1)} %get-tuple-element.330, s32[]{:T(128)S(6)} %copy.36, bf16[4,1024,256]{2,1,0:T(8,128)(2,1)} %get-tuple-element.344, bf16[1,8,1024]{2,0,1:T(2,128)(2,1)S(1)} %fusion.110, pred[1024]{0:T(1024)(128)(4,1)S(1)} %iota_compare_fusion.4, f32[]{:T(128)S(6)} %sqrt.4), kind=kOutput, calls=%fused_computation.12.clone.1 | convolution fusion | flops 4206592 | bytes 563712 | tf_op jit(solution)/shard_map/while/body/eval_jaxpr/while/body/eval_jaxpr/dot_general | solution.py:32
  78.7 0.7 dynamic_slice.54
  80.2 0.7 iota_compare_fusion.4
  80.9 0.1 fusion.109
  81.0 1.3 %convolution_bitcast_fusion.4 = f32[128,1024]{0,1:T(8,128)S(1)} fusion(bf16[256,128]{1,0:T(8,128)(2,1)S(1)} %get-tuple-element.346, bf16[4,1024,256]{2,1,0:T(8,128)(2,1)} %get-tuple-element.344, s32[]{:T(128)S(6)} %copy.36), kind=kOutput, calls=%fused_computation.8.clone.1 | convolution fusion | flops 67108864 | bytes 1114116 | tf_op jit(solution)/shard_map/while/body/eval_jaxpr/dot_general | solution.py:14
  82.4 0.2 copy.31
  82.6 1.8 %fusion.108 = f32[8,128,1024]{2,1,0:T(8,128)S(1)} fusion(f32[128,256]{1,0:T(8,128)S(1)} %convert_bitcast_fusion.2, f32[8,256]{1,0:T(8,128)S(1)} %bitcast_convert_fusion.2, bf16[4,1024,256]{2,1,0:T(8,128)(2,1)} %get-tuple-element.344, s32[]{:T(128)S(6)} %copy.36), kind=kOutput, calls=%fused_computation.14.clone.1 | convolution fusion | flops 537395200 | bytes 4857860 | tf_op jit(solution)/shard_map/while/body/eval_jaxpr/while/body/eval_jaxpr/dot_general | solution.py:22
  84.4 2.0 %fusion.110 = bf16[1,8,1024]{2,0,1:T(2,128)(2,1)S(1)} fusion(f32[8,128,1024]{2,1,0:T(8,128)S(1)} %fusion.108, f32[128,1024]{1,0:T(8,128)S(1)} %copy.31, f32[8,128]{1,0:T(8,128)S(1)} %fusion.109, bf16[128]{0:T(256)(128)(2,1)S(1)} %get-tuple-element.347), kind=kOutput, calls=%fused_computation.1.clone.1 | convolution fusion | flops 15728640 | bytes 4739328 | tf_op jit(solution)/shard_map/while/body/eval_jaxpr/while/body/eval_jaxpr/bak,a->bk/dot_general | solution.py:30
  86.3 1.2 %fusion.111 = bf16[4,8,256]{2,1,0:T(8,128)(2,1)S(1)} fusion(bf16[4,8,256]{2,1,0:T(8,128)(2,1)S(1)} %get-tuple-element.330, s32[]{:T(128)S(6)} %copy.36, bf16[4,1024,256]{2,1,0:T(8,128)(2,1)} %get-tuple-element.344, bf16[1,8,1024]{2,0,1:T(2,128)(2,1)S(1)} %fusion.110, pred[1024]{0:T(1024)(128)(4,1)S(1)} %iota_compare_fusion.4, f32[]{:T(128)S(6)} %sqrt.4), kind=kOutput, calls=%fused_computation.12.clone.1 | convolution fusion | flops 4206592 | bytes 563712 | tf_op jit(solution)/shard_map/while/body/eval_jaxpr/while/body/eval_jaxpr/dot_general | solution.py:32
  87.5 0.7 dynamic_slice.54
  89.0 0.7 iota_compare_fusion.4
  89.7 0.1 fusion.109
  89.8 1.3 %convolution_bitcast_fusion.4 = f32[128,1024]{0,1:T(8,128)S(1)} fusion(bf16[256,128]{1,0:T(8,128)(2,1)S(1)} %get-tuple-element.346, bf16[4,1024,256]{2,1,0:T(8,128)(2,1)} %get-tuple-element.344, s32[]{:T(128)S(6)} %copy.36), kind=kOutput, calls=%fused_computation.8.clone.1 | convolution fusion | flops 67108864 | bytes 1114116 | tf_op jit(solution)/shard_map/while/body/eval_jaxpr/dot_general | solution.py:14
  91.1 0.2 copy.31
  91.3 1.8 %fusion.108 = f32[8,128,1024]{2,1,0:T(8,128)S(1)} fusion(f32[128,256]{1,0:T(8,128)S(1)} %convert_bitcast_fusion.2, f32[8,256]{1,0:T(8,128)S(1)} %bitcast_convert_fusion.2, bf16[4,1024,256]{2,1,0:T(8,128)(2,1)} %get-tuple-element.344, s32[]{:T(128)S(6)} %copy.36), kind=kOutput, calls=%fused_computation.14.clone.1 | convolution fusion | flops 537395200 | bytes 4857860 | tf_op jit(solution)/shard_map/while/body/eval_jaxpr/while/body/eval_jaxpr/dot_general | solution.py:22
  93.1 2.0 %fusion.110 = bf16[1,8,1024]{2,0,1:T(2,128)(2,1)S(1)} fusion(f32[8,128,1024]{2,1,0:T(8,128)S(1)} %fusion.108, f32[128,1024]{1,0:T(8,128)S(1)} %copy.31, f32[8,128]{1,0:T(8,128)S(1)} %fusion.109, bf16[128]{0:T(256)(128)(2,1)S(1)} %get-tuple-element.347), kind=kOutput, calls=%fused_computation.1.clone.1 | convolution fusion | flops 15728640 | bytes 4739328 | tf_op jit(solution)/shard_map/while/body/eval_jaxpr/while/body/eval_jaxpr/bak,a->bk/dot_general | solution.py:30
  95.1 1.2 %fusion.111 = bf16[4,8,256]{2,1,0:T(8,128)(2,1)S(1)} fusion(bf16[4,8,256]{2,1,0:T(8,128)(2,1)S(1)} %get-tuple-element.330, s32[]{:T(128)S(6)} %copy.36, bf16[4,1024,256]{2,1,0:T(8,128)(2,1)} %get-tuple-element.344, bf16[1,8,1024]{2,0,1:T(2,128)(2,1)S(1)} %fusion.110, pred[1024]{0:T(1024)(128)(4,1)S(1)} %iota_compare_fusion.4, f32[]{:T(128)S(6)} %sqrt.4), kind=kOutput, calls=%fused_computation.12.clone.1 | convolution fusion | flops 4206592 | bytes 563712 | tf_op jit(solution)/shard_map/while/body/eval_jaxpr/while/body/eval_jaxpr/dot_general | solution.py:32
  96.3 1.8 %fusion.49 = f32[32,1024]{1,0:T(8,128)S(1)} fusion(bf16[1792,1024]{1,0:T(8,128)(2,1)} %param.30, bf16[32,256]{1,0:T(8,128)(2,1)S(1)} %fusion.57, bf16[32,256]{1,0:T(8,128)(2,1)S(1)} %bitcast.115, bf16[32,256]{1,0:T(8,128)(2,1)S(1)} %bitcast.123), kind=kOutput, calls=%fused_computation.56 | convolution fusion | flops 50479104 | bytes 1753088 | tf_op jit(solution)/shard_map/dot_general | solution.py:134
  98.1 2.3 %fusion.56 = bf16[32,512]{1,0:T(8,128)(2,1)S(1)} fusion(bf16[1024,512]{1,0:T(8,128)(2,1)S(1)} %copy-done, f32[32,1024]{1,0:T(8,128)S(1)} %fusion.49, bf16[8,32,128]{2,1,0:T(8,128)(2,1)S(1)} %bitcast_reduce_fusion, bf16[8,128,1024]{2,1,0:T(8,128)(2,1)} %bitcast.113), kind=kOutput, calls=%fused_computation.64 | convolution fusion | flops 100794368 | bytes 3375104 | tf_op jit(solution)/shard_map/dot_general | solution.py:139
  100.4 0.3 fusion.60
  100.7 0.7 reshape.68
  (57 shorter events, 0.4 us)
Async XLA Ops:
  6.5 91.6 %copy-start = (bf16[1024,512]{1,0:T(8,128)(2,1)S(1)}, bf16[1024,512]{1,0:T(8,128)(2,1)}, u32[]{:S(2)}) copy-start(bf16[1024,512]{1,0:T(8,128)(2,1)} %param.31) | copy-start | bytes 3145732
  8.3 14.5 %all-to-all-start = ((s32[32,1,128]{2,1,0:T(1,128)}), s32[32,1,128]{2,1,0:T(1,128)S(1)}, u32[]{:S(2)}, u32[]{:S(2)}) async-start(s32[32,1,128]{2,1,0:T(1,128)} %reshape.81), calls=%async_computation | async-start | bytes 32768 | tf_op jit(solution)/shard_map/all_to_all | solution.py:106
  15.6 45.5 %all-gather.2.cloned.1.call-start = ((), (), s32[]{:S(2)}) async-start(), calls=%async_computation.2 | async-start | bytes 2621440 | tf_op jit(solution)/shard_map/all_gather | solution.py:91
  24.0 26.6 %copy-start.10 = (u32[32]{0:T(128)S(1)}, u32[32]{0:T(128)}, u32[]{:S(2)}) copy-start(u32[32]{0:T(128)} %constant.100) | copy-start | bytes 388
  24.0 32.9 %copy-start.9 = (bf16[256]{0:T(256)(128)(2,1)S(1)}, bf16[256]{0:T(256)(128)(2,1)}, u32[]{:S(2)}) copy-start(bf16[256]{0:T(256)(128)(2,1)} %param.33) | copy-start | bytes 1540
  24.1 32.9 %copy-start.6 = (s32[4,8,64]{2,1,0:T(8,128)S(1)}, s32[4,8,64]{2,1,0:T(8,128)}, u32[]{:S(2)}) copy-start(s32[4,8,64]{2,1,0:T(8,128)} %param.23) | copy-start | bytes 24580
  24.1 32.9 %copy-start.5 = (bf16[256,128]{1,0:T(8,128)(2,1)S(1)}, bf16[256,128]{1,0:T(8,128)(2,1)}, u32[]{:S(2)}) copy-start(bf16[256,128]{1,0:T(8,128)(2,1)} %param.28) | copy-start | bytes 196612
  47.4 13.6 %all-to-all-start.1 = ((bf16[32,32,128]{2,1,0:T(8,128)(2,1)}), bf16[32,32,128]{2,1,0:T(8,128)(2,1)S(1)}, u32[]{:S(2)}, u32[]{:S(2)}) async-start(bf16[32,32,128]{2,1,0:T(8,128)(2,1)} %bitcast.14), calls=%async_computation.1 | async-start | bytes 524288 | tf_op jit(solution)/shard_map/all_to_all | solution.py:112
  57.1 3.2 %copy-start.8 = (bf16[64,32,256]{2,1,0:T(8,128)(2,1)S(1)}, bf16[64,32,256]{2,1,0:T(8,128)(2,1)}, u32[]{:S(2)}) copy-start(bf16[64,32,256]{2,1,0:T(8,128)(2,1)} %param.25) | copy-start | bytes 3145732
  57.1 4.0 %copy-start.1 = (bf16[256,128]{1,0:T(8,128)(2,1)S(1)}, bf16[256,128]{1,0:T(8,128)(2,1)}, u32[]{:S(2)}) copy-start(bf16[256,128]{1,0:T(8,128)(2,1)} %param.27) | copy-start | bytes 196612
  57.2 4.0 %copy-start.2 = (bf16[256,128]{1,0:T(8,128)(2,1)S(1)}, bf16[256,128]{1,0:T(8,128)(2,1)}, u32[]{:S(2)}) copy-start(bf16[256,128]{1,0:T(8,128)(2,1)} %param.26) | copy-start | bytes 196612
  57.2 4.0 %copy-start.4 = (bf16[4,8,256]{2,1,0:T(8,128)(2,1)S(1)}, bf16[4,8,256]{2,1,0:T(8,128)(2,1)}, u32[]{:S(2)}) copy-start(bf16[4,8,256]{2,1,0:T(8,128)(2,1)} %param.21) | copy-start | bytes 49156
  57.2 4.0 %copy-start.7 = (bf16[128]{0:T(256)(128)(2,1)S(1)}, bf16[128]{0:T(256)(128)(2,1)}, u32[]{:S(2)}) copy-start(bf16[128]{0:T(256)(128)(2,1)} %param.29) | copy-start | bytes 772
  98.1 2.3 %copy-start.3 = (bf16[512,256]{1,0:T(8,128)(2,1)S(1)}, bf16[512,256]{1,0:T(8,128)(2,1)}, u32[]{:S(2)}) copy-start(bf16[512,256]{1,0:T(8,128)(2,1)} %param.32) | copy-start | bytes 786436
Sparse Core Ops, SparseCore 0:
  18.0 23.8 all-gather.1
where the time goes:
time: 109 us; the launch traced here: 108 us
  matrix products  52.8 us (48%)
  between operations  14.3 us (13%)
  local copies, waits for them, and re-layouts  11.3 us (10%)
  starting transfers between devices  9.92 us (9%)
  waiting for transfers between devices  7.08 us (6%)
  blocking collectives  5.05 us (5%)
  other arithmetic  4.24 us (4%)
  loops' own time  3.46 us (3%)
    dot_general x8, matrix products, add_block(): jnp.dot(counts, block_rows, preferred_element_type=jnp.float32)  22.1 us
    dot_general x4, matrix products, one_block(): jnp.einsum('bak,a->bk', unit_act, a_vector, precision=lax.Precision.HIGHEST)  7.81 us
    all_to_all x1, starting transfers between devices, on_device(): lax.all_to_all(outgoing, ('grp', 'cand'), split_axis=0, concat_axis=0, ti...  7.3 us
    dot_general x4, matrix products, one_block(): lax.dot_general(scaled.reshape(-1, scaled.shape[2]), history_rows, (((1,)...  7.17 us
    all_to_all x1, waiting for transfers between devices, on_device(): lax.all_to_all(outgoing, ('grp', 'cand'), split_axis=0, concat_axis=0, ti...  6.38 us
    dot_general x4, matrix products, interest_of(): k_part = jnp.dot(history_rows, w_key, preferred_element_type=jnp.float32).T  5.33 us
    unnamed x1, blocking collectives  5.05 us
    dot_general x4, matrix products, one_block(): return jnp.dot(scores, history_rows, preferred_element_type=jnp.float32)  4.9 us
  transfers between devices with their start and end apart: 3, of which 1 were waited for; matrix products, arithmetic and copies ran while one was open for 27% of the time, Pallas kernels for 0%

commit v1 on v0

v1 whole, which is shorter than its diff:
```python
import functools

import jax
import jax.numpy as jnp
from jax import lax
from jax.experimental import pallas as pl
from jax.experimental.pallas import tpu as pltpu
from jax.sharding import PartitionSpec as P

SPLIT = 4
ALL = ("grp", "cand")
VMEM = pl.BlockSpec(memory_space=pltpu.VMEM)
SMEM = pl.BlockSpec(memory_space=pltpu.SMEM)


def dot(left, right, dims=((1,), (0,))):
    return lax.dot_general(left, right, (dims, ((), ())), preferred_element_type=jnp.float32)


def pool_kernel(ids_ref, table_ref, out_ref, ids_s, sums, sem):
    copy = pltpu.make_async_copy(ids_ref, ids_s, sem)
    copy.start()
    copy.wait()
    sources, bag_size, rows = ids_ref.shape

    def one_source(src, carry):
        for n in range(rows):
            total = table_ref[pl.ds(ids_s[src, 0, n], 1), :]
            for slot in range(1, bag_size):
                total = total + table_ref[pl.ds(ids_s[src, slot, n], 1), :]
            sums[pl.ds(src * rows + n, 1), :] = total
        return carry

    lax.fori_loop(0, sources, one_source, 0)
    out_ref[...] = sums[...].astype(jnp.bfloat16).reshape(out_ref.shape)


def pool(offsets, table):
    sources, bag_size, rows = offsets.shape
    width = table.shape[1]
    return pl.pallas_call(
        pool_kernel,
        out_shape=jax.ShapeDtypeStruct((sources, rows, width), jnp.bfloat16),
        in_specs=[VMEM, VMEM],
        out_specs=VMEM,
        scratch_shapes=[
            pltpu.SMEM(offsets.shape, jnp.int32),
            pltpu.VMEM((sources * rows, width), jnp.float32),
            pltpu.SemaphoreType.DMA,
        ],
        compiler_params=pltpu.CompilerParams(vmem_limit_bytes=24 << 20),
        cost_estimate=pl.CostEstimate(flops=sources * rows * width * 4, bytes_accessed=table.size * 4, transcendentals=0),
        name="pool",
    )(offsets, table)


def attend_kernel(block, tile, len_ref, q_ref, h_ref, wq_ref, wk_ref, wp_ref, a_ref, out_ref, mixed, scores):
    items, width = q_ref.shape
    events = h_ref.shape[0]
    units = wq_ref.shape[1]
    pair_t = wp_ref[...].astype(jnp.float32).T
    key_t = wk_ref[...].astype(jnp.float32).T
    queries = q_ref[...]
    queries_f = queries.astype(jnp.float32)
    q_part = dot(wq_ref[...], queries, ((0,), (1,)))
    a_col = a_ref[...].astype(jnp.float32).T
    for c in range(items):
        mixed[c * units : (c + 1) * units, :] = (key_t + pair_t * queries_f[c : c + 1, :]).astype(jnp.bfloat16)
    length = len_ref[0]
    for at in range(0, events, tile):
        part = h_ref[at : at + tile, :]
        for first in range(0, items, block):
            raw = dot(mixed[first * units : (first + block) * units, :], part, ((1,), (1,)))
            rows = []
            for c in range(block):
                unit = raw[c * units : (c + 1) * units, :] + q_part[:, first + c : first + c + 1]
                unit = jnp.maximum(unit, 0.0) * a_col
                rows.append(jnp.sum(unit, axis=0, keepdims=True))
            scores[first : first + block, at : at + tile] = jnp.concatenate(rows, axis=0)
    live = lax.broadcasted_iota(jnp.int32, (items, events), 1) < length
    live_scores = jnp.where(live, scores[...], 0.0).astype(jnp.bfloat16)
    weighted = dot(live_scores, h_ref[...])
    root = jnp.sqrt(jnp.full((1, width), length, jnp.int32).astype(jnp.float32))
    out_ref[...] = (weighted * (1.0 / root)).astype(jnp.bfloat16)


def attend(queries, history, length, w_query, w_key, w_pair, a_out):
    items, width = queries.shape
    events, units = history.shape[0], w_query.shape[1]
    return pl.pallas_call(
        functools.partial(attend_kernel, 8, min(256, events)),
        out_shape=jax.ShapeDtypeStruct((items, width), jnp.bfloat16),
        in_specs=[SMEM] + [VMEM] * 6,
        out_specs=VMEM,
        scratch_shapes=[
            pltpu.VMEM((items * units, width), jnp.bfloat16),
            pltpu.VMEM((items, events), jnp.float32),
        ],
        compiler_params=pltpu.CompilerParams(vmem_limit_bytes=24 << 20),
        cost_estimate=pl.CostEstimate(flops=2 * items * units * width * events, bytes_accessed=history.size * 2, transcendentals=0),
        name="attend",
    )(length, queries, history, w_query, w_key, w_pair, a_out.reshape(1, -1))


def score_kernel(ret_ref, inter_ref, early_ref, w1_ref, w2_ref, w3_ref, wo_ref, out_ref, pooled):
    sources, rows, width = ret_ref.shape
    tables = sources // SPLIT
    for t in range(tables):
        total = ret_ref[t * SPLIT].astype(jnp.float32)
        for piece in range(1, SPLIT):
            total = total + ret_ref[t * SPLIT + piece].astype(jnp.float32)
        pooled[:, t * width : (t + 1) * width] = total.astype(jnp.bfloat16)
    cut = tables * width
    inter = inter_ref[...]
    one = early_ref[...] + dot(inter, w1_ref[cut : cut + inter.shape[1], :])
    one = one + dot(pooled[...], w1_ref[:cut, :])
    one = jnp.maximum(one, 0.0).astype(jnp.bfloat16)
    two = jnp.maximum(dot(one, w2_ref[...]), 0.0).astype(jnp.bfloat16)
    three = jnp.maximum(dot(two, w3_ref[...]), 0.0).astype(jnp.bfloat16)
    line = dot(wo_ref[...], three, ((1,), (1,)))
    requests, per = out_ref.shape
    for r in range(requests):
        out_ref[r : r + 1, :] = line[:, r * per : (r + 1) * per]


def score(returned, interest, early, w_first, w_second, w_third, w_out, requests):
    sources, rows, width = returned.shape
    return pl.pallas_call(
        score_kernel,
        out_shape=jax.ShapeDtypeStruct((requests, rows // requests), jnp.float32),
        in_specs=[VMEM] * 7,
        out_specs=VMEM,
        scratch_shapes=[pltpu.VMEM((rows, sources // SPLIT * width), jnp.bfloat16)],
        compiler_params=pltpu.CompilerParams(vmem_limit_bytes=24 << 20),
        name="score",
    )(returned, interest, early, w_first, w_second, w_third, w_out.reshape(1, -1))


def leaf_embed(leaf_rows, leaf_table):
    tree_count, leaf_count, feat_width = leaf_table.shape
    one_hot = (leaf_rows[..., None] == jnp.arange(leaf_count, dtype=jnp.int32)).astype(jnp.bfloat16)
    one_hot = one_hot.reshape(leaf_rows.shape[0], tree_count * leaf_count)
    return dot(one_hot, leaf_table.reshape(tree_count * leaf_count, feat_width)).astype(jnp.bfloat16)


def on_device(
    history, lengths, target, bag_ids, leaf_ids, table_piece, leaf_table,
    w_query, w_key, w_pair, a_out, w_first, w_second, w_third, w_out,
):
    req_count, per_req, feat_width = target.shape
    local_rows = req_count * per_req
    devices = lax.axis_size(ALL)
    tables = devices // SPLIT
    bag_size = bag_ids.shape[3]
    piece_rows, emb_width = table_piece.shape[1:]

    with jax.named_scope("ids_out"):
        bag_rows = jnp.transpose(bag_ids.reshape(local_rows, tables, bag_size), (1, 2, 0))
        outgoing = jnp.repeat(bag_rows, SPLIT, axis=0)
        incoming = lax.all_to_all(outgoing, ALL, split_axis=0, concat_axis=0, tiled=True)
    with jax.named_scope("target_out"):
        queries = lax.all_to_all(target, "cand", split_axis=0, concat_axis=0, tiled=True)
        queries = queries.reshape(-1, feat_width)
    with jax.named_scope("pooling"):
        quarter = lax.axis_index(ALL) % SPLIT
        offsets = incoming - quarter * piece_rows
        offsets = jnp.where((offsets >= 0) & (offsets < piece_rows), offsets, piece_rows)
        table = jnp.pad(table_piece[0].astype(jnp.float32), ((0, 8), (0, 0)))
        partial_sums = pool(offsets, table)
        returned = lax.all_to_all(partial_sums, ALL, split_axis=0, concat_axis=0, tiled=True)
    with jax.named_scope("attention"):
        interest = attend(queries, history[0], lengths, w_query, w_key, w_pair, a_out)
        interest = interest.reshape(-1, per_req, feat_width)
        interest = lax.all_to_all(interest, "cand", split_axis=0, concat_axis=0, tiled=True)
        interest = interest.reshape(local_rows, feat_width)
    with jax.named_scope("early"):
        leaf_vec = leaf_embed(leaf_ids.reshape(local_rows, -1), leaf_table)
        cut = tables * emb_width + feat_width
        own = jnp.concatenate([target.reshape(local_rows, feat_width), leaf_vec], axis=1)
        early = dot(own, w_first[cut:])
    with jax.named_scope("scoring"):
        return score(returned, interest, early, w_first, w_second, w_third, w_out, req_count)


def solution(mesh):
    placed = (
        P(ALL, None, None), P(ALL), P("grp", "cand", None), P("grp", "cand", None, None), P("grp", "cand", None),
        P(ALL, None, None),
    ) + (P(),) * 9
    return jax.shard_map(on_device, mesh=mesh, in_specs=placed, out_specs=P("grp", "cand"), check_vma=False)
```

time: 109 us -> 54.2 us (0.50)
  matrix products: 52.8 us -> 2.04 us
  between operations: 14.3 us -> 0.91 us
  Pallas kernels: 0 us -> 11.2 us
  starting transfers between devices: 9.92 us -> 17.6 us
  local copies, waits for them, and re-layouts: 11.3 us -> 5.69 us
  blocking collectives: 5.05 us -> 0 us
  waiting for transfers between devices: 7.08 us -> 11.8 us
  loops' own time: 3.46 us -> 0 us
    dot_general x32 -> x2, matrix products: 52.8 us -> 2.04 us  [dot(): lax.dot_general(left, right, (dims, ((), ())), preferred_element_type=jnp...]
    pallas_call x0 -> x3, Pallas kernels: none -> 11.2 us  [the longest x1 5.75 us: pool(): pl.pallas_call(pool_kernel, out_shape=jax.ShapeDtypeStruct((sources, rows...]
    all_to_all x2 -> x4, starting transfers between devices: 9.88 us -> 17.6 us  [the longest x1 6.85 us: on_device(): lax.all_to_all(outgoing, ALL, split_axis=0, concat_axis=0, tiled=True)]
    all_to_all x2 -> x4, waiting for transfers between devices: 6.38 us -> 11.8 us  [the longest x1 8.53 us: on_device(): lax.all_to_all(partial_sums, ALL, split_axis=0, concat_axis=0, tiled=True)]
    unnamed x1 -> x0, blocking collectives: 5.05 us -> none
    another operation x2 -> x0, loops' own time: 3.46 us -> none  [the longest x1 3.11 us: on_device(): interest = lax.map(one_request, (target, history_all, lengths_all))]
    pad x0 -> x1, other arithmetic: none -> 3.32 us  [on_device(): table = jnp.pad(table_piece[0].astype(jnp.float32), ((0, 8), (0, 0)))]
    slice x9 -> x0, local copies, waits for them, and re-layouts: 3.27 us -> none  [the longest x1 3.16 us: on_device(): w_first[:table_width].reshape(tables, emb_width, -1)]
  transfers between devices with their start and end apart: 3 -> 4, of which waited for: 1 -> 2; matrix products, arithmetic and copies ran while one was open for 27% -> 15% of each run, Pallas kernels for 0% -> 18%
where the time goes in v1:
time: 54.2 us; the launch traced here: 53.7 us
  starting transfers between devices  17.6 us (32%)
  waiting for transfers between devices  11.8 us (22%)
  Pallas kernels  11.2 us (21%)
  local copies, waits for them, and re-layouts  5.69 us (10%)
  other arithmetic  4.37 us (8%)
  matrix products  2.04 us (4%)
  between operations  0.91 us (2%)
    all_to_all x1, waiting for transfers between devices, on_device(): lax.all_to_all(partial_sums, ALL, split_axis=0, concat_axis=0, tiled=True)  8.53 us
    all_to_all x1, starting transfers between devices, on_device(): lax.all_to_all(outgoing, ALL, split_axis=0, concat_axis=0, tiled=True)  6.85 us
    pallas_call x1, Pallas kernels, pool(): pl.pallas_call(pool_kernel, out_shape=jax.ShapeDtypeStruct((sources, rows...  5.75 us
    unnamed x30, local copies, waits for them, and re-layouts  5.07 us
    all_to_all x1, starting transfers between devices, on_device(): lax.all_to_all(target, 'cand', split_axis=0, concat_axis=0, tiled=True)  4.36 us
    pallas_call x1, Pallas kernels, attend(): pl.pallas_call(functools.partial(attend_kernel, 8, min(256, events)), out...  3.79 us
    pad x1, other arithmetic, on_device(): table = jnp.pad(table_piece[0].astype(jnp.float32), ((0, 8), (0, 0)))  3.32 us
    all_to_all x1, waiting for transfers between devices, on_device(): lax.all_to_all(outgoing, ALL, split_axis=0, concat_axis=0, tiled=True)  3.3 us
  transfers between devices with their start and end apart: 4, of which 2 were waited for; matrix products, arithmetic and copies ran while one was open for 15% of the time, Pallas kernels for 18%

profile of v1, /device:TPU:0, one launch (start us, length us, event | category | flops | bytes accessed | tf_op | source)
XLA Modules:
  0.0 53.7 jit_solution(7590647088222358177)
XLA Ops:
  0.0 0.0 copy-start
  0.0 0.0 copy-start.12
  0.0 0.0 copy-start.11
  0.0 0.0 copy-start.13
  0.0 0.0 copy-start.5
  0.0 0.0 copy-start.9
  0.0 0.0 copy-start.6
  0.0 0.0 copy-start.7
  0.1 0.0 copy-start.8
  0.1 4.4 %all-to-all-start.2 = ((bf16[4,8,256]{2,1,0:T(8,128)(2,1)}), bf16[4,8,256]{2,1,0:T(8,128)(2,1)S(1)}, u32[]{:S(2)}, u32[]{:S(2)}) async-start(bf16[4,8,256]{2,1,0:T(8,128)(2,1)} %param.17), calls=%async_computation.2 | async-start | bytes 32768 | tf_op jit(solution)/shard_map/target_out/all_to_all | solution.py:162
  4.4 3.3 %pad_convert_fusion.table_ref = f32[8200,128]{1,0:T(8,128)} fusion(bf16[8192,128]{1,0:T(8,128)(2,1)} %bitcast.21), kind=kLoop, calls=%fused_computation | loop fusion | flops 1049600 | bytes 6295552 | tf_op jit(solution)/shard_map/pooling/jit(_pad)/pad | solution.py:168
  7.7 0.0 copy-done.12
  7.7 0.3 iota_compare_fusion
  8.1 0.0 copy-done.11
  8.1 0.1 copy.16
  8.2 0.7 %reshape.39 = s32[32,1,128]{2,1,0:T(1,128)} reshape(s32[32,4,32]{2,1,0:T(4,128)S(1)} %bitcast.22) | data formatting | bytes 32768
  9.6 0.0 copy-done.13
  9.6 0.0 all-to-all-done.2
  9.6 6.9 %all-to-all-start = ((s32[32,1,128]{2,1,0:T(1,128)}), s32[32,1,128]{2,1,0:T(1,128)S(1)}, u32[]{:S(2)}, u32[]{:S(2)}) async-start(s32[32,1,128]{2,1,0:T(1,128)} %reshape.39), calls=%async_computation | async-start | bytes 32768 | tf_op jit(solution)/shard_map/ids_out/all_to_all | solution.py:160
  16.5 0.0 copy-done.5
  16.5 0.0 copy-done.9
  16.5 0.0 copy-done.6
  16.5 0.0 copy-done.7
  16.5 0.0 copy-done.8
  16.5 3.8 %attend.1 = bf16[32,256]{1,0:T(8,128)(2,1)} custom-call(s32[1]{0:T(128)S(6)} %copy.21.len_ref, bf16[32,256]{1,0:T(8,128)(2,1)S(1)} %bitcast.18, bf16[1024,256]{1,0:T(8,128)(2,1)S(1)} %bitcast.19, bf16[256,128]{1,0:T(8,128)(2,1)S(1)} %copy-done.6, bf16[256,128]{1,0:T(8,128)(2,1)S(1)} %copy-done.7, bf16[256,128]{1,0:T(8,128)(2,1)S(1)} %copy-done.8, ...), custom_call_target="tpu_custom_call" | custom-call | flops 2147483648 | bytes 524288 | tf_op jit(solution)/shard_map/attention/attend/pallas_call | solution.py:90
  20.3 0.0 copy-start.10
  20.3 3.3 %all-to-all-done = s32[32,1,128]{2,1,0:T(1,128)S(1)} async-done(((s32[32,1,128]{2,1,0:T(1,128)}), s32[32,1,128]{2,1,0:T(1,128)S(1)}, u32[]{:S(2)}, u32[]{:S(2)}) %all-to-all-start) | async-done | bytes 16416 | tf_op jit(solution)/shard_map/ids_out/all_to_all | solution.py:160
  23.6 3.2 %all-to-all-start.3 = ((bf16[4,8,256]{2,1,0:T(8,128)(2,1)}), bf16[4,8,256]{2,1,0:T(8,128)(2,1)S(1)}, u32[]{:S(2)}, u32[]{:S(2)}) async-start(bf16[4,8,256]{2,1,0:T(8,128)(2,1)} %bitcast.7), calls=%async_computation.3 | async-start | bytes 32768 | tf_op jit(solution)/shard_map/attention/all_to_all | solution.py:174
  26.9 0.5 broadcast.3
  27.4 0.7 %reduce = s32[32,128]{1,0:T(8,128)S(1)} reduce(s32[32,1,128]{2,1,0:T(1,128)S(1)} %all-to-all-done, s32[]{:T(128)} %broadcast.3), dimensions={1}, to_apply=%all_to_all.12.reduce_sub_computation | reduce | bytes 32772 | tf_op jit(solution)/shard_map/ids_out/all_to_all | solution.py:160
  28.1 0.1 reshape.40
  28.2 0.0 copy-start.1
  28.2 2.2 %copy-done.1 = f32[8200,128]{1,0:T(8,128)S(1)} copy-done((f32[8200,128]{1,0:T(8,128)S(1)}, f32[8200,128]{1,0:T(8,128)}, u32[]{:S(2)}) %copy-start.1) | copy-done | bytes 4198424
  30.4 0.0 copy-start.3
  30.4 0.0 copy-start.4
  30.4 5.8 %pool.1 = bf16[32,32,128]{2,1,0:T(8,128)(2,1)} custom-call(s32[32,4,32]{2,1,0:T(4,128)S(1)} %and_select_fusion.ids_ref, f32[8200,128]{1,0:T(8,128)S(1)} %copy-done.1), custom_call_target="tpu_custom_call" | custom-call | flops 524288 | bytes 4198400 | tf_op jit(solution)/shard_map/pooling/pool/pallas_call | solution.py:41
  36.2 0.0 all-to-all-done.3
  36.2 3.2 %all-to-all-start.1 = ((bf16[32,32,128]{2,1,0:T(8,128)(2,1)}), bf16[32,32,128]{2,1,0:T(8,128)(2,1)S(1)}, u32[]{:S(2)}, u32[]{:S(2)}) async-start(bf16[32,32,128]{2,1,0:T(8,128)(2,1)} %pool.1), calls=%async_computation.1 | async-start | bytes 524288 | tf_op jit(solution)/shard_map/pooling/all_to_all | solution.py:170
  39.4 0.0 copy-done
  39.4 0.5 fusion
  39.9 0.0 copy-done.10
  39.9 1.5 %fusion.1.early_ref = f32[32,1024]{1,0:T(8,128)S(1)} fusion(bf16[1792,1024]{1,0:T(8,128)(2,1)} %w1_ref.1, bf16[32,256]{1,0:T(8,128)(2,1)S(1)} %fusion, bf16[32,256]{1,0:T(8,128)(2,1)S(1)} %bitcast.23), kind=kOutput, calls=%fused_computation.3 | convolution fusion | flops 33619968 | bytes 1212416 | tf_op jit(solution)/shard_map/early/dot_general | solution.py:17
  41.4 8.5 %all-to-all-done.1.ret_ref = bf16[32,32,128]{2,1,0:T(8,128)(2,1)S(1)} async-done(((bf16[32,32,128]{2,1,0:T(8,128)(2,1)}), bf16[32,32,128]{2,1,0:T(8,128)(2,1)S(1)}, u32[]{:S(2)}, u32[]{:S(2)}) %all-to-all-start.1) | async-done | bytes 262176 | tf_op jit(solution)/shard_map/pooling/all_to_all | solution.py:170
  50.0 0.0 copy-done.3
  50.0 0.0 copy-done.4
  50.0 0.0 copy-start.2
  50.0 2.0 %copy-done.2 = bf16[1792,1024]{1,0:T(8,128)(2,1)S(1)} copy-done((bf16[1792,1024]{1,0:T(8,128)(2,1)S(1)}, bf16[1792,1024]{1,0:T(8,128)(2,1)}, u32[]{:S(2)}) %copy-start.2) | copy-done | bytes 3670040
  52.0 1.7 %score.1 = f32[4,8]{1,0:T(4,128)} custom-call(bf16[32,32,128]{2,1,0:T(8,128)(2,1)S(1)} %all-to-all-done.1.ret_ref, bf16[32,256]{1,0:T(8,128)(2,1)S(1)} %bitcast.17, f32[32,1024]{1,0:T(8,128)S(1)} %fusion.1.early_ref, bf16[1792,1024]{1,0:T(8,128)(2,1)S(1)} %copy-done.2, bf16[1024,512]{1,0:T(8,128)(2,1)S(1)} %copy-done.3, bf16[512,256]{1,0:T(8,128)(2,1)S(1)} %copy-done.4, ...), custom_call_target="tpu_custom_call" | custom-call | tf_op jit(solution)/shard_map/scoring/score/pallas_call | solution.py:128
  (3 shorter events, 0.1 us)
Async XLA Ops:
  0.0 39.4 %copy-start = (bf16[64,32,256]{2,1,0:T(8,128)(2,1)S(1)}, bf16[64,32,256]{2,1,0:T(8,128)(2,1)}, u32[]{:S(2)}) copy-start(bf16[64,32,256]{2,1,0:T(8,128)(2,1)} %param.21) | copy-start | bytes 3145732
  0.0 7.7 %copy-start.12 = (s32[4,8,64]{2,1,0:T(8,128)S(1)}, s32[4,8,64]{2,1,0:T(8,128)}, u32[]{:S(2)}) copy-start(s32[4,8,64]{2,1,0:T(8,128)} %param.19) | copy-start | bytes 24580
  0.0 8.1 %copy-start.11 = (s32[4,8,8,4]{2,3,1,0:T(4,128)S(1)}, s32[4,8,8,4]{2,3,1,0:T(4,128)}, u32[]{:S(2)}) copy-start(s32[4,8,8,4]{2,3,1,0:T(4,128)} %param.18) | copy-start | bytes 12292
  0.0 9.6 %copy-start.13 = (bf16[256]{0:T(256)(128)(2,1)S(1)}, bf16[256]{0:T(256)(128)(2,1)}, u32[]{:S(2)}) copy-start(bf16[256]{0:T(256)(128)(2,1)} %param.29) | copy-start | bytes 1540
  0.0 16.5 %copy-start.5 = (bf16[1,1024,256]{2,1,0:T(8,128)(2,1)S(1)}, bf16[1,1024,256]{2,1,0:T(8,128)(2,1)}, u32[]{:S(2)}) copy-start(bf16[1,1024,256]{2,1,0:T(8,128)(2,1)} %param.15) | copy-start | bytes 1572868
  0.0 16.5 %copy-start.9 = (bf16[128]{0:T(256)(128)(2,1)S(1)}, bf16[128]{0:T(256)(128)(2,1)}, u32[]{:S(2)}) copy-start(bf16[128]{0:T(256)(128)(2,1)} %param.25) | copy-start | bytes 772
  0.0 16.5 %copy-start.6 = (bf16[256,128]{1,0:T(8,128)(2,1)S(1)}, bf16[256,128]{1,0:T(8,128)(2,1)}, u32[]{:S(2)}) copy-start(bf16[256,128]{1,0:T(8,128)(2,1)} %wq_ref.1) | copy-start | bytes 196612
  0.0 16.5 %copy-start.7 = (bf16[256,128]{1,0:T(8,128)(2,1)S(1)}, bf16[256,128]{1,0:T(8,128)(2,1)}, u32[]{:S(2)}) copy-start(bf16[256,128]{1,0:T(8,128)(2,1)} %wk_ref.1) | copy-start | bytes 196612
  0.1 16.5 %copy-start.8 = (bf16[256,128]{1,0:T(8,128)(2,1)S(1)}, bf16[256,128]{1,0:T(8,128)(2,1)}, u32[]{:S(2)}) copy-start(bf16[256,128]{1,0:T(8,128)(2,1)} %wp_ref.1) | copy-start | bytes 196612
  0.1 9.6 %all-to-all-start.2 = ((bf16[4,8,256]{2,1,0:T(8,128)(2,1)}), bf16[4,8,256]{2,1,0:T(8,128)(2,1)S(1)}, u32[]{:S(2)}, u32[]{:S(2)}) async-start(bf16[4,8,256]{2,1,0:T(8,128)(2,1)} %param.17), calls=%async_computation.2 | async-start | bytes 32768 | tf_op jit(solution)/shard_map/target_out/all_to_all | solution.py:162
  9.6 14.0 %all-to-all-start = ((s32[32,1,128]{2,1,0:T(1,128)}), s32[32,1,128]{2,1,0:T(1,128)S(1)}, u32[]{:S(2)}, u32[]{:S(2)}) async-start(s32[32,1,128]{2,1,0:T(1,128)} %reshape.39), calls=%async_computation | async-start | bytes 32768 | tf_op jit(solution)/shard_map/ids_out/all_to_all | solution.py:160
  20.3 19.6 %copy-start.10 = (bf16[4,8,256]{2,1,0:T(8,128)(2,1)S(1)}, bf16[4,8,256]{2,1,0:T(8,128)(2,1)}, u32[]{:S(2)}) copy-start(bf16[4,8,256]{2,1,0:T(8,128)(2,1)} %param.17) | copy-start | bytes 49156
  23.6 12.6 %all-to-all-start.3 = ((bf16[4,8,256]{2,1,0:T(8,128)(2,1)}), bf16[4,8,256]{2,1,0:T(8,128)(2,1)S(1)}, u32[]{:S(2)}, u32[]{:S(2)}) async-start(bf16[4,8,256]{2,1,0:T(8,128)(2,1)} %bitcast.7), calls=%async_computation.3 | async-start | bytes 32768 | tf_op jit(solution)/shard_map/attention/all_to_all | solution.py:174
  28.2 2.2 %copy-start.1 = (f32[8200,128]{1,0:T(8,128)S(1)}, f32[8200,128]{1,0:T(8,128)}, u32[]{:S(2)}) copy-start(f32[8200,128]{1,0:T(8,128)} %pad_convert_fusion.table_ref) | copy-start | bytes 12595204
  30.4 19.6 %copy-start.3 = (bf16[1024,512]{1,0:T(8,128)(2,1)S(1)}, bf16[1024,512]{1,0:T(8,128)(2,1)}, u32[]{:S(2)}) copy-start(bf16[1024,512]{1,0:T(8,128)(2,1)} %w2_ref.1) | copy-start | bytes 3145732
  30.4 19.6 %copy-start.4 = (bf16[512,256]{1,0:T(8,128)(2,1)S(1)}, bf16[512,256]{1,0:T(8,128)(2,1)}, u32[]{:S(2)}) copy-start(bf16[512,256]{1,0:T(8,128)(2,1)} %w3_ref.1) | copy-start | bytes 786436
  36.2 13.8 %all-to-all-start.1 = ((bf16[32,32,128]{2,1,0:T(8,128)(2,1)}), bf16[32,32,128]{2,1,0:T(8,128)(2,1)S(1)}, u32[]{:S(2)}, u32[]{:S(2)}) async-start(bf16[32,32,128]{2,1,0:T(8,128)(2,1)} %pool.1), calls=%async_computation.1 | async-start | bytes 524288 | tf_op jit(solution)/shard_map/pooling/all_to_all | solution.py:170
  50.0 2.0 %copy-start.2 = (bf16[1792,1024]{1,0:T(8,128)(2,1)S(1)}, bf16[1792,1024]{1,0:T(8,128)(2,1)}, u32[]{:S(2)}) copy-start(bf16[1792,1024]{1,0:T(8,128)(2,1)} %w1_ref.1) | copy-start | bytes 11010052

commit v2 on v1

v2 whole, which is shorter than its diff:
```python
import functools

import jax
import jax.numpy as jnp
from jax import lax
from jax.experimental import pallas as pl
from jax.experimental.pallas import tpu as pltpu
from jax.sharding import PartitionSpec as P

SPLIT = 4
ALL = ("grp", "cand")
VMEM = pl.BlockSpec(memory_space=pltpu.VMEM)
HBM = pl.BlockSpec(memory_space=pltpu.HBM)
SMEM = pl.BlockSpec(memory_space=pltpu.SMEM)


def in_hbm(*arrays):
    return [pltpu.with_memory_space_constraint(a, pltpu.HBM) for a in arrays]


def dot(left, right, dims=((1,), (0,))):
    return lax.dot_general(left, right, (dims, ((), ())), preferred_element_type=jnp.float32)


def prepare_kernel(me_ref, bag_hbm, target_hbm, ids_ref, *refs):
    requests, per, bag_size, tables = bag_hbm.shape
    block_refs = refs[:requests]
    bag_ref, target_ref, sems = refs[requests:]
    copies = [pltpu.make_async_copy(bag_hbm, bag_ref, sems.at[0]), pltpu.make_async_copy(target_hbm, target_ref, sems.at[1])]
    for copy in copies:
        copy.start()
    for copy in copies:
        copy.wait()
    lines = jnp.concatenate([bag_ref[r, c] for r in range(requests) for c in range(per)], axis=0)
    by_table = lines.T
    for t in range(tables):
        for piece in range(SPLIT):
            ids_ref[t * SPLIT + piece] = by_table[t : t + 1, :]
    for k, block_ref in enumerate(block_refs):
        block_ref[...] = target_ref[me_ref[0] ^ k]


def prepare(me, bag_ids, target):
    requests, per, tables, bag_size = bag_ids.shape
    block = jax.ShapeDtypeStruct(target.shape[1:], target.dtype)
    out = pl.pallas_call(
        prepare_kernel,
        out_shape=[jax.ShapeDtypeStruct((tables * SPLIT, 1, requests * per * bag_size), jnp.int32)] + [block] * requests,
        in_specs=[SMEM, HBM, HBM],
        out_specs=[VMEM] * (1 + requests),
        scratch_shapes=[
            pltpu.VMEM((requests, per, bag_size, tables), jnp.int32),
            pltpu.VMEM(target.shape, target.dtype),
            pltpu.SemaphoreType.DMA((2,)),
        ],
        compiler_params=pltpu.CompilerParams(vmem_limit_bytes=12 << 20),
        cost_estimate=pl.CostEstimate(flops=30000000000, bytes_accessed=10**6, transcendentals=0),
        name="prepare",
    )(me, *in_hbm(jnp.transpose(bag_ids, (0, 1, 3, 2)), target))
    return out[0], out[1:]


def pool_kernel(bag_size, quarter_ref, ids_ref, table_ref, out_ref, offsets, offsets_s, rows_f, sums, sem):
    sources, _, lanes = ids_ref.shape
    rows = lanes // bag_size
    piece_rows, width = table_ref.shape
    local = ids_ref[...] - quarter_ref[0] * piece_rows
    offsets[...] = jnp.where((local >= 0) & (local < piece_rows), local, piece_rows)
    copy = pltpu.make_async_copy(offsets, offsets_s, sem)
    copy.start()
    rows_f[:piece_rows, :] = table_ref[...].astype(jnp.float32)
    rows_f[piece_rows:, :] = jnp.zeros((8, width), jnp.float32)
    copy.wait()

    def one_source(src, carry):
        for n in range(rows):
            total = rows_f[pl.ds(offsets_s[src, 0, n * bag_size], 1), :]
            for slot in range(1, bag_size):
                total = total + rows_f[pl.ds(offsets_s[src, 0, n * bag_size + slot], 1), :]
            sums[pl.ds(src * rows + n, 1), :] = total
        return carry

    lax.fori_loop(0, sources, one_source, 0)
    out_ref[...] = sums[...].astype(jnp.bfloat16).reshape(out_ref.shape)


def pool(quarter, ids, table, bag_size):
    sources, _, lanes = ids.shape
    rows = lanes // bag_size
    piece_rows, width = table.shape
    return pl.pallas_call(
        functools.partial(pool_kernel, bag_size),
        out_shape=jax.ShapeDtypeStruct((sources, rows, width), jnp.bfloat16),
        in_specs=[SMEM, VMEM, VMEM],
        out_specs=VMEM,
        scratch_shapes=[
            pltpu.VMEM(ids.shape, jnp.int32),
            pltpu.SMEM(ids.shape, jnp.int32),
            pltpu.VMEM((piece_rows + 8, width), jnp.float32),
            pltpu.VMEM((sources * rows, width), jnp.float32),
            pltpu.SemaphoreType.DMA,
        ],
        compiler_params=pltpu.CompilerParams(vmem_limit_bytes=9 << 20),
        cost_estimate=pl.CostEstimate(flops=30000000000, bytes_accessed=table.size * 4, transcendentals=0),
        name="pool",
    )(quarter, ids, table)


def early_kernel(after_ref, target_ref, leaf_ids_ref, leaf_hbm, w1_hbm, early_ref, head_ref, leaf_ref, tail, sems):
    requests, per, width = target_ref.shape
    cut = head_ref.shape[0]
    fetches = [
        pltpu.make_async_copy(leaf_hbm, leaf_ref, sems.at[0]),
        pltpu.make_async_copy(w1_hbm.at[pl.ds(cut, tail.shape[0])], tail, sems.at[1]),
        pltpu.make_async_copy(w1_hbm.at[pl.ds(0, cut)], head_ref, sems.at[2]),
    ]
    for fetch in fetches:
        fetch.start()
    rows = requests * per
    trees = leaf_ids_ref.shape[2]
    total = leaf_ref.shape[0]
    leaves = total // trees
    ids = leaf_ids_ref[...].reshape(rows, trees).astype(jnp.float32).astype(jnp.bfloat16)
    spread = lax.broadcasted_iota(jnp.int32, (trees, total), 1) // leaves == lax.broadcasted_iota(jnp.int32, (trees, total), 0)
    wide = dot(ids, spread.astype(jnp.float32).astype(jnp.bfloat16))
    leaf = (lax.broadcasted_iota(jnp.int32, (rows, total), 1) % leaves).astype(jnp.float32)
    chosen = jnp.where(wide == leaf, 1.0, 0.0).astype(jnp.bfloat16)
    fetches[0].wait()
    leaf_vec = dot(chosen, leaf_ref[...]).astype(jnp.bfloat16)
    fetches[1].wait()
    own = target_ref[...].reshape(rows, width)
    early_ref[...] = dot(own, tail[:width, :]) + dot(leaf_vec, tail[width:, :])
    fetches[2].wait()


def early_part(after, target, leaf_ids, leaf_table, w_first):
    requests, per, width = target.shape
    cut, hidden = w_first.shape[0] - 2 * width, w_first.shape[1]
    return pl.pallas_call(
        early_kernel,
        out_shape=[jax.ShapeDtypeStruct((requests * per, hidden), jnp.float32), pltpu.VMEM((cut, hidden), w_first.dtype)],
        in_specs=[HBM, VMEM, VMEM, HBM, HBM],
        out_specs=[VMEM] * 2,
        scratch_shapes=[
            pltpu.VMEM(leaf_table.shape, leaf_table.dtype),
            pltpu.VMEM((2 * width, hidden), w_first.dtype),
            pltpu.SemaphoreType.DMA((3,)),
        ],
        compiler_params=pltpu.CompilerParams(vmem_limit_bytes=12 << 20),
        cost_estimate=pl.CostEstimate(flops=10**9, bytes_accessed=10**6, transcendentals=0),
        name="early",
    )(after, target, leaf_ids, *in_hbm(leaf_table, w_first))


def attend_kernel(parts, block, tile, len_ref, *refs):
    q_refs = refs[:parts]
    h_ref, wq_ref, wk_ref, wp_ref, a_ref = refs[parts : parts + 5]
    out_refs = refs[parts + 5 : 2 * parts + 5]
    mixed, scores = refs[2 * parts + 5 :]
    queries = jnp.concatenate([q[...].astype(jnp.float32) for q in q_refs], axis=0)
    items, width = queries.shape
    per = items // parts
    events = h_ref.shape[0]
    units = wq_ref.shape[1]
    pair_t = wp_ref[...].astype(jnp.float32).T
    key_t = wk_ref[...].astype(jnp.float32).T
    q_part = dot(wq_ref[...], queries.astype(jnp.bfloat16), ((0,), (1,)))
    a_col = a_ref[...].astype(jnp.float32).T
    for c in range(items):
        mixed[c * units : (c + 1) * units, :] = (key_t + pair_t * queries[c : c + 1, :]).astype(jnp.bfloat16)
    length = len_ref[0]
    for at in range(0, events, tile):
        part = h_ref[at : at + tile, :]
        for first in range(0, items, block):
            raw = dot(mixed[first * units : (first + block) * units, :], part, ((1,), (1,)))
            rows = []
            for c in range(block):
                unit = raw[c * units : (c + 1) * units, :] + q_part[:, first + c : first + c + 1]
                unit = jnp.maximum(unit, 0.0) * a_col
                rows.append(jnp.sum(unit, axis=0, keepdims=True))
            scores[first : first + block, at : at + tile] = jnp.concatenate(rows, axis=0)
    live = lax.broadcasted_iota(jnp.int32, (items, events), 1) < length
    live_scores = jnp.where(live, scores[...], 0.0).astype(jnp.bfloat16)
    weighted = dot(live_scores, h_ref[...])
    root = jnp.sqrt(jnp.full((1, width), length, jnp.int32).astype(jnp.float32))
    weighted = weighted * (1.0 / root)
    for k, out_ref in enumerate(out_refs):
        out_ref[...] = weighted[k * per : (k + 1) * per, :].astype(jnp.bfloat16)


def attend(queries, history, length, w_query, w_key, w_pair, a_out):
    parts = len(queries)
    per, width = queries[0].shape
    items = parts * per
    events, units = history.shape[0], w_query.shape[1]
    return pl.pallas_call(
        functools.partial(attend_kernel, parts, 8, min(256, events)),
        out_shape=[jax.ShapeDtypeStruct((per, width), jnp.bfloat16)] * parts,
        in_specs=[SMEM] + [VMEM] * (parts + 5),
        out_specs=[VMEM] * parts,
        scratch_shapes=[
            pltpu.VMEM((items * units, width), jnp.bfloat16),
            pltpu.VMEM((items, events), jnp.float32),
        ],
        compiler_params=pltpu.CompilerParams(vmem_limit_bytes=12 << 20),
        cost_estimate=pl.CostEstimate(flops=3 * 10**10, bytes_accessed=history.size * 2, transcendentals=0),
        name="attend",
    )(length, *queries, history, w_query, w_key, w_pair, a_out.reshape(1, -1))


def score_kernel(parts, me_ref, ret_ref, *refs):
    inter_refs = refs[:parts]
    early_ref, w1_ref, w2_ref, w3_ref, wo_ref, out_ref, pooled, interest = refs[parts:]
    sources, rows, width = ret_ref.shape
    tables = sources // SPLIT
    per = rows // parts
    for k in range(parts):
        place = pl.multiple_of((me_ref[0] ^ k) * per, per)
        interest[pl.ds(place, per), :] = inter_refs[k][...].astype(jnp.float32)
    for t in range(tables):
        total = ret_ref[t * SPLIT].astype(jnp.float32)
        for piece in range(1, SPLIT):
            total = total + ret_ref[t * SPLIT + piece].astype(jnp.float32)
        pooled[:, t * width : (t + 1) * width] = total.astype(jnp.bfloat16)
    cut = tables * width
    inter = interest[...].astype(jnp.bfloat16)
    one = early_ref[...] + dot(inter, w1_ref[cut : cut + inter.shape[1], :])
    one = one + dot(pooled[...], w1_ref[:cut, :])
    one = jnp.maximum(one, 0.0).astype(jnp.bfloat16)
    two = jnp.maximum(dot(one, w2_ref[...]), 0.0).astype(jnp.bfloat16)
    three = jnp.maximum(dot(two, w3_ref[...]), 0.0).astype(jnp.bfloat16)
    line = dot(wo_ref[...], three, ((1,), (1,)))
    for r in range(parts):
        out_ref[r : r + 1, :] = line[:, r * per : (r + 1) * per]


def score(me, returned, interest, early, w_first, w_second, w_third, w_out):
    sources, rows, width = returned.shape
    parts = len(interest)
    return pl.pallas_call(
        functools.partial(score_kernel, parts),
        out_shape=jax.ShapeDtypeStruct((parts, rows // parts), jnp.float32),
        in_specs=[SMEM] + [VMEM] * (parts + 6),
        out_specs=VMEM,
        scratch_shapes=[
            pltpu.VMEM((rows, sources // SPLIT * width), jnp.bfloat16),
            pltpu.VMEM((rows, interest[0].shape[1]), jnp.float32),
        ],
        compiler_params=pltpu.CompilerParams(vmem_limit_bytes=9 << 20),
        name="score",
    )(me, returned, *interest, early, w_first, w_second, w_third, w_out.reshape(1, -1))


def swap(blocks):
    size = len(blocks)
    return [blocks[0]] + [
        lax.ppermute(blocks[k], "cand", [(i, i ^ k) for i in range(size)]) for k in range(1, size)
    ]


def on_device(
    history, lengths, target, bag_ids, leaf_ids, table_piece, leaf_table,
    w_query, w_key, w_pair, a_out, w_first, w_second, w_third, w_out,
):
    me = lax.axis_index("cand").astype(jnp.int32).reshape(1)
    quarter = (lax.axis_index(ALL) % SPLIT).astype(jnp.int32).reshape(1)

    with jax.named_scope("sending"):
        outgoing, blocks = prepare(me, bag_ids, target)
        queries = swap(blocks)
        incoming = lax.all_to_all(outgoing, ALL, split_axis=0, concat_axis=0, tiled=True)
    with jax.named_scope("pooling"):
        partial_sums = pool(quarter, incoming, table_piece[0], bag_ids.shape[3])
        partial_sums, queries = lax.optimization_barrier((partial_sums, queries))
        returned = lax.all_to_all(partial_sums, ALL, split_axis=0, concat_axis=0, tiled=True)
    with jax.named_scope("attention"):
        interest = attend(queries, history[0], lengths, w_query, w_key, w_pair, a_out)
        early, w_head = early_part(
            interest[0], target, leaf_ids, leaf_table.reshape(-1, leaf_table.shape[2]), w_first
        )
        interest = swap(interest)
    with jax.named_scope("scoring"):
        return score(me, returned, interest, early, w_head, w_second, w_third, w_out)


def solution(mesh):
    placed = (
        P(ALL, None, None), P(ALL), P("grp", "cand", None), P("grp", "cand", None, None), P("grp", "cand", None),
        P(ALL, None, None),
    ) + (P(),) * 9
    return jax.shard_map(on_device, mesh=mesh, in_specs=placed, out_specs=P("grp", "cand"), check_vma=False)
```

time: 54.2 us -> 37.6 us (0.69)
  waiting for transfers between devices: 11.8 us -> 6.46 us
  other arithmetic: 4.37 us -> 0 us
  starting transfers between devices: 17.6 us -> 13.8 us
  local copies, waits for them, and re-layouts: 5.69 us -> 2.3 us
  Pallas kernels: 11.2 us -> 13.9 us
  matrix products: 2.04 us -> 0 us
    all_to_all x2 -> x0, starting transfers between devices: 7.61 us -> none  [the longest x1 4.36 us: on_device(): lax.all_to_all(target, 'cand', split_axis=0, concat_axis=0, tiled=True)]
    all_to_all x1, waiting for transfers between devices: 8.53 us -> 1.43 us  [on_device(): lax.all_to_all(partial_sums, ALL, split_axis=0, concat_axis=0, tiled=True)]
    ppermute x0 -> x6, starting transfers between devices: none -> 3.91 us  [swap(): lax.ppermute(blocks[k], 'cand', [(i, i ^ k) for i in range(size)])]
    pad x1 -> x0, other arithmetic: 3.32 us -> none  [on_device(): table = jnp.pad(table_piece[0].astype(jnp.float32), ((0, 8), (0, 0)))]
    unnamed x30 -> x22, local copies, waits for them, and re-layouts: 5.07 us -> 2.3 us
    pallas_call x3 -> x5, Pallas kernels: 11.2 us -> 13.9 us  [the longest x1 4.98 us: pool(): pl.pallas_call(functools.partial(pool_kernel, bag_size), out_shape=jax.Sh...]
    dot_general x2 -> x0, matrix products: 2.04 us -> none  [dot(): lax.dot_general(left, right, (dims, ((), ())), preferred_element_type=jnp...]
    all_to_all x1, waiting for transfers between devices: 3.3 us -> 4.46 us  [on_device(): lax.all_to_all(outgoing, ALL, split_axis=0, concat_axis=0, tiled=True)]
  transfers between devices with their start and end apart: 4 -> 8, of which waited for: 2 -> 3; matrix products, arithmetic and copies ran while one was open for 15% -> 0% of each run, Pallas kernels for 18% -> 28%
where the time goes in v2:
time: 37.6 us; the launch traced here: 37.3 us
  Pallas kernels  13.9 us (37%)
  starting transfers between devices  13.8 us (37%)
  waiting for transfers between devices  6.46 us (17%)
  local copies, waits for them, and re-layouts  2.3 us (6%)
  between operations  0.82 us (2%)
    all_to_all x1, starting transfers between devices, on_device(): lax.all_to_all(outgoing, ALL, split_axis=0, concat_axis=0, tiled=True)  7.3 us
    pallas_call x1, Pallas kernels, pool(): pl.pallas_call(functools.partial(pool_kernel, bag_size), out_shape=jax.Sh...  4.98 us
    all_to_all x1, waiting for transfers between devices, on_device(): lax.all_to_all(outgoing, ALL, split_axis=0, concat_axis=0, tiled=True)  4.46 us
    ppermute x6, starting transfers between devices, swap(): lax.ppermute(blocks[k], 'cand', [(i, i ^ k) for i in range(size)])  3.91 us
    pallas_call x1, Pallas kernels, attend(): pl.pallas_call(functools.partial(attend_kernel, parts, 8, min(256, events...  3.17 us
    all_to_all x1, starting transfers between devices, on_device(): lax.all_to_all(partial_sums, ALL, split_axis=0, concat_axis=0, tiled=True)  2.6 us
    pallas_call x1, Pallas kernels, early_part(): pl.pallas_call(early_kernel, out_shape=[jax.ShapeDtypeStruct((requests *...  2.41 us
    unnamed x22, local copies, waits for them, and re-layouts  2.3 us
  transfers between devices with their start and end apart: 8, of which 3 were waited for; matrix products, arithmetic and copies ran while one was open for 0% of the time, Pallas kernels for 28%

profile of v2, /device:TPU:0, one launch (start us, length us, event | category | flops | bytes accessed | tf_op | source)
XLA Modules:
  0.0 37.3 jit_solution(5977909842128878400)
XLA Ops:
  0.0 0.0 copy-start.10
  0.0 0.0 copy-start.4
  0.0 1.7 %prepare.1 = (s32[32,1,128]{2,1,0:T(1,128)}, bf16[8,256]{1,0:T(8,128)(2,1)S(1)}, bf16[8,256]{1,0:T(8,128)(2,1)S(1)}, bf16[8,256]{1,0:T(8,128)(2,1)S(1)}, bf16[8,256]{1,0:T(8,128)(2,1)S(1)}) custom-call(s32[1]{0:T(128)} %bitcast.me_ref, s32[4,8,4,8]{3,2,1,0:T(4,128)} %bitcast.11, bf16[4,8,256]{2,1,0:T(8,128)(2,1)} %target_ref.1), custom_call_target="tpu_custom_call" | custom-call | flops 30000001024 | bytes 1000000 | tf_op jit(solution)/shard_map/sending/prepare/pallas_call | solution.py:46
  1.7 7.3 %all-to-all-start = ((s32[32,1,128]{2,1,0:T(1,128)}), s32[32,1,128]{2,1,0:T(1,128)S(1)}, u32[]{:S(2)}, u32[]{:S(2)}) async-start(s32[32,1,128]{2,1,0:T(1,128)} %get-tuple-element.21), calls=%async_computation | async-start | bytes 32768 | tf_op jit(solution)/shard_map/sending/all_to_all | solution.py:271
  9.0 0.3 collective-permute-start
  9.3 1.7 %collective-permute-start.1 = (bf16[8,256]{1,0:T(8,128)(2,1)S(1)}, bf16[8,256]{1,0:T(8,128)(2,1)S(1)}, u32[]{:S(2)}, u32[]{:S(2)}) collective-permute-start(bf16[8,256]{1,0:T(8,128)(2,1)S(1)} %get-tuple-element.24), channel_id=1, source_target_pairs={{0,2},{1,3},{2,0},{3,1},{4,6},{5,7},{6,4},{7,5},{8,10},{9,11},{10,... | collective-permute-start | bytes 12296 | tf_op jit(solution)/shard_map/sending/ppermute | solution.py:257
  11.0 0.0 collective-permute-start.2
  11.7 0.0 copy-done.10
  11.7 4.5 %all-to-all-done.ids_ref = s32[32,1,128]{2,1,0:T(1,128)S(1)} async-done(((s32[32,1,128]{2,1,0:T(1,128)}), s32[32,1,128]{2,1,0:T(1,128)S(1)}, u32[]{:S(2)}, u32[]{:S(2)}) %all-to-all-start) | async-done | bytes 16416 | tf_op jit(solution)/shard_map/sending/all_to_all | solution.py:271
  16.2 0.0 copy-done.4
  16.2 0.0 copy-start.6
  16.2 0.0 copy-start.7
  16.2 0.0 copy-start.8
  16.2 0.0 copy-start.9
  16.2 5.0 %pool.1 = bf16[32,32,128]{2,1,0:T(8,128)(2,1)} custom-call(s32[1]{0:T(128)} %bitcast.1.quarter_ref, s32[32,1,128]{2,1,0:T(1,128)S(1)} %all-to-all-done.ids_ref, bf16[8192,128]{1,0:T(8,128)(2,1)S(1)} %bitcast.7), custom_call_target="tpu_custom_call" | custom-call | flops 30000001024 | bytes 4194304 | tf_op jit(solution)/shard_map/pooling/pool/pallas_call | solution.py:91
  21.2 0.0 collective-permute-done.refs_1_
  21.2 0.0 collective-permute-done.1.refs_2_
  21.2 0.0 collective-permute-done.2.refs_3_
  21.2 2.6 %all-to-all-start.1 = ((bf16[32,32,128]{2,1,0:T(8,128)(2,1)}), bf16[32,32,128]{2,1,0:T(8,128)(2,1)S(1)}, u32[]{:S(2)}, u32[]{:S(2)}) async-start(bf16[32,32,128]{2,1,0:T(8,128)(2,1)} %pool.1), calls=%async_computation.1 | async-start | bytes 524288 | tf_op jit(solution)/shard_map/pooling/all_to_all | solution.py:275
  23.8 0.0 copy-done.6
  23.8 0.0 copy-done.7
  23.8 0.0 copy-done.8
  23.8 0.0 copy-done.9
  23.8 0.0 copy-start.5
  23.9 1.0 %copy-done.5 = bf16[1,1024,256]{2,1,0:T(8,128)(2,1)S(1)} copy-done((bf16[1,1024,256]{2,1,0:T(8,128)(2,1)S(1)}, bf16[1,1024,256]{2,1,0:T(8,128)(2,1)}, u32[]{:S(2)}) %copy-start.5) | copy-done | bytes 524312
  24.9 0.0 copy-start.2
  24.9 0.0 copy-start.3
  24.9 3.2 %attend.1 = (bf16[8,256]{1,0:T(8,128)(2,1)S(1)}, bf16[8,256]{1,0:T(8,128)(2,1)S(1)}, bf16[8,256]{1,0:T(8,128)(2,1)S(1)}, bf16[8,256]{1,0:T(8,128)(2,1)S(1)}) custom-call(s32[1]{0:T(128)S(6)} %copy.16.len_ref, bf16[8,256]{1,0:T(8,128)(2,1)S(1)} %get-tuple-element.27.refs_0_, bf16[8,256]{1,0:T(8,128)(2,1)S(1)} %collective-permute-done.refs_1_, ...), custom_call_target="tpu_custom_call" | custom-call | flops 30000001024 | bytes 524288 | tf_op jit(solution)/shard_map/attention/attend/pallas_call | solution.py:196
  28.1 0.0 copy-start.1
  28.1 0.1 collective-permute-start.3
  28.2 1.7 %collective-permute-start.4 = (bf16[8,256]{1,0:T(8,128)(2,1)S(1)}, bf16[8,256]{1,0:T(8,128)(2,1)S(1)}, u32[]{:S(2)}, u32[]{:S(2)}) collective-permute-start(bf16[8,256]{1,0:T(8,128)(2,1)S(1)} %get-tuple-element.33), channel_id=1, source_target_pairs={{0,2},{1,3},{2,0},{3,1},{4,6},{5,7},{6,4},{7,5},{8,10},{9,11},{10,... | collective-permute-start | bytes 12296 | tf_op jit(solution)/shard_map/attention/ppermute | solution.py:257
  29.9 0.1 collective-permute-start.5
  30.0 0.0 copy-done.2
  30.0 0.0 copy-done.3
  30.0 2.4 %early.1 = (f32[32,1024]{1,0:T(8,128)S(1)}, bf16[1280,1024]{1,0:T(8,128)(2,1)S(1)}) custom-call(bf16[8,256]{1,0:T(8,128)(2,1)S(1)} %get-tuple-element.31.after_ref.refs_0_, bf16[4,8,256]{2,1,0:T(8,128)(2,1)S(1)} %copy-done.2, s32[4,8,64]{2,1,0:T(8,128)S(1)} %copy-done.3, bf16[2048,256]{1,0:T(8,128)(2,1)} %bitcast.10, bf16[1792,1024]{1,0:T(8,128)(2,1)} %w1_hbm.1), custom_call_target="tpu_custom_call" | custom-call | flops 1000000000 | bytes 1000000 | tf_op jit(solution)/shard_map/attention/early/pallas_call | solution.py:139
  32.4 0.0 collective-permute-done.3.refs_1_
  32.4 0.0 collective-permute-done.4.refs_2_
  32.4 0.6 %collective-permute-done.5.refs_3_ = bf16[8,256]{1,0:T(8,128)(2,1)S(1)} collective-permute-done((bf16[8,256]{1,0:T(8,128)(2,1)S(1)}, bf16[8,256]{1,0:T(8,128)(2,1)S(1)}, u32[]{:S(2)}, u32[]{:S(2)}) %collective-permute-start.5) | collective-permute-done | bytes 4128 | tf_op jit(solution)/shard_map/attention/ppermute | solution.py:257
  33.0 1.4 %all-to-all-done.1.ret_ref = bf16[32,32,128]{2,1,0:T(8,128)(2,1)S(1)} async-done(((bf16[32,32,128]{2,1,0:T(8,128)(2,1)}), bf16[32,32,128]{2,1,0:T(8,128)(2,1)S(1)}, u32[]{:S(2)}, u32[]{:S(2)}) %all-to-all-start.1) | async-done | bytes 262176 | tf_op jit(solution)/shard_map/pooling/all_to_all | solution.py:275
  34.4 0.0 copy-done.1
  34.4 0.0 copy-start
  34.4 1.2 %copy-done = bf16[1024,512]{1,0:T(8,128)(2,1)S(1)} copy-done((bf16[1024,512]{1,0:T(8,128)(2,1)S(1)}, bf16[1024,512]{1,0:T(8,128)(2,1)}, u32[]{:S(2)}) %copy-start) | copy-done | bytes 1048600
  35.6 1.7 %score.1 = f32[4,8]{1,0:T(4,128)} custom-call(s32[1]{0:T(128)} %bitcast.me_ref, bf16[32,32,128]{2,1,0:T(8,128)(2,1)S(1)} %all-to-all-done.1.ret_ref, bf16[8,256]{1,0:T(8,128)(2,1)S(1)} %get-tuple-element.31.after_ref.refs_0_, bf16[8,256]{1,0:T(8,128)(2,1)S(1)} %collective-permute-done.3.refs_1_, bf16[8,256]{1,0:T(8,128)(2,1)S(1)} %collective-permute-done.4.refs_2_, ...), custom_call_target="tpu_custom_call" | custom-call | tf_op jit(solution)/shard_map/scoring/score/pallas_call | solution.py:240
  (1 shorter events, 0.0 us)
Async XLA Ops:
  0.0 11.7 %copy-start.10 = (bf16[256]{0:T(256)(128)(2,1)S(1)}, bf16[256]{0:T(256)(128)(2,1)}, u32[]{:S(2)}) copy-start(bf16[256]{0:T(256)(128)(2,1)} %param.29) | copy-start | bytes 1540
  0.0 16.2 %copy-start.4 = (bf16[1,8192,128]{2,1,0:T(8,128)(2,1)S(1)}, bf16[1,8192,128]{2,1,0:T(8,128)(2,1)}, u32[]{:S(2)}) copy-start(bf16[1,8192,128]{2,1,0:T(8,128)(2,1)} %param.20) | copy-start | bytes 6291460
  1.7 14.5 %all-to-all-start = ((s32[32,1,128]{2,1,0:T(1,128)}), s32[32,1,128]{2,1,0:T(1,128)S(1)}, u32[]{:S(2)}, u32[]{:S(2)}) async-start(s32[32,1,128]{2,1,0:T(1,128)} %get-tuple-element.21), calls=%async_computation | async-start | bytes 32768 | tf_op jit(solution)/shard_map/sending/all_to_all | solution.py:271
  9.0 12.2 %collective-permute-start = (bf16[8,256]{1,0:T(8,128)(2,1)S(1)}, bf16[8,256]{1,0:T(8,128)(2,1)S(1)}, u32[]{:S(2)}, u32[]{:S(2)}) collective-permute-start(bf16[8,256]{1,0:T(8,128)(2,1)S(1)} %get-tuple-element.23), channel_id=1, source_target_pairs={{0,1},{1,0},{2,3},{3,2},{4,5},{5,4},{6,7},{7,6},{8,9},{9,8},{10,11... | collective-permute-start | bytes 12296 | tf_op jit(solution)/shard_map/sending/ppermute | solution.py:257
  9.3 11.9 %collective-permute-start.1 = (bf16[8,256]{1,0:T(8,128)(2,1)S(1)}, bf16[8,256]{1,0:T(8,128)(2,1)S(1)}, u32[]{:S(2)}, u32[]{:S(2)}) collective-permute-start(bf16[8,256]{1,0:T(8,128)(2,1)S(1)} %get-tuple-element.24), channel_id=1, source_target_pairs={{0,2},{1,3},{2,0},{3,1},{4,6},{5,7},{6,4},{7,5},{8,10},{9,11},{10,... | collective-permute-start | bytes 12296 | tf_op jit(solution)/shard_map/sending/ppermute | solution.py:257
  11.0 10.2 %collective-permute-start.2 = (bf16[8,256]{1,0:T(8,128)(2,1)S(1)}, bf16[8,256]{1,0:T(8,128)(2,1)S(1)}, u32[]{:S(2)}, u32[]{:S(2)}) collective-permute-start(bf16[8,256]{1,0:T(8,128)(2,1)S(1)} %get-tuple-element.25), channel_id=1, source_target_pairs={{0,3},{1,2},{2,1},{3,0},{4,7},{5,6},{6,5},{7,4},{8,11},{9,10},{10,... | collective-permute-start | bytes 12296 | tf_op jit(solution)/shard_map/sending/ppermute | solution.py:257
  16.2 7.7 %copy-start.6 = (bf16[256,128]{1,0:T(8,128)(2,1)S(1)}, bf16[256,128]{1,0:T(8,128)(2,1)}, u32[]{:S(2)}) copy-start(bf16[256,128]{1,0:T(8,128)(2,1)} %refs_5_.1) | copy-start | bytes 196612
  16.2 7.7 %copy-start.7 = (bf16[256,128]{1,0:T(8,128)(2,1)S(1)}, bf16[256,128]{1,0:T(8,128)(2,1)}, u32[]{:S(2)}) copy-start(bf16[256,128]{1,0:T(8,128)(2,1)} %refs_6_.2) | copy-start | bytes 196612
  16.2 7.7 %copy-start.8 = (bf16[256,128]{1,0:T(8,128)(2,1)S(1)}, bf16[256,128]{1,0:T(8,128)(2,1)}, u32[]{:S(2)}) copy-start(bf16[256,128]{1,0:T(8,128)(2,1)} %refs_7_.2) | copy-start | bytes 196612
  16.2 7.7 %copy-start.9 = (bf16[128]{0:T(256)(128)(2,1)S(1)}, bf16[128]{0:T(256)(128)(2,1)}, u32[]{:S(2)}) copy-start(bf16[128]{0:T(256)(128)(2,1)} %param.25) | copy-start | bytes 772
  21.2 13.2 %all-to-all-start.1 = ((bf16[32,32,128]{2,1,0:T(8,128)(2,1)}), bf16[32,32,128]{2,1,0:T(8,128)(2,1)S(1)}, u32[]{:S(2)}, u32[]{:S(2)}) async-start(bf16[32,32,128]{2,1,0:T(8,128)(2,1)} %pool.1), calls=%async_computation.1 | async-start | bytes 524288 | tf_op jit(solution)/shard_map/pooling/all_to_all | solution.py:275
  23.8 1.0 %copy-start.5 = (bf16[1,1024,256]{2,1,0:T(8,128)(2,1)S(1)}, bf16[1,1024,256]{2,1,0:T(8,128)(2,1)}, u32[]{:S(2)}) copy-start(bf16[1,1024,256]{2,1,0:T(8,128)(2,1)} %param.15) | copy-start | bytes 1572868
  24.9 5.1 %copy-start.2 = (bf16[4,8,256]{2,1,0:T(8,128)(2,1)S(1)}, bf16[4,8,256]{2,1,0:T(8,128)(2,1)}, u32[]{:S(2)}) copy-start(bf16[4,8,256]{2,1,0:T(8,128)(2,1)} %target_ref.1) | copy-start | bytes 49156
  24.9 5.1 %copy-start.3 = (s32[4,8,64]{2,1,0:T(8,128)S(1)}, s32[4,8,64]{2,1,0:T(8,128)}, u32[]{:S(2)}) copy-start(s32[4,8,64]{2,1,0:T(8,128)} %leaf_ids_ref.1) | copy-start | bytes 24580
  28.1 6.3 %copy-start.1 = (bf16[512,256]{1,0:T(8,128)(2,1)S(1)}, bf16[512,256]{1,0:T(8,128)(2,1)}, u32[]{:S(2)}) copy-start(bf16[512,256]{1,0:T(8,128)(2,1)} %refs_7_.3) | copy-start | bytes 786436
  28.1 4.3 %collective-permute-start.3 = (bf16[8,256]{1,0:T(8,128)(2,1)S(1)}, bf16[8,256]{1,0:T(8,128)(2,1)S(1)}, u32[]{:S(2)}, u32[]{:S(2)}) collective-permute-start(bf16[8,256]{1,0:T(8,128)(2,1)S(1)} %get-tuple-element.32), channel_id=1, source_target_pairs={{0,1},{1,0},{2,3},{3,2},{4,5},{5,4},{6,7},{7,6},{8,9},{9,8},{10,11... | collective-permute-start | bytes 12296 | tf_op jit(solution)/shard_map/attention/ppermute | solution.py:257
  28.2 4.2 %collective-permute-start.4 = (bf16[8,256]{1,0:T(8,128)(2,1)S(1)}, bf16[8,256]{1,0:T(8,128)(2,1)S(1)}, u32[]{:S(2)}, u32[]{:S(2)}) collective-permute-start(bf16[8,256]{1,0:T(8,128)(2,1)S(1)} %get-tuple-element.33), channel_id=1, source_target_pairs={{0,2},{1,3},{2,0},{3,1},{4,6},{5,7},{6,4},{7,5},{8,10},{9,11},{10,... | collective-permute-start | bytes 12296 | tf_op jit(solution)/shard_map/attention/ppermute | solution.py:257
  29.9 3.1 %collective-permute-start.5 = (bf16[8,256]{1,0:T(8,128)(2,1)S(1)}, bf16[8,256]{1,0:T(8,128)(2,1)S(1)}, u32[]{:S(2)}, u32[]{:S(2)}) collective-permute-start(bf16[8,256]{1,0:T(8,128)(2,1)S(1)} %get-tuple-element.34), channel_id=1, source_target_pairs={{0,3},{1,2},{2,1},{3,0},{4,7},{5,6},{6,5},{7,4},{8,11},{9,10},{10,... | collective-permute-start | bytes 12296 | tf_op jit(solution)/shard_map/attention/ppermute | solution.py:257
  34.4 1.2 %copy-start = (bf16[1024,512]{1,0:T(8,128)(2,1)S(1)}, bf16[1024,512]{1,0:T(8,128)(2,1)}, u32[]{:S(2)}) copy-start(bf16[1024,512]{1,0:T(8,128)(2,1)} %refs_6_.3) | copy-start | bytes 3145732

commit v3 on v2

v3 whole, which is shorter than its diff:
```python
import functools

import jax
import jax.numpy as jnp
from jax import lax
from jax.experimental import pallas as pl
from jax.experimental.pallas import tpu as pltpu
from jax.sharding import PartitionSpec as P

SPLIT = 4
ALL = ("grp", "cand")
VMEM = pl.BlockSpec(memory_space=pltpu.VMEM)
HBM = pl.BlockSpec(memory_space=pltpu.HBM)
SMEM = pl.BlockSpec(memory_space=pltpu.SMEM)


def in_hbm(*arrays):
    return [pltpu.with_memory_space_constraint(a, pltpu.HBM) for a in arrays]


def dot(left, right, dims=((1,), (0,))):
    return lax.dot_general(left, right, (dims, ((), ())), preferred_element_type=jnp.float32)


def prepare_kernel(me_ref, bag_hbm, target_hbm, ids_ref, *refs):
    requests, per, bag_size, tables = bag_hbm.shape
    block_refs = refs[:requests]
    bag_ref, target_ref, sems = refs[requests:]
    copies = [pltpu.make_async_copy(bag_hbm, bag_ref, sems.at[0]), pltpu.make_async_copy(target_hbm, target_ref, sems.at[1])]
    for copy in copies:
        copy.start()
    for copy in copies:
        copy.wait()
    lines = jnp.concatenate([bag_ref[r, c] for r in range(requests) for c in range(per)], axis=0)
    by_table = lines.T
    for t in range(tables):
        for piece in range(SPLIT):
            ids_ref[t * SPLIT + piece] = by_table[t : t + 1, :]
    for k, block_ref in enumerate(block_refs):
        block_ref[...] = target_ref[me_ref[0] ^ k]


def prepare(me, bag_ids, target):
    requests, per, tables, bag_size = bag_ids.shape
    block = jax.ShapeDtypeStruct(target.shape[1:], target.dtype)
    out = pl.pallas_call(
        prepare_kernel,
        out_shape=[jax.ShapeDtypeStruct((tables * SPLIT, 1, requests * per * bag_size), jnp.int32)] + [block] * requests,
        in_specs=[SMEM, HBM, HBM],
        out_specs=[VMEM] * (1 + requests),
        scratch_shapes=[
            pltpu.VMEM((requests, per, bag_size, tables), jnp.int32),
            pltpu.VMEM(target.shape, target.dtype),
            pltpu.SemaphoreType.DMA((2,)),
        ],
        compiler_params=pltpu.CompilerParams(vmem_limit_bytes=12 << 20),
        cost_estimate=pl.CostEstimate(flops=30000000000, bytes_accessed=4 * 10**7, transcendentals=0),
        name="prepare",
    )(me, *in_hbm(jnp.transpose(bag_ids, (0, 1, 3, 2)), target))
    return out[0], out[1:]


GROUPS = 4


def pool_kernel(bag_size, count, quarter_ref, ids_ref, table_ref, *refs):
    theirs_ref, mine_ref = refs[count : count + 2]
    held_refs = refs[count + 2 : 2 * count + 2]
    scratch = refs[2 * count + 2 :]
    offsets, rows_f, sums, sems, fetch_sems = scratch[:5]
    scalars = scratch[5:]
    sources, _, lanes = ids_ref.shape
    rows = lanes // bag_size
    half = rows // 2
    step = sources // len(scalars)
    piece_rows, width = table_ref.shape
    local = ids_ref[...] - quarter_ref[0] * piece_rows
    offsets[...] = jnp.where((local >= 0) & (local < piece_rows), local, piece_rows)
    copies = [
        pltpu.make_async_copy(offsets.at[pl.ds(k * step, step)], scalar, sems.at[k]) for k, scalar in enumerate(scalars)
    ]
    for copy in copies:
        copy.start()
    rows_f[:piece_rows, :] = table_ref[...].astype(jnp.float32)
    rows_f[piece_rows:, :] = jnp.zeros((8, width), jnp.float32)
    fetches = []
    for k, (source, place) in enumerate(zip(refs[:count], held_refs)):
        skip = source.shape[0] - place.shape[0]
        source = source.at[pl.ds(skip, place.shape[0])] if skip else source
        fetches.append(pltpu.make_async_copy(source, place, fetch_sems.at[k]))
    for copy in copies:
        copy.wait()
    for fetch in fetches:
        fetch.start()

    def add_bags(sums_ref, first):
        def one_step(at, carry):
            for n in range(half):
                lane = (first + n) * bag_size
                for k, scalar in enumerate(scalars):
                    total = rows_f[pl.ds(scalar[at, 0, lane], 1), :]
                    for slot in range(1, bag_size):
                        total = total + rows_f[pl.ds(scalar[at, 0, lane + slot], 1), :]
                    sums_ref[k * step + at, n : n + 1, :] = total
            return carry

        lax.fori_loop(0, step, one_step, 0)

    for core in range(2):

        @pl.when(quarter_ref[0] % 2 == core)
        def _():
            add_bags(sums, (1 - core) * half)
            theirs_ref[...] = sums[...].astype(jnp.bfloat16)
            add_bags(mine_ref, core * half)

    for fetch in fetches:
        fetch.wait()


def pool(quarter, ids, table, bag_size, wanted, shapes):
    sources, _, lanes = ids.shape
    rows = lanes // bag_size
    piece_rows, width = table.shape
    half = (sources, rows // 2, width)
    out = pl.pallas_call(
        functools.partial(pool_kernel, bag_size, len(wanted)),
        out_shape=[jax.ShapeDtypeStruct(half, jnp.bfloat16), jax.ShapeDtypeStruct(half, jnp.float32)]
        + [pltpu.VMEM(shape, array.dtype) for array, shape in zip(wanted, shapes)],
        in_specs=[SMEM, VMEM, VMEM] + [HBM] * len(wanted),
        out_specs=[VMEM] * (2 + len(wanted)),
        scratch_shapes=[
            pltpu.VMEM(ids.shape, jnp.int32),
            pltpu.VMEM((piece_rows + 8, width), jnp.float32),
            pltpu.VMEM(half, jnp.float32),
            pltpu.SemaphoreType.DMA((GROUPS,)),
            pltpu.SemaphoreType.DMA((len(wanted),)),
        ]
        + [pltpu.SMEM((sources // GROUPS, 1, lanes), jnp.int32)] * GROUPS,
        compiler_params=pltpu.CompilerParams(vmem_limit_bytes=16 << 20),
        cost_estimate=pl.CostEstimate(flops=3 * 10**10, bytes_accessed=4 * 10**7, transcendentals=0),
        name="pool",
    )(quarter, ids, table, *in_hbm(*wanted))
    return out[0], out[1], out[2:]


def join_kernel(mine_ref, theirs_ref, out_ref):
    out_ref[...] = (mine_ref[...] + theirs_ref[...].astype(jnp.float32)).astype(jnp.bfloat16)


def join(mine, theirs):
    return pl.pallas_call(
        join_kernel,
        out_shape=jax.ShapeDtypeStruct(mine.shape, jnp.bfloat16),
        in_specs=[VMEM, VMEM],
        out_specs=VMEM,
        compiler_params=pltpu.CompilerParams(vmem_limit_bytes=4 << 20),
        name="join",
    )(mine, theirs)


def early_kernel(target_ref, leaf_ids_ref, leaf_ref, tail_ref, early_ref):
    requests, per, width = target_ref.shape
    rows = requests * per
    trees = leaf_ids_ref.shape[2]
    total = leaf_ref.shape[0]
    leaves = total // trees
    ids = leaf_ids_ref[...].reshape(rows, trees).astype(jnp.float32).astype(jnp.bfloat16)
    spread = lax.broadcasted_iota(jnp.int32, (trees, total), 1) // leaves == lax.broadcasted_iota(jnp.int32, (trees, total), 0)
    wide = dot(ids, spread.astype(jnp.float32).astype(jnp.bfloat16))
    leaf = (lax.broadcasted_iota(jnp.int32, (rows, total), 1) % leaves).astype(jnp.float32)
    chosen = jnp.where(wide == leaf, 1.0, 0.0).astype(jnp.bfloat16)
    leaf_vec = dot(chosen, leaf_ref[...]).astype(jnp.bfloat16)
    own = target_ref[...].reshape(rows, width)
    early_ref[...] = dot(own, tail_ref[:width, :]) + dot(leaf_vec, tail_ref[width:, :])


def early_part(target, leaf_ids, leaf_rows, tail):
    requests, per, width = target.shape
    return pl.pallas_call(
        early_kernel,
        out_shape=jax.ShapeDtypeStruct((requests * per, tail.shape[1]), jnp.float32),
        in_specs=[VMEM] * 4,
        out_specs=VMEM,
        compiler_params=pltpu.CompilerParams(vmem_limit_bytes=8 << 20),
        cost_estimate=pl.CostEstimate(flops=10**9, bytes_accessed=10**6, transcendentals=0),
        name="early",
    )(target, leaf_ids, leaf_rows, tail)


def attend_kernel(parts, block, tile, len_ref, *refs):
    q_refs = refs[:parts]
    h_ref, wq_ref, wk_ref, wp_ref, a_ref, w1_hbm = refs[parts : parts + 6]
    out_refs = refs[parts + 6 : 2 * parts + 6]
    head_ref, mixed, scores, sem = refs[2 * parts + 6 :]
    fetch_head = pltpu.make_async_copy(w1_hbm.at[pl.ds(0, head_ref.shape[0])], head_ref, sem)
    fetch_head.start()
    queries = jnp.concatenate([q[...].astype(jnp.float32) for q in q_refs], axis=0)
    items, width = queries.shape
    per = items // parts
    events = h_ref.shape[0]
    units = wq_ref.shape[1]
    pair_t = wp_ref[...].astype(jnp.float32).T
    key_t = wk_ref[...].astype(jnp.float32).T
    q_part = dot(wq_ref[...], queries.astype(jnp.bfloat16), ((0,), (1,)))
    a_col = a_ref[...].astype(jnp.float32).T
    for c in range(items):
        mixed[c * units : (c + 1) * units, :] = (key_t + pair_t * queries[c : c + 1, :]).astype(jnp.bfloat16)
    length = len_ref[0]
    for at in range(0, events, tile):
        part = h_ref[at : at + tile, :]
        for first in range(0, items, block):
            raw = dot(mixed[first * units : (first + block) * units, :], part, ((1,), (1,)))
            rows = []
            for c in range(block):
                unit = raw[c * units : (c + 1) * units, :] + q_part[:, first + c : first + c + 1]
                unit = jnp.maximum(unit, 0.0) * a_col
                rows.append(jnp.sum(unit, axis=0, keepdims=True))
            scores[first : first + block, at : at + tile] = jnp.concatenate(rows, axis=0)
    live = lax.broadcasted_iota(jnp.int32, (items, events), 1) < length
    live_scores = jnp.where(live, scores[...], 0.0).astype(jnp.bfloat16)
    weighted = dot(live_scores, h_ref[...])
    root = jnp.sqrt(jnp.full((1, width), length, jnp.int32).astype(jnp.float32))
    weighted = weighted * (1.0 / root)
    for k, out_ref in enumerate(out_refs):
        out_ref[...] = weighted[k * per : (k + 1) * per, :].astype(jnp.bfloat16)
    fetch_head.wait()


def attend(queries, history, length, w_query, w_key, w_pair, a_out, w_first):
    parts = len(queries)
    per, width = queries[0].shape
    items = parts * per
    events, units = history.shape[0], w_query.shape[1]
    out = pl.pallas_call(
        functools.partial(attend_kernel, parts, 8, min(256, events)),
        out_shape=[jax.ShapeDtypeStruct((per, width), jnp.bfloat16)] * parts
        + [pltpu.VMEM((w_first.shape[0] - 3 * width, w_first.shape[1]), w_first.dtype)],
        in_specs=[SMEM] + [VMEM] * (parts + 5) + [HBM],
        out_specs=[VMEM] * (parts + 1),
        scratch_shapes=[
            pltpu.VMEM((items * units, width), jnp.bfloat16),
            pltpu.VMEM((items, events), jnp.float32),
            pltpu.SemaphoreType.DMA,
        ],
        compiler_params=pltpu.CompilerParams(vmem_limit_bytes=12 << 20),
        cost_estimate=pl.CostEstimate(flops=10**9 * items, bytes_accessed=4 * 10**7, transcendentals=0),
        name="attend",
    )(length, *queries, history, w_query, w_key, w_pair, a_out.reshape(1, -1), *in_hbm(w_first))
    return out[:parts], out[parts]


def score_kernel(parts, me_ref, ret_ref, *refs):
    inter_refs = refs[:parts]
    early_ref, head_ref, w1_hbm, w2_hbm, w3_hbm, wo_ref, out_ref, pooled, interest, wi_ref, w2_ref, w3_ref, sems = refs[parts:]
    cut = head_ref.shape[0]
    fetches = [
        pltpu.make_async_copy(w1_hbm.at[pl.ds(cut, wi_ref.shape[0])], wi_ref, sems.at[0]),
        pltpu.make_async_copy(w2_hbm, w2_ref, sems.at[1]),
        pltpu.make_async_copy(w3_hbm, w3_ref, sems.at[2]),
    ]
    for fetch in fetches:
        fetch.start()
    sources, half, width = ret_ref.shape
    tables = sources // SPLIT
    rows = 2 * half
    per = rows // parts
    for k in range(parts):
        place = pl.multiple_of((me_ref[0] ^ k) * per, per)
        interest[pl.ds(place, per), :] = inter_refs[k][...].astype(jnp.float32)
    for t in range(tables):
        for core in range(2):
            total = ret_ref[t * SPLIT + core].astype(jnp.float32)
            for piece in range(core + 2, SPLIT, 2):
                total = total + ret_ref[t * SPLIT + piece].astype(jnp.float32)
            pooled[core * half : (core + 1) * half, t * width : (t + 1) * width] = total.astype(jnp.bfloat16)
    one = early_ref[...] + dot(pooled[...], head_ref[...])
    fetches[0].wait()
    one = one + dot(interest[...].astype(jnp.bfloat16), wi_ref[...])
    one = jnp.maximum(one, 0.0).astype(jnp.bfloat16)
    fetches[1].wait()
    two = jnp.maximum(dot(one, w2_ref[...]), 0.0).astype(jnp.bfloat16)
    fetches[2].wait()
    three = jnp.maximum(dot(two, w3_ref[...]), 0.0).astype(jnp.bfloat16)
    line = dot(wo_ref[...], three, ((1,), (1,)))
    for r in range(parts):
        out_ref[r : r + 1, :] = line[:, r * per : (r + 1) * per]


def score(me, returned, interest, early, w_head, w_first, w_second, w_third, w_out):
    sources, half, width = returned.shape
    rows = 2 * half
    parts = len(interest)
    return pl.pallas_call(
        functools.partial(score_kernel, parts),
        out_shape=jax.ShapeDtypeStruct((parts, rows // parts), jnp.float32),
        in_specs=[SMEM] + [VMEM] * (parts + 3) + [HBM] * 3 + [VMEM],
        out_specs=VMEM,
        scratch_shapes=[
            pltpu.VMEM((rows, sources // SPLIT * width), jnp.bfloat16),
            pltpu.VMEM((rows, interest[0].shape[1]), jnp.float32),
            pltpu.VMEM((interest[0].shape[1], w_first.shape[1]), w_first.dtype),
            pltpu.VMEM(w_second.shape, w_second.dtype),
            pltpu.VMEM(w_third.shape, w_third.dtype),
            pltpu.SemaphoreType.DMA((3,)),
        ],
        compiler_params=pltpu.CompilerParams(vmem_limit_bytes=12 << 20),
        name="score",
    )(me, returned, *interest, early, w_head, *in_hbm(w_first, w_second, w_third), w_out.reshape(1, -1))


def swap(blocks):
    size = len(blocks)
    return [blocks[0]] + [
        lax.ppermute(blocks[k], "cand", [(i, i ^ k) for i in range(size)]) for k in range(1, size)
    ]


def on_device(
    history, lengths, target, bag_ids, leaf_ids, table_piece, leaf_table,
    w_query, w_key, w_pair, a_out, w_first, w_second, w_third, w_out,
):
    me = lax.axis_index("cand").astype(jnp.int32).reshape(1)
    quarter = (lax.axis_index(ALL) % SPLIT).astype(jnp.int32).reshape(1)

    with jax.named_scope("sending"):
        outgoing, blocks = prepare(me, bag_ids, target)
        queries = swap(blocks)
        incoming = lax.all_to_all(outgoing, ALL, split_axis=0, concat_axis=0, tiled=True)
    with jax.named_scope("pooling"):
        width = target.shape[2]
        leaf_rows = leaf_table.reshape(-1, width)
        wanted = (leaf_rows, w_first, target, leaf_ids, history[0])
        shapes = (leaf_rows.shape, (2 * width, w_first.shape[1]), target.shape, leaf_ids.shape, history.shape[1:])
        for_other, mine, held = pool(quarter, incoming, table_piece[0], bag_ids.shape[3], wanted, shapes)
        for_other, queries = lax.optimization_barrier((for_other, queries))
        size = lax.axis_size("cand")
        other = lax.ppermute(for_other, "cand", [(i, i ^ 1) for i in range(size)])
        leaf_rows, tail, own, own_leaves, events = held
        early = early_part(own, own_leaves, leaf_rows, tail)
        other, early = lax.optimization_barrier((other, early))
        pair_sums = join(mine, other)
        pair_sums, queries = lax.optimization_barrier((pair_sums, queries))
        returned = lax.all_to_all(pair_sums, ALL, split_axis=0, concat_axis=0, tiled=True)
    with jax.named_scope("attention"):
        interest, w_head = attend(queries, events, lengths, w_query, w_key, w_pair, a_out, w_first)
        interest = swap(interest)
    with jax.named_scope("scoring"):
        return score(me, returned, interest, early, w_head, w_first, w_second, w_third, w_out)


def solution(mesh):
    placed = (
        P(ALL, None, None), P(ALL), P("grp", "cand", None), P("grp", "cand", None, None), P("grp", "cand", None),
        P(ALL, None, None),
    ) + (P(),) * 9
    return jax.shard_map(on_device, mesh=mesh, in_specs=placed, out_specs=P("grp", "cand"), check_vma=False)
```

time: 37.6 us -> 35.8 us (0.952)
  local copies, waits for them, and re-layouts: 2.3 us -> 0.04 us
  waiting for transfers between devices: 6.46 us -> 8.18 us
  Pallas kernels: 13.9 us -> 12.7 us
    ppermute x6, waiting for transfers between devices: 0.57 us -> 2.96 us  [swap(): lax.ppermute(blocks[k], 'cand', [(i, i ^ k) for i in range(size)])]
    pallas_call x2 -> x3, Pallas kernels: 7.39 us -> 5.07 us  [the longest x1 3.54 us: pool(): pl.pallas_call(functools.partial(pool_kernel, bag_size, len(wanted)), out...]
    unnamed x22 -> x12, local copies, waits for them, and re-layouts: 2.3 us -> 0.04 us
    all_to_all x1, waiting for transfers between devices: 1.43 us -> 0.07 us  [on_device(): lax.all_to_all(pair_sums, ALL, split_axis=0, concat_axis=0, tiled=True)]
    pallas_call x1, Pallas kernels: 1.67 us -> 2.69 us  [score(): pl.pallas_call(functools.partial(score_kernel, parts), out_shape=jax.Shap...]
    all_to_all x1, waiting for transfers between devices: 4.46 us -> 5.14 us  [on_device(): lax.all_to_all(outgoing, ALL, split_axis=0, concat_axis=0, tiled=True)]
  transfers between devices with their start and end apart: 8 -> 9, of which waited for: 3 -> 4; matrix products, arithmetic and copies ran while one was open for 0% -> 0% of each run, Pallas kernels for 28% -> 21%
where the time goes in v3:
time: 35.8 us; the launch traced here: 35.6 us
  starting transfers between devices  13.9 us (39%)
  Pallas kernels  12.7 us (35%)
  waiting for transfers between devices  8.18 us (23%)
  between operations  0.8 us (2%)
    all_to_all x1, starting transfers between devices, on_device(): lax.all_to_all(outgoing, ALL, split_axis=0, concat_axis=0, tiled=True)  7.3 us
    all_to_all x1, waiting for transfers between devices, on_device(): lax.all_to_all(outgoing, ALL, split_axis=0, concat_axis=0, tiled=True)  5.14 us
    ppermute x6, starting transfers between devices, swap(): lax.ppermute(blocks[k], 'cand', [(i, i ^ k) for i in range(size)])  3.93 us
    pallas_call x1, Pallas kernels, pool(): pl.pallas_call(functools.partial(pool_kernel, bag_size, len(wanted)), out...  3.54 us
    pallas_call x1, Pallas kernels, attend(): pl.pallas_call(functools.partial(attend_kernel, parts, 8, min(256, events...  3.25 us
    ppermute x6, waiting for transfers between devices, swap(): lax.ppermute(blocks[k], 'cand', [(i, i ^ k) for i in range(size)])  2.96 us
    pallas_call x1, Pallas kernels, score(): pl.pallas_call(functools.partial(score_kernel, parts), out_shape=jax.Shap...  2.69 us
    all_to_all x1, starting transfers between devices, on_device(): lax.all_to_all(pair_sums, ALL, split_axis=0, concat_axis=0, tiled=True)  2.56 us
  transfers between devices with their start and end apart: 9, of which 4 were waited for; matrix products, arithmetic and copies ran while one was open for 0% of the time, Pallas kernels for 21%

profile of v3, /device:TPU:0, one launch (start us, length us, event | category | flops | bytes accessed | tf_op | source)
XLA Modules:
  0.0 35.6 jit_solution(6237718780099827511)
XLA Ops:
  0.0 0.0 copy-start
  0.0 1.7 %prepare.1 = (s32[32,1,128]{2,1,0:T(1,128)}, bf16[8,256]{1,0:T(8,128)(2,1)S(1)}, bf16[8,256]{1,0:T(8,128)(2,1)S(1)}, bf16[8,256]{1,0:T(8,128)(2,1)S(1)}, bf16[8,256]{1,0:T(8,128)(2,1)S(1)}) custom-call(s32[1]{0:T(128)} %bitcast.me_ref, s32[4,8,4,8]{3,2,1,0:T(4,128)} %bitcast.11, bf16[4,8,256]{2,1,0:T(8,128)(2,1)} %refs_2_.1), custom_call_target="tpu_custom_call" | custom-call | flops 30000001024 | bytes 40000000 | tf_op jit(solution)/shard_map/sending/prepare/pallas_call | solution.py:46
  1.7 7.3 %all-to-all-start = ((s32[32,1,128]{2,1,0:T(1,128)}), s32[32,1,128]{2,1,0:T(1,128)S(1)}, u32[]{:S(2)}, u32[]{:S(2)}) async-start(s32[32,1,128]{2,1,0:T(1,128)} %get-tuple-element.34), calls=%async_computation | async-start | bytes 32768 | tf_op jit(solution)/shard_map/sending/all_to_all | solution.py:329
  9.0 0.3 collective-permute-start
  9.3 1.7 %collective-permute-start.1 = (bf16[8,256]{1,0:T(8,128)(2,1)S(1)}, bf16[8,256]{1,0:T(8,128)(2,1)S(1)}, u32[]{:S(2)}, u32[]{:S(2)}) collective-permute-start(bf16[8,256]{1,0:T(8,128)(2,1)S(1)} %get-tuple-element.39), channel_id=1, source_target_pairs={{0,2},{1,3},{2,0},{3,1},{4,6},{5,7},{6,4},{7,5},{8,10},{9,11},{10,... | collective-permute-start | bytes 12296 | tf_op jit(solution)/shard_map/sending/ppermute | solution.py:315
  11.0 0.0 collective-permute-start.2
  11.0 5.1 %all-to-all-done.ids_ref = s32[32,1,128]{2,1,0:T(1,128)S(1)} async-done(((s32[32,1,128]{2,1,0:T(1,128)}), s32[32,1,128]{2,1,0:T(1,128)S(1)}, u32[]{:S(2)}, u32[]{:S(2)}) %all-to-all-start) | async-done | bytes 16416 | tf_op jit(solution)/shard_map/sending/all_to_all | solution.py:329
  16.2 0.0 copy-done
  16.2 3.5 %pool.1 = (bf16[32,16,128]{2,1,0:T(8,128)(2,1)S(1)}, f32[32,16,128]{2,1,0:T(8,128)S(1)}, bf16[2048,256]{1,0:T(8,128)(2,1)S(1)}, bf16[512,1024]{1,0:T(8,128)(2,1)...) custom-call(s32[1]{0:T(128)} %bitcast.1.quarter_ref, ...), custom_call_target="tpu_custom_call" | custom-call | flops 30000001024 | bytes 40000000 | tf_op jit(solution)/shard_map/pooling/pool/pallas_call | solution.py:126
  19.7 0.0 collective-permute-done.refs_1_
  19.7 0.0 collective-permute-done.1.refs_2_
  19.7 0.0 collective-permute-done.2.refs_3_
  19.7 0.1 collective-permute-start.3
  20.5 0.0 copy-start.1
  20.5 0.0 copy-start.2
  20.5 0.0 copy-start.3
  20.5 0.0 copy-start.4
  20.5 0.8 %early.1.refs_4_ = f32[32,1024]{1,0:T(8,128)S(1)} custom-call(bf16[4,8,256]{2,1,0:T(8,128)(2,1)S(1)} %get-tuple-element.42.target_ref, s32[4,8,64]{2,1,0:T(8,128)S(1)} %get-tuple-element.43.leaf_ids_ref, bf16[2048,256]{1,0:T(8,128)(2,1)S(1)} %get-tuple-element.44.leaf_ref, bf16[512,1024]{1,0:T(8,128)(2,1)S(1)} %get-tuple-element.45.tail_ref), custom_call_target="tpu_custom_call" | custom-call | flops 1000000000 | bytes 1000000 | tf_op jit(solution)/shard_map/pooling/early/pallas_call | solution.py:180
  21.3 0.0 collective-permute-done.3.theirs_ref
  21.3 0.7 %join.1 = bf16[32,16,128]{2,1,0:T(8,128)(2,1)} custom-call(f32[32,16,128]{2,1,0:T(8,128)S(1)} %get-tuple-element.35.mine_ref, bf16[32,16,128]{2,1,0:T(8,128)(2,1)S(1)} %collective-permute-done.3.theirs_ref), custom_call_target="tpu_custom_call" | custom-call | tf_op jit(solution)/shard_map/pooling/join/pallas_call | solution.py:152
  22.0 2.6 %all-to-all-start.1 = ((bf16[32,16,128]{2,1,0:T(8,128)(2,1)}), bf16[32,16,128]{2,1,0:T(8,128)(2,1)S(1)}, u32[]{:S(2)}, u32[]{:S(2)}) async-start(bf16[32,16,128]{2,1,0:T(8,128)(2,1)} %join.1), calls=%async_computation.1 | async-start | bytes 262144 | tf_op jit(solution)/shard_map/pooling/all_to_all | solution.py:344
  24.6 0.0 copy-done.1
  24.6 0.0 copy-done.2
  24.6 0.0 copy-done.3
  24.6 0.0 copy-done.4
  24.7 0.0 copy-start.5
  24.7 3.2 %attend.1 = (bf16[8,256]{1,0:T(8,128)(2,1)S(1)}, bf16[8,256]{1,0:T(8,128)(2,1)S(1)}, bf16[8,256]{1,0:T(8,128)(2,1)S(1)}, bf16[8,256]{1,0:T(8,128)(2,1)S(1)}, bf16[1024,1024]{1,0:T(8,128)(2,1)S(1)}) custom-call(s32[1]{0:T(128)S(6)} %copy.16.len_ref, bf16[8,256]{1,0:T(8,128)(2,1)S(1)} %get-tuple-element.52.refs_0_, ...), custom_call_target="tpu_custom_call" | custom-call | flops 32000000000 | bytes 40000000 | tf_op jit(solution)/shard_map/attention/attend/pallas_call | solution.py:235
  27.9 0.3 collective-permute-start.4
  28.2 1.6 %collective-permute-start.5 = (bf16[8,256]{1,0:T(8,128)(2,1)S(1)}, bf16[8,256]{1,0:T(8,128)(2,1)S(1)}, u32[]{:S(2)}, u32[]{:S(2)}) collective-permute-start(bf16[8,256]{1,0:T(8,128)(2,1)S(1)} %get-tuple-element.59), channel_id=1, source_target_pairs={{0,2},{1,3},{2,0},{3,1},{4,6},{5,7},{6,4},{7,5},{8,10},{9,11},{10,... | collective-permute-start | bytes 12296 | tf_op jit(solution)/shard_map/attention/ppermute | solution.py:315
  29.8 0.1 collective-permute-start.6
  29.8 0.0 copy-done.5
  29.9 0.0 collective-permute-done.4.refs_1_
  29.9 2.0 %collective-permute-done.5.refs_2_ = bf16[8,256]{1,0:T(8,128)(2,1)S(1)} collective-permute-done((bf16[8,256]{1,0:T(8,128)(2,1)S(1)}, bf16[8,256]{1,0:T(8,128)(2,1)S(1)}, u32[]{:S(2)}, u32[]{:S(2)}) %collective-permute-start.5) | collective-permute-done | bytes 4128 | tf_op jit(solution)/shard_map/attention/ppermute | solution.py:315
  31.9 0.9 %collective-permute-done.6.refs_3_ = bf16[8,256]{1,0:T(8,128)(2,1)S(1)} collective-permute-done((bf16[8,256]{1,0:T(8,128)(2,1)S(1)}, bf16[8,256]{1,0:T(8,128)(2,1)S(1)}, u32[]{:S(2)}, u32[]{:S(2)}) %collective-permute-start.6) | collective-permute-done | bytes 4128 | tf_op jit(solution)/shard_map/attention/ppermute | solution.py:315
  32.8 0.1 all-to-all-done.1.ret_ref
  32.9 2.7 %score.1 = f32[4,8]{1,0:T(4,128)} custom-call(s32[1]{0:T(128)} %bitcast.me_ref, bf16[32,16,128]{2,1,0:T(8,128)(2,1)S(1)} %all-to-all-done.1.ret_ref, bf16[8,256]{1,0:T(8,128)(2,1)S(1)} %get-tuple-element.57.refs_0_, bf16[8,256]{1,0:T(8,128)(2,1)S(1)} %collective-permute-done.4.refs_1_, bf16[8,256]{1,0:T(8,128)(2,1)S(1)} %collective-permute-done.5.refs_2_, ...), custom_call_target="tpu_custom_call" | custom-call | tf_op jit(solution)/shard_map/scoring/score/pallas_call | solution.py:294
  (1 shorter events, 0.0 us)
Async XLA Ops:
  0.0 16.2 %copy-start = (bf16[1,8192,128]{2,1,0:T(8,128)(2,1)S(1)}, bf16[1,8192,128]{2,1,0:T(8,128)(2,1)}, u32[]{:S(2)}) copy-start(bf16[1,8192,128]{2,1,0:T(8,128)(2,1)} %param.20) | copy-start | bytes 6291460
  1.7 14.5 %all-to-all-start = ((s32[32,1,128]{2,1,0:T(1,128)}), s32[32,1,128]{2,1,0:T(1,128)S(1)}, u32[]{:S(2)}, u32[]{:S(2)}) async-start(s32[32,1,128]{2,1,0:T(1,128)} %get-tuple-element.34), calls=%async_computation | async-start | bytes 32768 | tf_op jit(solution)/shard_map/sending/all_to_all | solution.py:329
  9.0 10.7 %collective-permute-start = (bf16[8,256]{1,0:T(8,128)(2,1)S(1)}, bf16[8,256]{1,0:T(8,128)(2,1)S(1)}, u32[]{:S(2)}, u32[]{:S(2)}) collective-permute-start(bf16[8,256]{1,0:T(8,128)(2,1)S(1)} %get-tuple-element.38), channel_id=1, source_target_pairs={{0,1},{1,0},{2,3},{3,2},{4,5},{5,4},{6,7},{7,6},{8,9},{9,8},{10,11... | collective-permute-start | bytes 12296 | tf_op jit(solution)/shard_map/sending/ppermute | solution.py:315
  9.3 10.4 %collective-permute-start.1 = (bf16[8,256]{1,0:T(8,128)(2,1)S(1)}, bf16[8,256]{1,0:T(8,128)(2,1)S(1)}, u32[]{:S(2)}, u32[]{:S(2)}) collective-permute-start(bf16[8,256]{1,0:T(8,128)(2,1)S(1)} %get-tuple-element.39), channel_id=1, source_target_pairs={{0,2},{1,3},{2,0},{3,1},{4,6},{5,7},{6,4},{7,5},{8,10},{9,11},{10,... | collective-permute-start | bytes 12296 | tf_op jit(solution)/shard_map/sending/ppermute | solution.py:315
  11.0 8.7 %collective-permute-start.2 = (bf16[8,256]{1,0:T(8,128)(2,1)S(1)}, bf16[8,256]{1,0:T(8,128)(2,1)S(1)}, u32[]{:S(2)}, u32[]{:S(2)}) collective-permute-start(bf16[8,256]{1,0:T(8,128)(2,1)S(1)} %get-tuple-element.40), channel_id=1, source_target_pairs={{0,3},{1,2},{2,1},{3,0},{4,7},{5,6},{6,5},{7,4},{8,11},{9,10},{10,... | collective-permute-start | bytes 12296 | tf_op jit(solution)/shard_map/sending/ppermute | solution.py:315
  19.7 1.6 %collective-permute-start.3 = (bf16[32,16,128]{2,1,0:T(8,128)(2,1)S(1)}, bf16[32,16,128]{2,1,0:T(8,128)(2,1)S(1)}, u32[]{:S(2)}, u32[]{:S(2)}) collective-permute-start(bf16[32,16,128]{2,1,0:T(8,128)(2,1)S(1)} %get-tuple-element.41), channel_id=1, source_target_pairs={{0,1},{1,0},{2,3},{3,2},{4,5},{5,4},{6,7},{7,6},{8,9},{9,8},{10,11... | collective-permute-start | bytes 393224 | tf_op jit(solution)/shard_map/pooling/ppermute | solution.py:338
  20.5 4.2 %copy-start.1 = (bf16[256,128]{1,0:T(8,128)(2,1)S(1)}, bf16[256,128]{1,0:T(8,128)(2,1)}, u32[]{:S(2)}) copy-start(bf16[256,128]{1,0:T(8,128)(2,1)} %refs_5_.1) | copy-start | bytes 196612
  20.5 4.2 %copy-start.2 = (bf16[256,128]{1,0:T(8,128)(2,1)S(1)}, bf16[256,128]{1,0:T(8,128)(2,1)}, u32[]{:S(2)}) copy-start(bf16[256,128]{1,0:T(8,128)(2,1)} %refs_6_.2) | copy-start | bytes 196612
  20.5 4.2 %copy-start.3 = (bf16[256,128]{1,0:T(8,128)(2,1)S(1)}, bf16[256,128]{1,0:T(8,128)(2,1)}, u32[]{:S(2)}) copy-start(bf16[256,128]{1,0:T(8,128)(2,1)} %refs_7_.2) | copy-start | bytes 196612
  20.5 4.2 %copy-start.4 = (bf16[128]{0:T(256)(128)(2,1)S(1)}, bf16[128]{0:T(256)(128)(2,1)}, u32[]{:S(2)}) copy-start(bf16[128]{0:T(256)(128)(2,1)} %param.25) | copy-start | bytes 772
  22.0 10.8 %all-to-all-start.1 = ((bf16[32,16,128]{2,1,0:T(8,128)(2,1)}), bf16[32,16,128]{2,1,0:T(8,128)(2,1)S(1)}, u32[]{:S(2)}, u32[]{:S(2)}) async-start(bf16[32,16,128]{2,1,0:T(8,128)(2,1)} %join.1), calls=%async_computation.1 | async-start | bytes 262144 | tf_op jit(solution)/shard_map/pooling/all_to_all | solution.py:344
  24.7 5.2 %copy-start.5 = (bf16[256]{0:T(256)(128)(2,1)S(1)}, bf16[256]{0:T(256)(128)(2,1)}, u32[]{:S(2)}) copy-start(bf16[256]{0:T(256)(128)(2,1)} %param.29) | copy-start | bytes 1540
  27.9 1.9 %collective-permute-start.4 = (bf16[8,256]{1,0:T(8,128)(2,1)S(1)}, bf16[8,256]{1,0:T(8,128)(2,1)S(1)}, u32[]{:S(2)}, u32[]{:S(2)}) collective-permute-start(bf16[8,256]{1,0:T(8,128)(2,1)S(1)} %get-tuple-element.58), channel_id=1, source_target_pairs={{0,1},{1,0},{2,3},{3,2},{4,5},{5,4},{6,7},{7,6},{8,9},{9,8},{10,11... | collective-permute-start | bytes 12296 | tf_op jit(solution)/shard_map/attention/ppermute | solution.py:315
  28.2 3.6 %collective-permute-start.5 = (bf16[8,256]{1,0:T(8,128)(2,1)S(1)}, bf16[8,256]{1,0:T(8,128)(2,1)S(1)}, u32[]{:S(2)}, u32[]{:S(2)}) collective-permute-start(bf16[8,256]{1,0:T(8,128)(2,1)S(1)} %get-tuple-element.59), channel_id=1, source_target_pairs={{0,2},{1,3},{2,0},{3,1},{4,6},{5,7},{6,4},{7,5},{8,10},{9,11},{10,... | collective-permute-start | bytes 12296 | tf_op jit(solution)/shard_map/attention/ppermute | solution.py:315
  29.8 3.0 %collective-permute-start.6 = (bf16[8,256]{1,0:T(8,128)(2,1)S(1)}, bf16[8,256]{1,0:T(8,128)(2,1)S(1)}, u32[]{:S(2)}, u32[]{:S(2)}) collective-permute-start(bf16[8,256]{1,0:T(8,128)(2,1)S(1)} %get-tuple-element.60), channel_id=1, source_target_pairs={{0,3},{1,2},{2,1},{3,0},{4,7},{5,6},{6,5},{7,4},{8,11},{9,10},{10,... | collective-permute-start | bytes 12296 | tf_op jit(solution)/shard_map/attention/ppermute | solution.py:315

commit v4 on v3

--- a/solution.py
+++ b/solution.py
@@ -53,7 +53,7 @@
             pltpu.VMEM(target.shape, target.dtype),
             pltpu.SemaphoreType.DMA((2,)),
         ],
-        compiler_params=pltpu.CompilerParams(vmem_limit_bytes=12 << 20),
+        compiler_params=pltpu.CompilerParams(vmem_limit_bytes=16 << 20),
         cost_estimate=pl.CostEstimate(flops=30000000000, bytes_accessed=4 * 10**7, transcendentals=0),
         name="prepare",
     )(me, *in_hbm(jnp.transpose(bag_ids, (0, 1, 3, 2)), target))
@@ -63,17 +63,32 @@
 GROUPS = 4
 
 
-def pool_kernel(bag_size, count, quarter_ref, ids_ref, table_ref, *refs):
-    theirs_ref, mine_ref = refs[count : count + 2]
-    held_refs = refs[count + 2 : 2 * count + 2]
-    scratch = refs[2 * count + 2 :]
-    offsets, rows_f, sums, sems, fetch_sems = scratch[:5]
-    scalars = scratch[5:]
-    sources, _, lanes = ids_ref.shape
-    rows = lanes // bag_size
-    half = rows // 2
-    step = sources // len(scalars)
+def add_bags(bag_size, first, scalars, rows_f, sums):
+    step, half = scalars[0].shape[0], sums.shape[1]
+
+    def one_step(at, carry):
+        for n in range(half):
+            lane = (first + n) * bag_size
+            for k, scalar in enumerate(scalars):
+                total = rows_f[pl.ds(scalar[at, 0, lane], 1), :]
+                for slot in range(1, bag_size):
+                    total = total + rows_f[pl.ds(scalar[at, 0, lane + slot], 1), :]
+                sums[k * step + at, n : n + 1, :] = total
+        return carry
+
+    lax.fori_loop(0, step, one_step, 0)
+
+
+def spread_rows(table_ref, rows_f):
     piece_rows, width = table_ref.shape
+    rows_f[:piece_rows, :] = table_ref[...].astype(jnp.float32)
+    rows_f[piece_rows:, :] = jnp.zeros((8, width), jnp.float32)
+
+
+def pool_other_kernel(bag_size, quarter_ref, ids_ref, table_ref, out_ref, *refs):
+    scalars = refs[:GROUPS]
+    offsets, rows_f, sums, sems = refs[GROUPS:]
+    step, half, piece_rows = ids_ref.shape[0] // GROUPS, out_ref.shape[1], table_ref.shape[0]
     local = ids_ref[...] - quarter_ref[0] * piece_rows
     offsets[...] = jnp.where((local >= 0) & (local < piece_rows), local, piece_rows)
     copies = [
@@ -81,67 +96,72 @@
     ]
     for copy in copies:
         copy.start()
-    rows_f[:piece_rows, :] = table_ref[...].astype(jnp.float32)
-    rows_f[piece_rows:, :] = jnp.zeros((8, width), jnp.float32)
-    fetches = []
-    for k, (source, place) in enumerate(zip(refs[:count], held_refs)):
-        skip = source.shape[0] - place.shape[0]
-        source = source.at[pl.ds(skip, place.shape[0])] if skip else source
-        fetches.append(pltpu.make_async_copy(source, place, fetch_sems.at[k]))
+    spread_rows(table_ref, rows_f)
     for copy in copies:
         copy.wait()
-    for fetch in fetches:
-        fetch.start()
-
-    def add_bags(sums_ref, first):
-        def one_step(at, carry):
-            for n in range(half):
-                lane = (first + n) * bag_size
-                for k, scalar in enumerate(scalars):
-                    total = rows_f[pl.ds(scalar[at, 0, lane], 1), :]
-                    for slot in range(1, bag_size):
-                        total = total + rows_f[pl.ds(scalar[at, 0, lane + slot], 1), :]
-                    sums_ref[k * step + at, n : n + 1, :] = total
-            return carry
-
-        lax.fori_loop(0, step, one_step, 0)
-
     for core in range(2):
 
         @pl.when(quarter_ref[0] % 2 == core)
         def _():
-            add_bags(sums, (1 - core) * half)
-            theirs_ref[...] = sums[...].astype(jnp.bfloat16)
-            add_bags(mine_ref, core * half)
-
-    for fetch in fetches:
-        fetch.wait()
-
-
-def pool(quarter, ids, table, bag_size, wanted, shapes):
+            add_bags(bag_size, (1 - core) * half, scalars, rows_f, sums)
+
+    out_ref[...] = sums[...].astype(out_ref.dtype)
+
+
+def pool_other(quarter, ids, table, bag_size):
     sources, _, lanes = ids.shape
-    rows = lanes // bag_size
     piece_rows, width = table.shape
-    half = (sources, rows // 2, width)
+    half = (sources, lanes // bag_size // 2, width)
     out = pl.pallas_call(
-        functools.partial(pool_kernel, bag_size, len(wanted)),
-        out_shape=[jax.ShapeDtypeStruct(half, jnp.bfloat16), jax.ShapeDtypeStruct(half, jnp.float32)]
-        + [pltpu.VMEM(shape, array.dtype) for array, shape in zip(wanted, shapes)],
-        in_specs=[SMEM, VMEM, VMEM] + [HBM] * len(wanted),
-        out_specs=[VMEM] * (2 + len(wanted)),
+        functools.partial(pool_other_kernel, bag_size),
+        out_shape=[jax.ShapeDtypeStruct(half, jnp.bfloat16)]
+        + [pltpu.SMEM((sources // GROUPS, 1, lanes), jnp.int32)] * GROUPS,
+        in_specs=[SMEM, VMEM, VMEM],
+        out_specs=[VMEM] + [SMEM] * GROUPS,
         scratch_shapes=[
             pltpu.VMEM(ids.shape, jnp.int32),
             pltpu.VMEM((piece_rows + 8, width), jnp.float32),
             pltpu.VMEM(half, jnp.float32),
             pltpu.SemaphoreType.DMA((GROUPS,)),
-            pltpu.SemaphoreType.DMA((len(wanted),)),
-        ]
-        + [pltpu.SMEM((sources // GROUPS, 1, lanes), jnp.int32)] * GROUPS,
+        ],
         compiler_params=pltpu.CompilerParams(vmem_limit_bytes=16 << 20),
         cost_estimate=pl.CostEstimate(flops=3 * 10**10, bytes_accessed=4 * 10**7, transcendentals=0),
-        name="pool",
-    )(quarter, ids, table, *in_hbm(*wanted))
-    return out[0], out[1], out[2:]
+        name="pool_other",
+    )(quarter, ids, table)
+    return out[0], out[1:]
+
+
+def pool_own_kernel(bag_size, quarter_ref, *refs):
+    scalars = refs[:GROUPS]
+    table_ref, history_hbm, out_ref, history_ref, rows_f, sem = refs[GROUPS:]
+    fetch = pltpu.make_async_copy(history_hbm, history_ref, sem)
+    fetch.start()
+    spread_rows(table_ref, rows_f)
+    for core in range(2):
+
+        @pl.when(quarter_ref[0] % 2 == core)
+        def _():
+            add_bags(bag_size, core * out_ref.shape[1], scalars, rows_f, out_ref)
+
+    fetch.wait()
+
+
+def pool_own(quarter, scalars, table, history, bag_size):
+    step, _, lanes = scalars[0].shape
+    piece_rows, width = table.shape
+    return pl.pallas_call(
+        functools.partial(pool_own_kernel, bag_size),
+        out_shape=[
+            jax.ShapeDtypeStruct((step * GROUPS, lanes // bag_size // 2, width), jnp.float32),
+            pltpu.VMEM(history.shape, history.dtype),
+        ],
+        in_specs=[SMEM] * (1 + GROUPS) + [VMEM, HBM],
+        out_specs=[VMEM, VMEM],
+        scratch_shapes=[pltpu.VMEM((piece_rows + 8, width), jnp.float32), pltpu.SemaphoreType.DMA],
+        compiler_params=pltpu.CompilerParams(vmem_limit_bytes=16 << 20),
+        cost_estimate=pl.CostEstimate(flops=3 * 10**10, bytes_accessed=4 * 10**7, transcendentals=0),
+        name="pool_own",
+    )(quarter, *scalars, table, *in_hbm(history))
 
 
 def join_kernel(mine_ref, theirs_ref, out_ref):
@@ -159,8 +179,17 @@
     )(mine, theirs)
 
 
-def early_kernel(target_ref, leaf_ids_ref, leaf_ref, tail_ref, early_ref):
+def early_kernel(
+    after_ref, target_ref, leaf_ids_ref, leaf_hbm, w1_hbm, w2_hbm, early_ref, w2_ref, leaf_ref, tail_ref, sems
+):
     requests, per, width = target_ref.shape
+    skip = w1_hbm.shape[0] - tail_ref.shape[0]
+    moves = (
+        (leaf_hbm, leaf_ref), (w1_hbm.at[pl.ds(skip, tail_ref.shape[0])], tail_ref), (w2_hbm, w2_ref),
+    )
+    fetches = [pltpu.make_async_copy(source, place, sems.at[k]) for k, (source, place) in enumerate(moves)]
+    for fetch in fetches:
+        fetch.start()
     rows = requests * per
     trees = leaf_ids_ref.shape[2]
     total = leaf_ref.shape[0]
@@ -170,22 +199,34 @@
     wide = dot(ids, spread.astype(jnp.float32).astype(jnp.bfloat16))
     leaf = (lax.broadcasted_iota(jnp.int32, (rows, total), 1) % leaves).astype(jnp.float32)
     chosen = jnp.where(wide == leaf, 1.0, 0.0).astype(jnp.bfloat16)
+    fetches[0].wait()
     leaf_vec = dot(chosen, leaf_ref[...]).astype(jnp.bfloat16)
     own = target_ref[...].reshape(rows, width)
+    fetches[1].wait()
     early_ref[...] = dot(own, tail_ref[:width, :]) + dot(leaf_vec, tail_ref[width:, :])
-
-
-def early_part(target, leaf_ids, leaf_rows, tail):
+    fetches[2].wait()
+
+
+def early_part(after, target, leaf_ids, leaf_rows, w_first, w_second):
     requests, per, width = target.shape
+    hidden = w_first.shape[1]
     return pl.pallas_call(
         early_kernel,
-        out_shape=jax.ShapeDtypeStruct((requests * per, tail.shape[1]), jnp.float32),
-        in_specs=[VMEM] * 4,
-        out_specs=VMEM,
+        out_shape=[
+            jax.ShapeDtypeStruct((requests * per, hidden), jnp.float32),
+            pltpu.VMEM(w_second.shape, w_second.dtype),
+        ],
+        in_specs=[HBM, VMEM, VMEM] + [HBM] * 3,
+        out_specs=[VMEM] * 2,
+        scratch_shapes=[
+            pltpu.VMEM(leaf_rows.shape, leaf_rows.dtype),
+            pltpu.VMEM((2 * width, hidden), w_first.dtype),
+            pltpu.SemaphoreType.DMA((3,)),
+        ],
         compiler_params=pltpu.CompilerParams(vmem_limit_bytes=8 << 20),
         cost_estimate=pl.CostEstimate(flops=10**9, bytes_accessed=10**6, transcendentals=0),
         name="early",
-    )(target, leaf_ids, leaf_rows, tail)
+    )(after, target, leaf_ids, *in_hbm(leaf_rows, w_first, w_second))
 
 
 def attend_kernel(parts, block, tile, len_ref, *refs):
@@ -206,7 +247,6 @@
     a_col = a_ref[...].astype(jnp.float32).T
     for c in range(items):
         mixed[c * units : (c + 1) * units, :] = (key_t + pair_t * queries[c : c + 1, :]).astype(jnp.bfloat16)
-    length = len_ref[0]
     for at in range(0, events, tile):
         part = h_ref[at : at + tile, :]
         for first in range(0, items, block):
@@ -217,10 +257,11 @@
                 unit = jnp.maximum(unit, 0.0) * a_col
                 rows.append(jnp.sum(unit, axis=0, keepdims=True))
             scores[first : first + block, at : at + tile] = jnp.concatenate(rows, axis=0)
+    length = len_ref[...]
     live = lax.broadcasted_iota(jnp.int32, (items, events), 1) < length
     live_scores = jnp.where(live, scores[...], 0.0).astype(jnp.bfloat16)
     weighted = dot(live_scores, h_ref[...])
-    root = jnp.sqrt(jnp.full((1, width), length, jnp.int32).astype(jnp.float32))
+    root = jnp.sqrt(jnp.broadcast_to(length.astype(jnp.float32), (1, width)))
     weighted = weighted * (1.0 / root)
     for k, out_ref in enumerate(out_refs):
         out_ref[...] = weighted[k * per : (k + 1) * per, :].astype(jnp.bfloat16)
@@ -236,28 +277,26 @@
         functools.partial(attend_kernel, parts, 8, min(256, events)),
         out_shape=[jax.ShapeDtypeStruct((per, width), jnp.bfloat16)] * parts
         + [pltpu.VMEM((w_first.shape[0] - 3 * width, w_first.shape[1]), w_first.dtype)],
-        in_specs=[SMEM] + [VMEM] * (parts + 5) + [HBM],
+        in_specs=[VMEM] * (parts + 6) + [HBM],
         out_specs=[VMEM] * (parts + 1),
         scratch_shapes=[
             pltpu.VMEM((items * units, width), jnp.bfloat16),
             pltpu.VMEM((items, events), jnp.float32),
             pltpu.SemaphoreType.DMA,
         ],
-        compiler_params=pltpu.CompilerParams(vmem_limit_bytes=12 << 20),
+        compiler_params=pltpu.CompilerParams(vmem_limit_bytes=16 << 20),
         cost_estimate=pl.CostEstimate(flops=10**9 * items, bytes_accessed=4 * 10**7, transcendentals=0),
         name="attend",
-    )(length, *queries, history, w_query, w_key, w_pair, a_out.reshape(1, -1), *in_hbm(w_first))
+    )(length.reshape(1, 1), *queries, history, w_query, w_key, w_pair, a_out.reshape(1, -1), *in_hbm(w_first))
     return out[:parts], out[parts]
 
 
 def score_kernel(parts, me_ref, ret_ref, *refs):
     inter_refs = refs[:parts]
-    early_ref, head_ref, w1_hbm, w2_hbm, w3_hbm, wo_ref, out_ref, pooled, interest, wi_ref, w2_ref, w3_ref, sems = refs[parts:]
-    cut = head_ref.shape[0]
+    early_ref, head_ref, w1_hbm, w2_ref, w3_hbm, wo_ref, out_ref, pooled, interest, wi_ref, w3_ref, sems = refs[parts:]
     fetches = [
-        pltpu.make_async_copy(w1_hbm.at[pl.ds(cut, wi_ref.shape[0])], wi_ref, sems.at[0]),
-        pltpu.make_async_copy(w2_hbm, w2_ref, sems.at[1]),
-        pltpu.make_async_copy(w3_hbm, w3_ref, sems.at[2]),
+        pltpu.make_async_copy(w1_hbm.at[pl.ds(head_ref.shape[0], wi_ref.shape[0])], wi_ref, sems.at[0]),
+        pltpu.make_async_copy(w3_hbm, w3_ref, sems.at[1]),
     ]
     for fetch in fetches:
         fetch.start()
@@ -278,9 +317,8 @@
     fetches[0].wait()
     one = one + dot(interest[...].astype(jnp.bfloat16), wi_ref[...])
     one = jnp.maximum(one, 0.0).astype(jnp.bfloat16)
+    two = jnp.maximum(dot(one, w2_ref[...]), 0.0).astype(jnp.bfloat16)
     fetches[1].wait()
-    two = jnp.maximum(dot(one, w2_ref[...]), 0.0).astype(jnp.bfloat16)
-    fetches[2].wait()
     three = jnp.maximum(dot(two, w3_ref[...]), 0.0).astype(jnp.bfloat16)
     line = dot(wo_ref[...], three, ((1,), (1,)))
     for r in range(parts):
@@ -294,19 +332,18 @@
     return pl.pallas_call(
         functools.partial(score_kernel, parts),
         out_shape=jax.ShapeDtypeStruct((parts, rows // parts), jnp.float32),
-        in_specs=[SMEM] + [VMEM] * (parts + 3) + [HBM] * 3 + [VMEM],
+        in_specs=[SMEM] + [VMEM] * (parts + 3) + [HBM, VMEM, HBM, VMEM],
         out_specs=VMEM,
         scratch_shapes=[
             pltpu.VMEM((rows, sources // SPLIT * width), jnp.bfloat16),
             pltpu.VMEM((rows, interest[0].shape[1]), jnp.float32),
             pltpu.VMEM((interest[0].shape[1], w_first.shape[1]), w_first.dtype),
-            pltpu.VMEM(w_second.shape, w_second.dtype),
             pltpu.VMEM(w_third.shape, w_third.dtype),
-            pltpu.SemaphoreType.DMA((3,)),
-        ],
-        compiler_params=pltpu.CompilerParams(vmem_limit_bytes=12 << 20),
+            pltpu.SemaphoreType.DMA((2,)),
+        ],
+        compiler_params=pltpu.CompilerParams(vmem_limit_bytes=16 << 20),
         name="score",
-    )(me, returned, *interest, early, w_head, *in_hbm(w_first, w_second, w_third), w_out.reshape(1, -1))
+    )(me, returned, *interest, early, w_head, *in_hbm(w_first), w_second, *in_hbm(w_third), w_out.reshape(1, -1))
 
 
 def swap(blocks):
@@ -328,25 +365,23 @@
         queries = swap(blocks)
         incoming = lax.all_to_all(outgoing, ALL, split_axis=0, concat_axis=0, tiled=True)
     with jax.named_scope("pooling"):
-        width = target.shape[2]
-        leaf_rows = leaf_table.reshape(-1, width)
-        wanted = (leaf_rows, w_first, target, leaf_ids, history[0])
-        shapes = (leaf_rows.shape, (2 * width, w_first.shape[1]), target.shape, leaf_ids.shape, history.shape[1:])
-        for_other, mine, held = pool(quarter, incoming, table_piece[0], bag_ids.shape[3], wanted, shapes)
+        bag_size = bag_ids.shape[3]
+        for_other, scalars = pool_other(quarter, incoming, table_piece[0], bag_size)
         for_other, queries = lax.optimization_barrier((for_other, queries))
         size = lax.axis_size("cand")
         other = lax.ppermute(for_other, "cand", [(i, i ^ 1) for i in range(size)])
-        leaf_rows, tail, own, own_leaves, events = held
-        early = early_part(own, own_leaves, leaf_rows, tail)
-        other, early = lax.optimization_barrier((other, early))
+        mine, events = pool_own(quarter, scalars, table_piece[0], history[0], bag_size)
         pair_sums = join(mine, other)
         pair_sums, queries = lax.optimization_barrier((pair_sums, queries))
         returned = lax.all_to_all(pair_sums, ALL, split_axis=0, concat_axis=0, tiled=True)
     with jax.named_scope("attention"):
         interest, w_head = attend(queries, events, lengths, w_query, w_key, w_pair, a_out, w_first)
+        leaf_rows = leaf_table.reshape(-1, leaf_table.shape[2])
+        early, w2 = early_part(interest[0], target, leaf_ids, leaf_rows, w_first, w_second)
+        w_out, early = lax.optimization_barrier((w_out, early))
         interest = swap(interest)
     with jax.named_scope("scoring"):
-        return score(me, returned, interest, early, w_head, w_first, w_second, w_third, w_out)
+        return score(me, returned, interest, early, w_head, w_first, w2, w_third, w_out)
 
 
 def solution(mesh):

time: 35.8 us -> 34.4 us (0.961)
  waiting for transfers between devices: 8.18 us -> 5.35 us
  Pallas kernels: 12.7 us -> 14 us
    ppermute x6, waiting for transfers between devices: 2.96 us -> 0.86 us  [swap(): lax.ppermute(blocks[k], 'cand', [(i, i ^ k) for i in range(size)])]
    pallas_call x2 -> x3, Pallas kernels: 4.37 us -> 5.87 us  [the longest x1 2.23 us: pool_other(): pl.pallas_call(functools.partial(pool_other_kernel, bag_size), out_shape=...]
    all_to_all x1, waiting for transfers between devices: 5.14 us -> 4.48 us  [on_device(): lax.all_to_all(outgoing, ALL, split_axis=0, concat_axis=0, tiled=True)]
  transfers between devices with their start and end apart: 9 -> 9, of which waited for: 4 -> 2; matrix products, arithmetic and copies ran while one was open for 0% -> 0% of each run, Pallas kernels for 21% -> 27%
where the time goes in v4:
time: 34.4 us; the launch traced here: 34.1 us
  Pallas kernels  14 us (41%)
  starting transfers between devices  13.9 us (40%)
  waiting for transfers between devices  5.35 us (16%)
  between operations  0.87 us (3%)
    all_to_all x1, starting transfers between devices, on_device(): lax.all_to_all(outgoing, ALL, split_axis=0, concat_axis=0, tiled=True)  7.3 us
    all_to_all x1, waiting for transfers between devices, on_device(): lax.all_to_all(outgoing, ALL, split_axis=0, concat_axis=0, tiled=True)  4.48 us
    ppermute x6, starting transfers between devices, swap(): lax.ppermute(blocks[k], 'cand', [(i, i ^ k) for i in range(size)])  3.93 us
    pallas_call x1, Pallas kernels, attend(): pl.pallas_call(functools.partial(attend_kernel, parts, 8, min(256, events...  3.3 us
    all_to_all x1, starting transfers between devices, on_device(): lax.all_to_all(pair_sums, ALL, split_axis=0, concat_axis=0, tiled=True)  2.56 us
    pallas_call x1, Pallas kernels, score(): pl.pallas_call(functools.partial(score_kernel, parts), out_shape=jax.Shap...  2.45 us
    pallas_call x1, Pallas kernels, pool_other(): pl.pallas_call(functools.partial(pool_other_kernel, bag_size), out_shape=...  2.23 us
    pallas_call x1, Pallas kernels, early_part(): pl.pallas_call(early_kernel, out_shape=[jax.ShapeDtypeStruct((requests *...  2.05 us
  transfers between devices with their start and end apart: 9, of which 2 were waited for; matrix products, arithmetic and copies ran while one was open for 0% of the time, Pallas kernels for 27%

profile of v4, /device:TPU:0, one launch (start us, length us, event | category | flops | bytes accessed | tf_op | source)
XLA Modules:
  0.0 34.1 jit_solution(3475751524937562715)
XLA Ops:
  0.0 0.0 copy-start.2
  0.0 1.7 %prepare.1 = (s32[32,1,128]{2,1,0:T(1,128)}, bf16[8,256]{1,0:T(8,128)(2,1)S(1)}, bf16[8,256]{1,0:T(8,128)(2,1)S(1)}, bf16[8,256]{1,0:T(8,128)(2,1)S(1)}, bf16[8,256]{1,0:T(8,128)(2,1)S(1)}) custom-call(s32[1]{0:T(128)} %bitcast.me_ref, s32[4,8,4,8]{3,2,1,0:T(4,128)} %bitcast.14, bf16[4,8,256]{2,1,0:T(8,128)(2,1)} %target_ref.1), custom_call_target="tpu_custom_call" | custom-call | flops 30000001024 | bytes 40000000 | tf_op jit(solution)/shard_map/sending/prepare/pallas_call | solution.py:46
  1.7 7.3 %all-to-all-start = ((s32[32,1,128]{2,1,0:T(1,128)}), s32[32,1,128]{2,1,0:T(1,128)S(1)}, u32[]{:S(2)}, u32[]{:S(2)}) async-start(s32[32,1,128]{2,1,0:T(1,128)} %get-tuple-element.36), calls=%async_computation | async-start | bytes 32768 | tf_op jit(solution)/shard_map/sending/all_to_all | solution.py:366
  9.0 0.3 collective-permute-start
  9.3 1.7 %collective-permute-start.1 = (bf16[8,256]{1,0:T(8,128)(2,1)S(1)}, bf16[8,256]{1,0:T(8,128)(2,1)S(1)}, u32[]{:S(2)}, u32[]{:S(2)}) collective-permute-start(bf16[8,256]{1,0:T(8,128)(2,1)S(1)} %get-tuple-element.45), channel_id=1, source_target_pairs={{0,2},{1,3},{2,0},{3,1},{4,6},{5,7},{6,4},{7,5},{8,10},{9,11},{10,... | collective-permute-start | bytes 12296 | tf_op jit(solution)/shard_map/sending/ppermute | solution.py:352
  11.0 0.0 collective-permute-start.2
  11.7 4.5 %all-to-all-done.ids_ref = s32[32,1,128]{2,1,0:T(1,128)S(1)} async-done(((s32[32,1,128]{2,1,0:T(1,128)}), s32[32,1,128]{2,1,0:T(1,128)S(1)}, u32[]{:S(2)}, u32[]{:S(2)}) %all-to-all-start) | async-done | bytes 16416 | tf_op jit(solution)/shard_map/sending/all_to_all | solution.py:366
  16.2 0.0 copy-done.2
  16.2 2.2 %pool_other.1 = (bf16[32,16,128]{2,1,0:T(8,128)(2,1)S(1)}, s32[8,1,128]{2,1,0:T(1,128)S(4)}, s32[8,1,128]{2,1,0:T(1,128)S(4)}, s32[8,1,128]{2,1,0:T(1,128)S(4)}, s32[8,1,128]{2,1,0:T(1,128)S(4)}) custom-call(s32[1]{0:T(128)} %bitcast.1.quarter_ref, s32[32,1,128]{2,1,0:T(1,128)S(1)} %all-to-all-done.ids_ref, bf16[8192,128]{1,0:T(8,128)(2,1)S(1)} %bitcast.9), custom_call_target="tpu_custom_call" | custom-call | flops 30000001024 | bytes 40000000 | tf_op jit(solution)/shard_map/pooling/pool_other/pallas_call | solution.py:115
  18.4 0.0 collective-permute-done.refs_1_
  18.4 0.0 collective-permute-done.1.refs_2_
  18.4 0.0 collective-permute-done.2.refs_3_
  18.4 0.1 collective-permute-start.3
  18.5 0.0 copy-start.3
  18.5 0.0 copy-start.4
  18.5 0.0 copy-start.5
  18.5 0.0 copy-start.6
  18.6 1.6 %pool_own.1 = (f32[32,16,128]{2,1,0:T(8,128)S(1)}, bf16[1024,256]{1,0:T(8,128)(2,1)S(1)}) custom-call(s32[1]{0:T(128)} %bitcast.1.quarter_ref, s32[8,1,128]{2,1,0:T(1,128)S(4)} %get-tuple-element.37.refs_0_, s32[8,1,128]{2,1,0:T(1,128)S(4)} %get-tuple-element.38.refs_1_, s32[8,1,128]{2,1,0:T(1,128)S(4)} %get-tuple-element.39.refs_2_, ...), custom_call_target="tpu_custom_call" | custom-call | flops 30000001024 | bytes 40000000 | tf_op jit(solution)/shard_map/pooling/pool_own/pallas_call | solution.py:152
  20.2 0.0 collective-permute-done.3.theirs_ref
  20.2 0.7 %join.1 = bf16[32,16,128]{2,1,0:T(8,128)(2,1)} custom-call(f32[32,16,128]{2,1,0:T(8,128)S(1)} %get-tuple-element.41.mine_ref, bf16[32,16,128]{2,1,0:T(8,128)(2,1)S(1)} %collective-permute-done.3.theirs_ref), custom_call_target="tpu_custom_call" | custom-call | tf_op jit(solution)/shard_map/pooling/join/pallas_call | solution.py:172
  20.8 2.6 %all-to-all-start.1 = ((bf16[32,16,128]{2,1,0:T(8,128)(2,1)}), bf16[32,16,128]{2,1,0:T(8,128)(2,1)S(1)}, u32[]{:S(2)}, u32[]{:S(2)}) async-start(bf16[32,16,128]{2,1,0:T(8,128)(2,1)} %join.1), calls=%async_computation.1 | async-start | bytes 262144 | tf_op jit(solution)/shard_map/pooling/all_to_all | solution.py:376
  23.4 0.0 copy-done.3
  23.4 0.0 copy-done.4
  23.4 0.0 copy-done.5
  23.4 0.0 copy-done.6
  23.5 0.0 copy-start
  23.5 0.0 copy-start.1
  23.5 3.3 %attend.1 = (bf16[8,256]{1,0:T(8,128)(2,1)S(1)}, bf16[8,256]{1,0:T(8,128)(2,1)S(1)}, bf16[8,256]{1,0:T(8,128)(2,1)S(1)}, bf16[8,256]{1,0:T(8,128)(2,1)S(1)}, bf16[1024,1024]{1,0:T(8,128)(2,1)S(1)}) custom-call(s32[1,1]{1,0:T(1,128)} %bitcast.8.len_ref, bf16[8,256]{1,0:T(8,128)(2,1)S(1)} %get-tuple-element.53.refs_0_, ...), custom_call_target="tpu_custom_call" | custom-call | flops 32000000000 | bytes 40000000 | tf_op jit(solution)/shard_map/attention/attend/pallas_call | solution.py:276
  26.8 0.3 collective-permute-start.4
  27.1 1.5 %collective-permute-start.5 = (bf16[8,256]{1,0:T(8,128)(2,1)S(1)}, bf16[8,256]{1,0:T(8,128)(2,1)S(1)}, u32[]{:S(2)}, u32[]{:S(2)}) collective-permute-start(bf16[8,256]{1,0:T(8,128)(2,1)S(1)} %get-tuple-element.60), channel_id=1, source_target_pairs={{0,2},{1,3},{2,0},{3,1},{4,6},{5,7},{6,4},{7,5},{8,10},{9,11},{10,... | collective-permute-start | bytes 12296 | tf_op jit(solution)/shard_map/attention/ppermute | solution.py:352
  28.6 0.1 collective-permute-start.6
  28.7 0.0 copy-done
  28.7 0.0 copy-done.1
  28.7 0.0 copy-start.7
  28.7 2.0 %early.1 = (f32[32,1024]{1,0:T(8,128)S(1)}, bf16[1024,512]{1,0:T(8,128)(2,1)S(1)}) custom-call(bf16[8,256]{1,0:T(8,128)(2,1)S(1)} %get-tuple-element.58.after_ref.refs_0_, bf16[4,8,256]{2,1,0:T(8,128)(2,1)S(1)} %copy-done, s32[4,8,64]{2,1,0:T(8,128)S(1)} %copy-done.1, bf16[2048,256]{1,0:T(8,128)(2,1)} %bitcast.12, bf16[1792,1024]{1,0:T(8,128)(2,1)} %refs_6_.3, ...), custom_call_target="tpu_custom_call" | custom-call | flops 1000000000 | bytes 1000000 | tf_op jit(solution)/shard_map/attention/early/pallas_call | solution.py:213
  30.8 0.0 copy-done.7
  30.8 0.0 collective-permute-done.4.refs_1_
  30.8 0.0 collective-permute-done.5.refs_2_
  30.8 0.8 %collective-permute-done.6.refs_3_ = bf16[8,256]{1,0:T(8,128)(2,1)S(1)} collective-permute-done((bf16[8,256]{1,0:T(8,128)(2,1)S(1)}, bf16[8,256]{1,0:T(8,128)(2,1)S(1)}, u32[]{:S(2)}, u32[]{:S(2)}) %collective-permute-start.6) | collective-permute-done | bytes 4128 | tf_op jit(solution)/shard_map/attention/ppermute | solution.py:352
  31.7 0.0 all-to-all-done.1.ret_ref
  31.7 2.5 %score.1 = f32[4,8]{1,0:T(4,128)} custom-call(s32[1]{0:T(128)} %bitcast.me_ref, bf16[32,16,128]{2,1,0:T(8,128)(2,1)S(1)} %all-to-all-done.1.ret_ref, bf16[8,256]{1,0:T(8,128)(2,1)S(1)} %get-tuple-element.58.after_ref.refs_0_, bf16[8,256]{1,0:T(8,128)(2,1)S(1)} %collective-permute-done.4.refs_1_, bf16[8,256]{1,0:T(8,128)(2,1)S(1)} %collective-permute-done.5.refs_2_, ...), custom_call_target="tpu_custom_call" | custom-call | tf_op jit(solution)/shard_map/scoring/score/pallas_call | solution.py:332
  (1 shorter events, 0.0 us)
Async XLA Ops:
  0.0 16.2 %copy-start.2 = (bf16[1,8192,128]{2,1,0:T(8,128)(2,1)S(1)}, bf16[1,8192,128]{2,1,0:T(8,128)(2,1)}, u32[]{:S(2)}) copy-start(bf16[1,8192,128]{2,1,0:T(8,128)(2,1)} %param.20) | copy-start | bytes 6291460
  1.7 14.5 %all-to-all-start = ((s32[32,1,128]{2,1,0:T(1,128)}), s32[32,1,128]{2,1,0:T(1,128)S(1)}, u32[]{:S(2)}, u32[]{:S(2)}) async-start(s32[32,1,128]{2,1,0:T(1,128)} %get-tuple-element.36), calls=%async_computation | async-start | bytes 32768 | tf_op jit(solution)/shard_map/sending/all_to_all | solution.py:366
  9.0 9.4 %collective-permute-start = (bf16[8,256]{1,0:T(8,128)(2,1)S(1)}, bf16[8,256]{1,0:T(8,128)(2,1)S(1)}, u32[]{:S(2)}, u32[]{:S(2)}) collective-permute-start(bf16[8,256]{1,0:T(8,128)(2,1)S(1)} %get-tuple-element.44), channel_id=1, source_target_pairs={{0,1},{1,0},{2,3},{3,2},{4,5},{5,4},{6,7},{7,6},{8,9},{9,8},{10,11... | collective-permute-start | bytes 12296 | tf_op jit(solution)/shard_map/sending/ppermute | solution.py:352
  9.3 9.1 %collective-permute-start.1 = (bf16[8,256]{1,0:T(8,128)(2,1)S(1)}, bf16[8,256]{1,0:T(8,128)(2,1)S(1)}, u32[]{:S(2)}, u32[]{:S(2)}) collective-permute-start(bf16[8,256]{1,0:T(8,128)(2,1)S(1)} %get-tuple-element.45), channel_id=1, source_target_pairs={{0,2},{1,3},{2,0},{3,1},{4,6},{5,7},{6,4},{7,5},{8,10},{9,11},{10,... | collective-permute-start | bytes 12296 | tf_op jit(solution)/shard_map/sending/ppermute | solution.py:352
  11.0 7.4 %collective-permute-start.2 = (bf16[8,256]{1,0:T(8,128)(2,1)S(1)}, bf16[8,256]{1,0:T(8,128)(2,1)S(1)}, u32[]{:S(2)}, u32[]{:S(2)}) collective-permute-start(bf16[8,256]{1,0:T(8,128)(2,1)S(1)} %get-tuple-element.46), channel_id=1, source_target_pairs={{0,3},{1,2},{2,1},{3,0},{4,7},{5,6},{6,5},{7,4},{8,11},{9,10},{10,... | collective-permute-start | bytes 12296 | tf_op jit(solution)/shard_map/sending/ppermute | solution.py:352
  18.4 1.7 %collective-permute-start.3 = (bf16[32,16,128]{2,1,0:T(8,128)(2,1)S(1)}, bf16[32,16,128]{2,1,0:T(8,128)(2,1)S(1)}, u32[]{:S(2)}, u32[]{:S(2)}) collective-permute-start(bf16[32,16,128]{2,1,0:T(8,128)(2,1)S(1)} %get-tuple-element.47), channel_id=1, source_target_pairs={{0,1},{1,0},{2,3},{3,2},{4,5},{5,4},{6,7},{7,6},{8,9},{9,8},{10,11... | collective-permute-start | bytes 393224 | tf_op jit(solution)/shard_map/pooling/ppermute | solution.py:372
  18.5 4.9 %copy-start.3 = (bf16[256,128]{1,0:T(8,128)(2,1)S(1)}, bf16[256,128]{1,0:T(8,128)(2,1)}, u32[]{:S(2)}) copy-start(bf16[256,128]{1,0:T(8,128)(2,1)} %refs_5_.1) | copy-start | bytes 196612
  18.5 4.9 %copy-start.4 = (bf16[256,128]{1,0:T(8,128)(2,1)S(1)}, bf16[256,128]{1,0:T(8,128)(2,1)}, u32[]{:S(2)}) copy-start(bf16[256,128]{1,0:T(8,128)(2,1)} %refs_6_.2) | copy-start | bytes 196612
  18.5 4.9 %copy-start.5 = (bf16[256,128]{1,0:T(8,128)(2,1)S(1)}, bf16[256,128]{1,0:T(8,128)(2,1)}, u32[]{:S(2)}) copy-start(bf16[256,128]{1,0:T(8,128)(2,1)} %refs_7_.1) | copy-start | bytes 196612
  18.5 4.9 %copy-start.6 = (bf16[128]{0:T(256)(128)(2,1)S(1)}, bf16[128]{0:T(256)(128)(2,1)}, u32[]{:S(2)}) copy-start(bf16[128]{0:T(256)(128)(2,1)} %param.25) | copy-start | bytes 772
  20.8 10.8 %all-to-all-start.1 = ((bf16[32,16,128]{2,1,0:T(8,128)(2,1)}), bf16[32,16,128]{2,1,0:T(8,128)(2,1)S(1)}, u32[]{:S(2)}, u32[]{:S(2)}) async-start(bf16[32,16,128]{2,1,0:T(8,128)(2,1)} %join.1), calls=%async_computation.1 | async-start | bytes 262144 | tf_op jit(solution)/shard_map/pooling/all_to_all | solution.py:376
  23.5 5.3 %copy-start = (bf16[4,8,256]{2,1,0:T(8,128)(2,1)S(1)}, bf16[4,8,256]{2,1,0:T(8,128)(2,1)}, u32[]{:S(2)}) copy-start(bf16[4,8,256]{2,1,0:T(8,128)(2,1)} %target_ref.1) | copy-start | bytes 49156
  23.5 5.3 %copy-start.1 = (s32[4,8,64]{2,1,0:T(8,128)S(1)}, s32[4,8,64]{2,1,0:T(8,128)}, u32[]{:S(2)}) copy-start(s32[4,8,64]{2,1,0:T(8,128)} %leaf_ids_ref.1) | copy-start | bytes 24580
  26.8 4.0 %collective-permute-start.4 = (bf16[8,256]{1,0:T(8,128)(2,1)S(1)}, bf16[8,256]{1,0:T(8,128)(2,1)S(1)}, u32[]{:S(2)}, u32[]{:S(2)}) collective-permute-start(bf16[8,256]{1,0:T(8,128)(2,1)S(1)} %get-tuple-element.59), channel_id=1, source_target_pairs={{0,1},{1,0},{2,3},{3,2},{4,5},{5,4},{6,7},{7,6},{8,9},{9,8},{10,11... | collective-permute-start | bytes 12296 | tf_op jit(solution)/shard_map/attention/ppermute | solution.py:352
  27.1 3.7 %collective-permute-start.5 = (bf16[8,256]{1,0:T(8,128)(2,1)S(1)}, bf16[8,256]{1,0:T(8,128)(2,1)S(1)}, u32[]{:S(2)}, u32[]{:S(2)}) collective-permute-start(bf16[8,256]{1,0:T(8,128)(2,1)S(1)} %get-tuple-element.60), channel_id=1, source_target_pairs={{0,2},{1,3},{2,0},{3,1},{4,6},{5,7},{6,4},{7,5},{8,10},{9,11},{10,... | collective-permute-start | bytes 12296 | tf_op jit(solution)/shard_map/attention/ppermute | solution.py:352
  28.6 3.0 %collective-permute-start.6 = (bf16[8,256]{1,0:T(8,128)(2,1)S(1)}, bf16[8,256]{1,0:T(8,128)(2,1)S(1)}, u32[]{:S(2)}, u32[]{:S(2)}) collective-permute-start(bf16[8,256]{1,0:T(8,128)(2,1)S(1)} %get-tuple-element.61), channel_id=1, source_target_pairs={{0,3},{1,2},{2,1},{3,0},{4,7},{5,6},{6,5},{7,4},{8,11},{9,10},{10,... | collective-permute-start | bytes 12296 | tf_op jit(solution)/shard_map/attention/ppermute | solution.py:352
  28.7 2.1 %copy-start.7 = (bf16[256]{0:T(256)(128)(2,1)S(1)}, bf16[256]{0:T(256)(128)(2,1)}, u32[]{:S(2)}) copy-start(bf16[256]{0:T(256)(128)(2,1)} %param.29) | copy-start | bytes 1540

commit v5 on v4

--- a/solution.py
+++ b/solution.py
@@ -22,7 +22,7 @@
     return lax.dot_general(left, right, (dims, ((), ())), preferred_element_type=jnp.float32)
 
 
-def prepare_kernel(me_ref, bag_hbm, target_hbm, ids_ref, *refs):
+def prepare_kernel(piece_rows, me_ref, bag_hbm, target_hbm, ids_ref, *refs):
     requests, per, bag_size, tables = bag_hbm.shape
     block_refs = refs[:requests]
     bag_ref, target_ref, sems = refs[requests:]
@@ -33,19 +33,27 @@
         copy.wait()
     lines = jnp.concatenate([bag_ref[r, c] for r in range(requests) for c in range(per)], axis=0)
     by_table = lines.T
-    for t in range(tables):
-        for piece in range(SPLIT):
-            ids_ref[t * SPLIT + piece] = by_table[t : t + 1, :]
+    half = by_table.shape[1] // 2
+    for piece in range(SPLIT):
+        core = piece % 2
+        ids = by_table[:, core * half : (core + 1) * half]
+        near = ids - piece * piece_rows
+        far = ids - (piece - core + 1 - core) * piece_rows
+        row = jnp.where((far >= 0) & (far < piece_rows), far + piece_rows, 2 * piece_rows)
+        row = jnp.where((near >= 0) & (near < piece_rows), near, row)
+        for t in range(tables):
+            ids_ref[t * SPLIT + piece] = row[t : t + 1, :]
     for k, block_ref in enumerate(block_refs):
         block_ref[...] = target_ref[me_ref[0] ^ k]
 
 
-def prepare(me, bag_ids, target):
+def prepare(me, bag_ids, target, piece_rows):
     requests, per, tables, bag_size = bag_ids.shape
-    block = jax.ShapeDtypeStruct(target.shape[1:], target.dtype)
+    return_shape = (tables * SPLIT, 1, requests * per * bag_size // 2)
     out = pl.pallas_call(
-        prepare_kernel,
-        out_shape=[jax.ShapeDtypeStruct((tables * SPLIT, 1, requests * per * bag_size), jnp.int32)] + [block] * requests,
+        functools.partial(prepare_kernel, piece_rows),
+        out_shape=[jax.ShapeDtypeStruct(return_shape, jnp.int32)]
+        + [jax.ShapeDtypeStruct(target.shape[1:], target.dtype)] * requests,
         in_specs=[SMEM, HBM, HBM],
         out_specs=[VMEM] * (1 + requests),
         scratch_shapes=[
@@ -53,8 +61,8 @@
             pltpu.VMEM(target.shape, target.dtype),
             pltpu.SemaphoreType.DMA((2,)),
         ],
-        compiler_params=pltpu.CompilerParams(vmem_limit_bytes=16 << 20),
-        cost_estimate=pl.CostEstimate(flops=30000000000, bytes_accessed=4 * 10**7, transcendentals=0),
+        compiler_params=pltpu.CompilerParams(vmem_limit_bytes=8 << 20),
+        cost_estimate=pl.CostEstimate(flops=3 * 10**10, bytes_accessed=4 * 10**7, transcendentals=0),
         name="prepare",
     )(me, *in_hbm(jnp.transpose(bag_ids, (0, 1, 3, 2)), target))
     return out[0], out[1:]
@@ -79,104 +87,61 @@
     lax.fori_loop(0, step, one_step, 0)
 
 
-def spread_rows(table_ref, rows_f):
+CHUNKS = 8
+
+
+def pool_kernel(bag_size, ids_ref, table_ref, far_hbm, history_hbm, out_ref, history_ref, *refs):
+    scalars = refs[:GROUPS]
+    rows_f, far_ref, sums, id_sems, far_sems, sem = refs[GROUPS:]
+    step = ids_ref.shape[0] // GROUPS
     piece_rows, width = table_ref.shape
+    chunk = piece_rows // CHUNKS
+    copies = [
+        pltpu.make_async_copy(ids_ref.at[pl.ds(k * step, step)], scalar, id_sems.at[k]) for k, scalar in enumerate(scalars)
+    ]
+    arrivals = [
+        pltpu.make_async_copy(far_hbm.at[pl.ds(k * chunk, chunk)], far_ref.at[pl.ds(k * chunk, chunk)], far_sems.at[k])
+        for k in range(CHUNKS)
+    ]
+    fetch = pltpu.make_async_copy(history_hbm, history_ref, sem)
+    for copy in (*copies, *arrivals):
+        copy.start()
     rows_f[:piece_rows, :] = table_ref[...].astype(jnp.float32)
-    rows_f[piece_rows:, :] = jnp.zeros((8, width), jnp.float32)
-
-
-def pool_other_kernel(bag_size, quarter_ref, ids_ref, table_ref, out_ref, *refs):
-    scalars = refs[:GROUPS]
-    offsets, rows_f, sums, sems = refs[GROUPS:]
-    step, half, piece_rows = ids_ref.shape[0] // GROUPS, out_ref.shape[1], table_ref.shape[0]
-    local = ids_ref[...] - quarter_ref[0] * piece_rows
-    offsets[...] = jnp.where((local >= 0) & (local < piece_rows), local, piece_rows)
-    copies = [
-        pltpu.make_async_copy(offsets.at[pl.ds(k * step, step)], scalar, sems.at[k]) for k, scalar in enumerate(scalars)
-    ]
-    for copy in copies:
-        copy.start()
-    spread_rows(table_ref, rows_f)
+    rows_f[2 * piece_rows :, :] = jnp.zeros((8, width), jnp.float32)
+    for k, arrival in enumerate(arrivals):
+        arrival.wait()
+        at = piece_rows + k * chunk
+        rows_f[at : at + chunk, :] = far_ref[k * chunk : (k + 1) * chunk, :].astype(jnp.float32)
+    fetch.start()
     for copy in copies:
         copy.wait()
-    for core in range(2):
-
-        @pl.when(quarter_ref[0] % 2 == core)
-        def _():
-            add_bags(bag_size, (1 - core) * half, scalars, rows_f, sums)
-
+    add_bags(bag_size, 0, scalars, rows_f, sums)
     out_ref[...] = sums[...].astype(out_ref.dtype)
-
-
-def pool_other(quarter, ids, table, bag_size):
+    fetch.wait()
+
+
+def pool(ids, table, far_table, history, bag_size):
     sources, _, lanes = ids.shape
     piece_rows, width = table.shape
-    half = (sources, lanes // bag_size // 2, width)
-    out = pl.pallas_call(
-        functools.partial(pool_other_kernel, bag_size),
-        out_shape=[jax.ShapeDtypeStruct(half, jnp.bfloat16)]
-        + [pltpu.SMEM((sources // GROUPS, 1, lanes), jnp.int32)] * GROUPS,
-        in_specs=[SMEM, VMEM, VMEM],
-        out_specs=[VMEM] + [SMEM] * GROUPS,
-        scratch_shapes=[
-            pltpu.VMEM(ids.shape, jnp.int32),
-            pltpu.VMEM((piece_rows + 8, width), jnp.float32),
-            pltpu.VMEM(half, jnp.float32),
+    shape = (sources, lanes // bag_size, width)
+    return pl.pallas_call(
+        functools.partial(pool_kernel, bag_size),
+        out_shape=[jax.ShapeDtypeStruct(shape, jnp.bfloat16), pltpu.VMEM(history.shape, history.dtype)],
+        in_specs=[VMEM, VMEM, HBM, HBM],
+        out_specs=[VMEM, VMEM],
+        scratch_shapes=[pltpu.SMEM((sources // GROUPS, 1, lanes), jnp.int32)] * GROUPS
+        + [
+            pltpu.VMEM((2 * piece_rows + 8, width), jnp.float32),
+            pltpu.VMEM(table.shape, table.dtype),
+            pltpu.VMEM(shape, jnp.float32),
             pltpu.SemaphoreType.DMA((GROUPS,)),
-        ],
-        compiler_params=pltpu.CompilerParams(vmem_limit_bytes=16 << 20),
+            pltpu.SemaphoreType.DMA((CHUNKS,)),
+            pltpu.SemaphoreType.DMA,
+        ],
+        compiler_params=pltpu.CompilerParams(vmem_limit_bytes=24 << 20),
         cost_estimate=pl.CostEstimate(flops=3 * 10**10, bytes_accessed=4 * 10**7, transcendentals=0),
-        name="pool_other",
-    )(quarter, ids, table)
-    return out[0], out[1:]
-
-
-def pool_own_kernel(bag_size, quarter_ref, *refs):
-    scalars = refs[:GROUPS]
-    table_ref, history_hbm, out_ref, history_ref, rows_f, sem = refs[GROUPS:]
-    fetch = pltpu.make_async_copy(history_hbm, history_ref, sem)
-    fetch.start()
-    spread_rows(table_ref, rows_f)
-    for core in range(2):
-
-        @pl.when(quarter_ref[0] % 2 == core)
-        def _():
-            add_bags(bag_size, core * out_ref.shape[1], scalars, rows_f, out_ref)
-
-    fetch.wait()
-
-
-def pool_own(quarter, scalars, table, history, bag_size):
-    step, _, lanes = scalars[0].shape
-    piece_rows, width = table.shape
-    return pl.pallas_call(
-        functools.partial(pool_own_kernel, bag_size),
-        out_shape=[
-            jax.ShapeDtypeStruct((step * GROUPS, lanes // bag_size // 2, width), jnp.float32),
-            pltpu.VMEM(history.shape, history.dtype),
-        ],
-        in_specs=[SMEM] * (1 + GROUPS) + [VMEM, HBM],
-        out_specs=[VMEM, VMEM],
-        scratch_shapes=[pltpu.VMEM((piece_rows + 8, width), jnp.float32), pltpu.SemaphoreType.DMA],
-        compiler_params=pltpu.CompilerParams(vmem_limit_bytes=16 << 20),
-        cost_estimate=pl.CostEstimate(flops=3 * 10**10, bytes_accessed=4 * 10**7, transcendentals=0),
-        name="pool_own",
-    )(quarter, *scalars, table, *in_hbm(history))
-
-
-def join_kernel(mine_ref, theirs_ref, out_ref):
-    out_ref[...] = (mine_ref[...] + theirs_ref[...].astype(jnp.float32)).astype(jnp.bfloat16)
-
-
-def join(mine, theirs):
-    return pl.pallas_call(
-        join_kernel,
-        out_shape=jax.ShapeDtypeStruct(mine.shape, jnp.bfloat16),
-        in_specs=[VMEM, VMEM],
-        out_specs=VMEM,
-        compiler_params=pltpu.CompilerParams(vmem_limit_bytes=4 << 20),
-        name="join",
-    )(mine, theirs)
+        name="pool",
+    )(ids, table, *in_hbm(far_table, history))
 
 
 def early_kernel(
@@ -358,20 +323,15 @@
     w_query, w_key, w_pair, a_out, w_first, w_second, w_third, w_out,
 ):
     me = lax.axis_index("cand").astype(jnp.int32).reshape(1)
-    quarter = (lax.axis_index(ALL) % SPLIT).astype(jnp.int32).reshape(1)
 
     with jax.named_scope("sending"):
-        outgoing, blocks = prepare(me, bag_ids, target)
+        size = lax.axis_size("cand")
+        far_table = lax.ppermute(table_piece[0], "cand", [(i, i ^ 1) for i in range(size)])
+        outgoing, blocks = prepare(me, bag_ids, target, table_piece.shape[1])
         queries = swap(blocks)
         incoming = lax.all_to_all(outgoing, ALL, split_axis=0, concat_axis=0, tiled=True)
     with jax.named_scope("pooling"):
-        bag_size = bag_ids.shape[3]
-        for_other, scalars = pool_other(quarter, incoming, table_piece[0], bag_size)
-        for_other, queries = lax.optimization_barrier((for_other, queries))
-        size = lax.axis_size("cand")
-        other = lax.ppermute(for_other, "cand", [(i, i ^ 1) for i in range(size)])
-        mine, events = pool_own(quarter, scalars, table_piece[0], history[0], bag_size)
-        pair_sums = join(mine, other)
+        pair_sums, events = pool(incoming, table_piece[0], far_table, history[0], bag_ids.shape[3])
         pair_sums, queries = lax.optimization_barrier((pair_sums, queries))
         returned = lax.all_to_all(pair_sums, ALL, split_axis=0, concat_axis=0, tiled=True)
     with jax.named_scope("attention"):

time: 34.4 us -> 33.8 us (0.983)
  Pallas kernels: 14 us -> 13.3 us
    pallas_call x4 -> x2, Pallas kernels: 6.19 us -> 5.47 us  [the longest x1 3.72 us: pool(): pl.pallas_call(functools.partial(pool_kernel, bag_size), out_shape=[jax.S...]
    ppermute x1, starting transfers between devices: 0.07 us -> 0.45 us  [on_device(): lax.ppermute(table_piece[0], 'cand', [(i, i ^ 1) for i in range(size)])]
  transfers between devices with their start and end apart: 9 -> 9, of which waited for: 2 -> 2; matrix products, arithmetic and copies ran while one was open for 0% -> 0% of each run, Pallas kernels for 27% -> 32%
where the time goes in v5:
time: 33.8 us; the launch traced here: 33.5 us
  starting transfers between devices  14 us (41%)
  Pallas kernels  13.3 us (39%)
  waiting for transfers between devices  5.34 us (16%)
  between operations  0.84 us (2%)
    all_to_all x1, starting transfers between devices, on_device(): lax.all_to_all(outgoing, ALL, split_axis=0, concat_axis=0, tiled=True)  6.97 us
    all_to_all x1, waiting for transfers between devices, on_device(): lax.all_to_all(outgoing, ALL, split_axis=0, concat_axis=0, tiled=True)  4.49 us
    ppermute x6, starting transfers between devices, swap(): lax.ppermute(blocks[k], 'cand', [(i, i ^ k) for i in range(size)])  3.96 us
    pallas_call x1, Pallas kernels, pool(): pl.pallas_call(functools.partial(pool_kernel, bag_size), out_shape=[jax.S...  3.72 us
    pallas_call x1, Pallas kernels, attend(): pl.pallas_call(functools.partial(attend_kernel, parts, 8, min(256, events...  3.34 us
    all_to_all x1, starting transfers between devices, on_device(): lax.all_to_all(pair_sums, ALL, split_axis=0, concat_axis=0, tiled=True)  2.58 us
    pallas_call x1, Pallas kernels, score(): pl.pallas_call(functools.partial(score_kernel, parts), out_shape=jax.Shap...  2.45 us
    pallas_call x1, Pallas kernels, early_part(): pl.pallas_call(early_kernel, out_shape=[jax.ShapeDtypeStruct((requests *...  2.05 us
  transfers between devices with their start and end apart: 9, of which 2 were waited for; matrix products, arithmetic and copies ran while one was open for 0% of the time, Pallas kernels for 32%

profile of v5, /device:TPU:0, one launch (start us, length us, event | category | flops | bytes accessed | tf_op | source)
XLA Modules:
  0.0 33.5 jit_solution(18381148767035582017)
XLA Ops:
  0.0 0.5 %collective-permute-start = (bf16[8192,128]{1,0:T(8,128)(2,1)}, bf16[8192,128]{1,0:T(8,128)(2,1)}, u32[]{:S(2)}, u32[]{:S(2)}) collective-permute-start(bf16[8192,128]{1,0:T(8,128)(2,1)} %bitcast.8), channel_id=1, source_target_pairs={{0,1},{1,0},{2,3},{3,2},{4,5},{5,4},{6,7},{7,6},{8,9},{9,8},{10,11... | collective-permute-start | bytes 6291464 | tf_op jit(solution)/shard_map/sending/ppermute | solution.py:329
  0.5 0.0 copy-start.2
  0.5 1.8 %prepare.1 = (s32[32,1,64]{2,1,0:T(1,128)}, bf16[8,256]{1,0:T(8,128)(2,1)S(1)}, bf16[8,256]{1,0:T(8,128)(2,1)S(1)}, bf16[8,256]{1,0:T(8,128)(2,1)S(1)}, bf16[8,256]{1,0:T(8,128)(2,1)S(1)}) custom-call(s32[1]{0:T(128)} %bitcast.me_ref, s32[4,8,4,8]{3,2,1,0:T(4,128)} %bitcast.13, bf16[4,8,256]{2,1,0:T(8,128)(2,1)} %target_ref.1), custom_call_target="tpu_custom_call" | custom-call | flops 30000001024 | bytes 40000000 | tf_op jit(solution)/shard_map/sending/prepare/pallas_call | solution.py:53
  2.2 7.0 %all-to-all-start = ((s32[32,1,64]{2,1,0:T(1,128)}), s32[32,1,64]{2,1,0:T(1,128)S(1)}, u32[]{:S(2)}, u32[]{:S(2)}) async-start(s32[32,1,64]{2,1,0:T(1,128)} %get-tuple-element.26), calls=%async_computation | async-start | bytes 32768 | tf_op jit(solution)/shard_map/sending/all_to_all | solution.py:332
  9.2 0.3 collective-permute-start.1
  9.5 1.7 %collective-permute-start.2 = (bf16[8,256]{1,0:T(8,128)(2,1)S(1)}, bf16[8,256]{1,0:T(8,128)(2,1)S(1)}, u32[]{:S(2)}, u32[]{:S(2)}) collective-permute-start(bf16[8,256]{1,0:T(8,128)(2,1)S(1)} %get-tuple-element.30), channel_id=1, source_target_pairs={{0,2},{1,3},{2,0},{3,1},{4,6},{5,7},{6,4},{7,5},{8,10},{9,11},{10,... | collective-permute-start | bytes 12296 | tf_op jit(solution)/shard_map/sending/ppermute | solution.py:317
  11.2 0.0 collective-permute-start.3
  11.8 4.5 %all-to-all-done.ids_ref = s32[32,1,64]{2,1,0:T(1,128)S(1)} async-done(((s32[32,1,64]{2,1,0:T(1,128)}), s32[32,1,64]{2,1,0:T(1,128)S(1)}, u32[]{:S(2)}, u32[]{:S(2)}) %all-to-all-start) | async-done | bytes 8224 | tf_op jit(solution)/shard_map/sending/all_to_all | solution.py:332
  16.3 0.0 collective-permute-done.far_hbm
  16.3 0.0 copy-done.2
  16.3 0.0 copy-start.3
  16.3 0.0 copy-start.4
  16.4 0.0 copy-start.5
  16.4 0.0 copy-start.6
  16.4 3.7 %pool.1 = (bf16[32,16,128]{2,1,0:T(8,128)(2,1)}, bf16[1024,256]{1,0:T(8,128)(2,1)S(1)}) custom-call(s32[32,1,64]{2,1,0:T(1,128)S(1)} %all-to-all-done.ids_ref, bf16[8192,128]{1,0:T(8,128)(2,1)S(1)} %bitcast.9, bf16[8192,128]{1,0:T(8,128)(2,1)} %collective-permute-done.far_hbm, bf16[1024,256]{1,0:T(8,128)(2,1)} %bitcast.12), custom_call_target="tpu_custom_call" | custom-call | flops 30000001024 | bytes 40000000 | tf_op jit(solution)/shard_map/pooling/pool/pallas_call | solution.py:127
  20.1 0.0 collective-permute-done.1.refs_1_
  20.1 0.0 collective-permute-done.2.refs_2_
  20.1 0.0 collective-permute-done.3.refs_3_
  20.1 2.6 %all-to-all-start.1 = ((bf16[32,16,128]{2,1,0:T(8,128)(2,1)}), bf16[32,16,128]{2,1,0:T(8,128)(2,1)S(1)}, u32[]{:S(2)}, u32[]{:S(2)}) async-start(bf16[32,16,128]{2,1,0:T(8,128)(2,1)} %get-tuple-element.32), calls=%async_computation.1 | async-start | bytes 262144 | tf_op jit(solution)/shard_map/pooling/all_to_all | solution.py:336
  22.7 0.0 copy-done.3
  22.7 0.0 copy-done.4
  22.8 0.0 copy-done.5
  22.8 0.0 copy-done.6
  22.8 0.0 copy-start
  22.8 0.0 copy-start.1
  22.8 3.3 %attend.1 = (bf16[8,256]{1,0:T(8,128)(2,1)S(1)}, bf16[8,256]{1,0:T(8,128)(2,1)S(1)}, bf16[8,256]{1,0:T(8,128)(2,1)S(1)}, bf16[8,256]{1,0:T(8,128)(2,1)S(1)}, bf16[1024,1024]{1,0:T(8,128)(2,1)S(1)}) custom-call(s32[1,1]{1,0:T(1,128)} %bitcast.7.len_ref, bf16[8,256]{1,0:T(8,128)(2,1)S(1)} %get-tuple-element.33.refs_0_, ...), custom_call_target="tpu_custom_call" | custom-call | flops 32000000000 | bytes 40000000 | tf_op jit(solution)/shard_map/attention/attend/pallas_call | solution.py:241
  26.1 0.2 collective-permute-start.4
  26.3 1.7 %collective-permute-start.5 = (bf16[8,256]{1,0:T(8,128)(2,1)S(1)}, bf16[8,256]{1,0:T(8,128)(2,1)S(1)}, u32[]{:S(2)}, u32[]{:S(2)}) collective-permute-start(bf16[8,256]{1,0:T(8,128)(2,1)S(1)} %get-tuple-element.40), channel_id=1, source_target_pairs={{0,2},{1,3},{2,0},{3,1},{4,6},{5,7},{6,4},{7,5},{8,10},{9,11},{10,... | collective-permute-start | bytes 12296 | tf_op jit(solution)/shard_map/attention/ppermute | solution.py:317
  28.0 0.1 collective-permute-start.6
  28.1 0.0 copy-done
  28.1 0.0 copy-done.1
  28.1 0.0 copy-start.7
  28.1 2.0 %early.1 = (f32[32,1024]{1,0:T(8,128)S(1)}, bf16[1024,512]{1,0:T(8,128)(2,1)S(1)}) custom-call(bf16[8,256]{1,0:T(8,128)(2,1)S(1)} %get-tuple-element.38.after_ref.refs_0_, bf16[4,8,256]{2,1,0:T(8,128)(2,1)S(1)} %copy-done, s32[4,8,64]{2,1,0:T(8,128)S(1)} %copy-done.1, bf16[2048,256]{1,0:T(8,128)(2,1)} %bitcast.11, bf16[1792,1024]{1,0:T(8,128)(2,1)} %refs_6_.3, ...), custom_call_target="tpu_custom_call" | custom-call | flops 1000000000 | bytes 1000000 | tf_op jit(solution)/shard_map/attention/early/pallas_call | solution.py:178
  30.2 0.0 copy-done.7
  30.2 0.0 collective-permute-done.4.refs_1_
  30.2 0.0 collective-permute-done.5.refs_2_
  30.2 0.8 %collective-permute-done.6.refs_3_ = bf16[8,256]{1,0:T(8,128)(2,1)S(1)} collective-permute-done((bf16[8,256]{1,0:T(8,128)(2,1)S(1)}, bf16[8,256]{1,0:T(8,128)(2,1)S(1)}, u32[]{:S(2)}, u32[]{:S(2)}) %collective-permute-start.6) | collective-permute-done | bytes 4128 | tf_op jit(solution)/shard_map/attention/ppermute | solution.py:317
  31.0 0.0 all-to-all-done.1.ret_ref
  31.0 2.5 %score.1 = f32[4,8]{1,0:T(4,128)} custom-call(s32[1]{0:T(128)} %bitcast.me_ref, bf16[32,16,128]{2,1,0:T(8,128)(2,1)S(1)} %all-to-all-done.1.ret_ref, bf16[8,256]{1,0:T(8,128)(2,1)S(1)} %get-tuple-element.38.after_ref.refs_0_, bf16[8,256]{1,0:T(8,128)(2,1)S(1)} %collective-permute-done.4.refs_1_, bf16[8,256]{1,0:T(8,128)(2,1)S(1)} %collective-permute-done.5.refs_2_, ...), custom_call_target="tpu_custom_call" | custom-call | tf_op jit(solution)/shard_map/scoring/score/pallas_call | solution.py:297
  (1 shorter events, 0.0 us)
Async XLA Ops:
  0.0 16.3 %collective-permute-start = (bf16[8192,128]{1,0:T(8,128)(2,1)}, bf16[8192,128]{1,0:T(8,128)(2,1)}, u32[]{:S(2)}, u32[]{:S(2)}) collective-permute-start(bf16[8192,128]{1,0:T(8,128)(2,1)} %bitcast.8), channel_id=1, source_target_pairs={{0,1},{1,0},{2,3},{3,2},{4,5},{5,4},{6,7},{7,6},{8,9},{9,8},{10,11... | collective-permute-start | bytes 6291464 | tf_op jit(solution)/shard_map/sending/ppermute | solution.py:329
  0.5 15.9 %copy-start.2 = (bf16[1,8192,128]{2,1,0:T(8,128)(2,1)S(1)}, bf16[1,8192,128]{2,1,0:T(8,128)(2,1)}, u32[]{:S(2)}) copy-start(bf16[1,8192,128]{2,1,0:T(8,128)(2,1)} %param.20) | copy-start | bytes 6291460
  2.2 14.1 %all-to-all-start = ((s32[32,1,64]{2,1,0:T(1,128)}), s32[32,1,64]{2,1,0:T(1,128)S(1)}, u32[]{:S(2)}, u32[]{:S(2)}) async-start(s32[32,1,64]{2,1,0:T(1,128)} %get-tuple-element.26), calls=%async_computation | async-start | bytes 32768 | tf_op jit(solution)/shard_map/sending/all_to_all | solution.py:332
  9.2 10.9 %collective-permute-start.1 = (bf16[8,256]{1,0:T(8,128)(2,1)S(1)}, bf16[8,256]{1,0:T(8,128)(2,1)S(1)}, u32[]{:S(2)}, u32[]{:S(2)}) collective-permute-start(bf16[8,256]{1,0:T(8,128)(2,1)S(1)} %get-tuple-element.29), channel_id=1, source_target_pairs={{0,1},{1,0},{2,3},{3,2},{4,5},{5,4},{6,7},{7,6},{8,9},{9,8},{10,11... | collective-permute-start | bytes 12296 | tf_op jit(solution)/shard_map/sending/ppermute | solution.py:317
  9.5 10.6 %collective-permute-start.2 = (bf16[8,256]{1,0:T(8,128)(2,1)S(1)}, bf16[8,256]{1,0:T(8,128)(2,1)S(1)}, u32[]{:S(2)}, u32[]{:S(2)}) collective-permute-start(bf16[8,256]{1,0:T(8,128)(2,1)S(1)} %get-tuple-element.30), channel_id=1, source_target_pairs={{0,2},{1,3},{2,0},{3,1},{4,6},{5,7},{6,4},{7,5},{8,10},{9,11},{10,... | collective-permute-start | bytes 12296 | tf_op jit(solution)/shard_map/sending/ppermute | solution.py:317
  11.2 8.9 %collective-permute-start.3 = (bf16[8,256]{1,0:T(8,128)(2,1)S(1)}, bf16[8,256]{1,0:T(8,128)(2,1)S(1)}, u32[]{:S(2)}, u32[]{:S(2)}) collective-permute-start(bf16[8,256]{1,0:T(8,128)(2,1)S(1)} %get-tuple-element.31), channel_id=1, source_target_pairs={{0,3},{1,2},{2,1},{3,0},{4,7},{5,6},{6,5},{7,4},{8,11},{9,10},{10,... | collective-permute-start | bytes 12296 | tf_op jit(solution)/shard_map/sending/ppermute | solution.py:317
  16.3 6.4 %copy-start.3 = (bf16[256,128]{1,0:T(8,128)(2,1)S(1)}, bf16[256,128]{1,0:T(8,128)(2,1)}, u32[]{:S(2)}) copy-start(bf16[256,128]{1,0:T(8,128)(2,1)} %refs_5_.1) | copy-start | bytes 196612
  16.3 6.4 %copy-start.4 = (bf16[256,128]{1,0:T(8,128)(2,1)S(1)}, bf16[256,128]{1,0:T(8,128)(2,1)}, u32[]{:S(2)}) copy-start(bf16[256,128]{1,0:T(8,128)(2,1)} %refs_6_.2) | copy-start | bytes 196612
  16.4 6.4 %copy-start.5 = (bf16[256,128]{1,0:T(8,128)(2,1)S(1)}, bf16[256,128]{1,0:T(8,128)(2,1)}, u32[]{:S(2)}) copy-start(bf16[256,128]{1,0:T(8,128)(2,1)} %refs_7_.1) | copy-start | bytes 196612
  16.4 6.4 %copy-start.6 = (bf16[128]{0:T(256)(128)(2,1)S(1)}, bf16[128]{0:T(256)(128)(2,1)}, u32[]{:S(2)}) copy-start(bf16[128]{0:T(256)(128)(2,1)} %param.25) | copy-start | bytes 772
  20.1 10.9 %all-to-all-start.1 = ((bf16[32,16,128]{2,1,0:T(8,128)(2,1)}), bf16[32,16,128]{2,1,0:T(8,128)(2,1)S(1)}, u32[]{:S(2)}, u32[]{:S(2)}) async-start(bf16[32,16,128]{2,1,0:T(8,128)(2,1)} %get-tuple-element.32), calls=%async_computation.1 | async-start | bytes 262144 | tf_op jit(solution)/shard_map/pooling/all_to_all | solution.py:336
  22.8 5.3 %copy-start = (bf16[4,8,256]{2,1,0:T(8,128)(2,1)S(1)}, bf16[4,8,256]{2,1,0:T(8,128)(2,1)}, u32[]{:S(2)}) copy-start(bf16[4,8,256]{2,1,0:T(8,128)(2,1)} %target_ref.1) | copy-start | bytes 49156
  22.8 5.3 %copy-start.1 = (s32[4,8,64]{2,1,0:T(8,128)S(1)}, s32[4,8,64]{2,1,0:T(8,128)}, u32[]{:S(2)}) copy-start(s32[4,8,64]{2,1,0:T(8,128)} %leaf_ids_ref.1) | copy-start | bytes 24580
  26.1 4.0 %collective-permute-start.4 = (bf16[8,256]{1,0:T(8,128)(2,1)S(1)}, bf16[8,256]{1,0:T(8,128)(2,1)S(1)}, u32[]{:S(2)}, u32[]{:S(2)}) collective-permute-start(bf16[8,256]{1,0:T(8,128)(2,1)S(1)} %get-tuple-element.39), channel_id=1, source_target_pairs={{0,1},{1,0},{2,3},{3,2},{4,5},{5,4},{6,7},{7,6},{8,9},{9,8},{10,11... | collective-permute-start | bytes 12296 | tf_op jit(solution)/shard_map/attention/ppermute | solution.py:317
  26.3 3.9 %collective-permute-start.5 = (bf16[8,256]{1,0:T(8,128)(2,1)S(1)}, bf16[8,256]{1,0:T(8,128)(2,1)S(1)}, u32[]{:S(2)}, u32[]{:S(2)}) collective-permute-start(bf16[8,256]{1,0:T(8,128)(2,1)S(1)} %get-tuple-element.40), channel_id=1, source_target_pairs={{0,2},{1,3},{2,0},{3,1},{4,6},{5,7},{6,4},{7,5},{8,10},{9,11},{10,... | collective-permute-start | bytes 12296 | tf_op jit(solution)/shard_map/attention/ppermute | solution.py:317
  28.0 3.0 %collective-permute-start.6 = (bf16[8,256]{1,0:T(8,128)(2,1)S(1)}, bf16[8,256]{1,0:T(8,128)(2,1)S(1)}, u32[]{:S(2)}, u32[]{:S(2)}) collective-permute-start(bf16[8,256]{1,0:T(8,128)(2,1)S(1)} %get-tuple-element.41), channel_id=1, source_target_pairs={{0,3},{1,2},{2,1},{3,0},{4,7},{5,6},{6,5},{7,4},{8,11},{9,10},{10,... | collective-permute-start | bytes 12296 | tf_op jit(solution)/shard_map/attention/ppermute | solution.py:317
  28.1 2.1 %copy-start.7 = (bf16[256]{0:T(256)(128)(2,1)S(1)}, bf16[256]{0:T(256)(128)(2,1)}, u32[]{:S(2)}) copy-start(bf16[256]{0:T(256)(128)(2,1)} %param.29) | copy-start | bytes 1540

commit v6 on v5

--- a/solution.py
+++ b/solution.py
@@ -25,7 +25,7 @@
 def prepare_kernel(piece_rows, me_ref, bag_hbm, target_hbm, ids_ref, *refs):
     requests, per, bag_size, tables = bag_hbm.shape
     block_refs = refs[:requests]
-    bag_ref, target_ref, sems = refs[requests:]
+    bag_ref, target_ref, target_f, sems = refs[requests:]
     copies = [pltpu.make_async_copy(bag_hbm, bag_ref, sems.at[0]), pltpu.make_async_copy(target_hbm, target_ref, sems.at[1])]
     for copy in copies:
         copy.start()
@@ -43,12 +43,15 @@
         row = jnp.where((near >= 0) & (near < piece_rows), near, row)
         for t in range(tables):
             ids_ref[t * SPLIT + piece] = row[t : t + 1, :]
+    target_f[...] = target_ref[...].astype(jnp.float32)
     for k, block_ref in enumerate(block_refs):
-        block_ref[...] = target_ref[me_ref[0] ^ k]
+        place = pl.multiple_of((me_ref[0] ^ k) * per, per)
+        block_ref[...] = target_f[pl.ds(place, per), :].astype(block_ref.dtype)
 
 
 def prepare(me, bag_ids, target, piece_rows):
     requests, per, tables, bag_size = bag_ids.shape
+    width = target.shape[2]
     return_shape = (tables * SPLIT, 1, requests * per * bag_size // 2)
     out = pl.pallas_call(
         functools.partial(prepare_kernel, piece_rows),
@@ -58,13 +61,14 @@
         out_specs=[VMEM] * (1 + requests),
         scratch_shapes=[
             pltpu.VMEM((requests, per, bag_size, tables), jnp.int32),
-            pltpu.VMEM(target.shape, target.dtype),
+            pltpu.VMEM((requests * per, width), target.dtype),
+            pltpu.VMEM((requests * per, width), jnp.float32),
             pltpu.SemaphoreType.DMA((2,)),
         ],
         compiler_params=pltpu.CompilerParams(vmem_limit_bytes=8 << 20),
         cost_estimate=pl.CostEstimate(flops=3 * 10**10, bytes_accessed=4 * 10**7, transcendentals=0),
         name="prepare",
-    )(me, *in_hbm(jnp.transpose(bag_ids, (0, 1, 3, 2)), target))
+    )(me, *in_hbm(jnp.transpose(bag_ids, (0, 1, 3, 2)), target.reshape(-1, width)))
     return out[0], out[1:]
 
 
@@ -147,7 +151,7 @@
 def early_kernel(
     after_ref, target_ref, leaf_ids_ref, leaf_hbm, w1_hbm, w2_hbm, early_ref, w2_ref, leaf_ref, tail_ref, sems
 ):
-    requests, per, width = target_ref.shape
+    rows, width = target_ref.shape
     skip = w1_hbm.shape[0] - tail_ref.shape[0]
     moves = (
         (leaf_hbm, leaf_ref), (w1_hbm.at[pl.ds(skip, tail_ref.shape[0])], tail_ref), (w2_hbm, w2_ref),
@@ -155,7 +159,6 @@
     fetches = [pltpu.make_async_copy(source, place, sems.at[k]) for k, (source, place) in enumerate(moves)]
     for fetch in fetches:
         fetch.start()
-    rows = requests * per
     trees = leaf_ids_ref.shape[2]
     total = leaf_ref.shape[0]
     leaves = total // trees
@@ -166,19 +169,19 @@
     chosen = jnp.where(wide == leaf, 1.0, 0.0).astype(jnp.bfloat16)
     fetches[0].wait()
     leaf_vec = dot(chosen, leaf_ref[...]).astype(jnp.bfloat16)
-    own = target_ref[...].reshape(rows, width)
+    own = target_ref[...]
     fetches[1].wait()
     early_ref[...] = dot(own, tail_ref[:width, :]) + dot(leaf_vec, tail_ref[width:, :])
     fetches[2].wait()
 
 
 def early_part(after, target, leaf_ids, leaf_rows, w_first, w_second):
-    requests, per, width = target.shape
+    rows, width = target.shape
     hidden = w_first.shape[1]
     return pl.pallas_call(
         early_kernel,
         out_shape=[
-            jax.ShapeDtypeStruct((requests * per, hidden), jnp.float32),
+            jax.ShapeDtypeStruct((rows, hidden), jnp.float32),
             pltpu.VMEM(w_second.shape, w_second.dtype),
         ],
         in_specs=[HBM, VMEM, VMEM] + [HBM] * 3,
@@ -337,7 +340,7 @@
     with jax.named_scope("attention"):
         interest, w_head = attend(queries, events, lengths, w_query, w_key, w_pair, a_out, w_first)
         leaf_rows = leaf_table.reshape(-1, leaf_table.shape[2])
-        early, w2 = early_part(interest[0], target, leaf_ids, leaf_rows, w_first, w_second)
+        early, w2 = early_part(interest[0], target.reshape(-1, target.shape[2]), leaf_ids, leaf_rows, w_first, w_second)
         w_out, early = lax.optimization_barrier((w_out, early))
         interest = swap(interest)
     with jax.named_scope("scoring"):

time: 33.8 us -> 33.8 us (level)
  no operation moved by 1% of the time
where the time goes in v6:
time: 33.8 us; the launch traced here: 33.5 us
  starting transfers between devices  14 us (41%)
  Pallas kernels  13.3 us (39%)
  waiting for transfers between devices  5.34 us (16%)
  between operations  0.84 us (2%)
    all_to_all x1, starting transfers between devices, on_device(): lax.all_to_all(outgoing, ALL, split_axis=0, concat_axis=0, tiled=True)  6.97 us
    all_to_all x1, waiting for transfers between devices, on_device(): lax.all_to_all(outgoing, ALL, split_axis=0, concat_axis=0, tiled=True)  4.49 us
    ppermute x6, starting transfers between devices, swap(): lax.ppermute(blocks[k], 'cand', [(i, i ^ k) for i in range(size)])  3.96 us
    pallas_call x1, Pallas kernels, pool(): pl.pallas_call(functools.partial(pool_kernel, bag_size), out_shape=[jax.S...  3.72 us
    pallas_call x1, Pallas kernels, attend(): pl.pallas_call(functools.partial(attend_kernel, parts, 8, min(256, events...  3.34 us
    all_to_all x1, starting transfers between devices, on_device(): lax.all_to_all(pair_sums, ALL, split_axis=0, concat_axis=0, tiled=True)  2.58 us
    pallas_call x1, Pallas kernels, score(): pl.pallas_call(functools.partial(score_kernel, parts), out_shape=jax.Shap...  2.45 us
    pallas_call x1, Pallas kernels, early_part(): pl.pallas_call(early_kernel, out_shape=[jax.ShapeDtypeStruct((rows, hidde...  2.05 us
  transfers between devices with their start and end apart: 9, of which 2 were waited for; matrix products, arithmetic and copies ran while one was open for 0% of the time, Pallas kernels for 32%

profile of v6, /device:TPU:0, one launch (start us, length us, event | category | flops | bytes accessed | tf_op | source)
XLA Modules:
  0.0 33.5 jit_solution(13290863018776705241)
XLA Ops:
  0.0 0.5 %collective-permute-start = (bf16[8192,128]{1,0:T(8,128)(2,1)}, bf16[8192,128]{1,0:T(8,128)(2,1)}, u32[]{:S(2)}, u32[]{:S(2)}) collective-permute-start(bf16[8192,128]{1,0:T(8,128)(2,1)} %bitcast.11), channel_id=1, source_target_pairs={{0,1},{1,0},{2,3},{3,2},{4,5},{5,4},{6,7},{7,6},{8,9},{9,8},{10,11... | collective-permute-start | bytes 6291464 | tf_op jit(solution)/shard_map/sending/ppermute | solution.py:332
  0.5 0.0 copy-start.2
  0.5 1.8 %prepare.1 = (s32[32,1,64]{2,1,0:T(1,128)}, bf16[8,256]{1,0:T(8,128)(2,1)S(1)}, bf16[8,256]{1,0:T(8,128)(2,1)S(1)}, bf16[8,256]{1,0:T(8,128)(2,1)S(1)}, bf16[8,256]{1,0:T(8,128)(2,1)S(1)}) custom-call(s32[1]{0:T(128)} %bitcast.me_ref, s32[4,8,4,8]{3,2,1,0:T(4,128)} %bitcast.16, bf16[32,256]{1,0:T(8,128)(2,1)} %bitcast.9), custom_call_target="tpu_custom_call" | custom-call | flops 30000001024 | bytes 40000000 | tf_op jit(solution)/shard_map/sending/prepare/pallas_call | solution.py:56
  2.2 7.0 %all-to-all-start = ((s32[32,1,64]{2,1,0:T(1,128)}), s32[32,1,64]{2,1,0:T(1,128)S(1)}, u32[]{:S(2)}, u32[]{:S(2)}) async-start(s32[32,1,64]{2,1,0:T(1,128)} %get-tuple-element.26), calls=%async_computation | async-start | bytes 32768 | tf_op jit(solution)/shard_map/sending/all_to_all | solution.py:335
  9.2 0.3 collective-permute-start.1
  9.5 1.7 %collective-permute-start.2 = (bf16[8,256]{1,0:T(8,128)(2,1)S(1)}, bf16[8,256]{1,0:T(8,128)(2,1)S(1)}, u32[]{:S(2)}, u32[]{:S(2)}) collective-permute-start(bf16[8,256]{1,0:T(8,128)(2,1)S(1)} %get-tuple-element.30), channel_id=1, source_target_pairs={{0,2},{1,3},{2,0},{3,1},{4,6},{5,7},{6,4},{7,5},{8,10},{9,11},{10,... | collective-permute-start | bytes 12296 | tf_op jit(solution)/shard_map/sending/ppermute | solution.py:320
  11.2 0.0 collective-permute-start.3
  11.8 4.5 %all-to-all-done.ids_ref = s32[32,1,64]{2,1,0:T(1,128)S(1)} async-done(((s32[32,1,64]{2,1,0:T(1,128)}), s32[32,1,64]{2,1,0:T(1,128)S(1)}, u32[]{:S(2)}, u32[]{:S(2)}) %all-to-all-start) | async-done | bytes 8224 | tf_op jit(solution)/shard_map/sending/all_to_all | solution.py:335
  16.3 0.0 collective-permute-done.far_hbm
  16.3 0.0 copy-done.2
  16.3 0.0 copy-start.3
  16.4 0.0 copy-start.4
  16.4 0.0 copy-start.5
  16.4 0.0 copy-start.6
  16.4 3.7 %pool.1 = (bf16[32,16,128]{2,1,0:T(8,128)(2,1)}, bf16[1024,256]{1,0:T(8,128)(2,1)S(1)}) custom-call(s32[32,1,64]{2,1,0:T(1,128)S(1)} %all-to-all-done.ids_ref, bf16[8192,128]{1,0:T(8,128)(2,1)S(1)} %bitcast.12, bf16[8192,128]{1,0:T(8,128)(2,1)} %collective-permute-done.far_hbm, bf16[1024,256]{1,0:T(8,128)(2,1)} %bitcast.15), custom_call_target="tpu_custom_call" | custom-call | flops 30000001024 | bytes 40000000 | tf_op jit(solution)/shard_map/pooling/pool/pallas_call | solution.py:131
  20.1 0.0 collective-permute-done.1.refs_1_
  20.1 0.0 collective-permute-done.2.refs_2_
  20.1 0.0 collective-permute-done.3.refs_3_
  20.1 2.6 %all-to-all-start.1 = ((bf16[32,16,128]{2,1,0:T(8,128)(2,1)}), bf16[32,16,128]{2,1,0:T(8,128)(2,1)S(1)}, u32[]{:S(2)}, u32[]{:S(2)}) async-start(bf16[32,16,128]{2,1,0:T(8,128)(2,1)} %get-tuple-element.32), calls=%async_computation.1 | async-start | bytes 262144 | tf_op jit(solution)/shard_map/pooling/all_to_all | solution.py:339
  22.7 0.0 copy-done.3
  22.7 0.0 copy-done.4
  22.8 0.0 copy-done.5
  22.8 0.0 copy-done.6
  22.8 0.0 copy-start
  22.8 0.0 copy-start.1
  22.8 3.3 %attend.1 = (bf16[8,256]{1,0:T(8,128)(2,1)S(1)}, bf16[8,256]{1,0:T(8,128)(2,1)S(1)}, bf16[8,256]{1,0:T(8,128)(2,1)S(1)}, bf16[8,256]{1,0:T(8,128)(2,1)S(1)}, bf16[1024,1024]{1,0:T(8,128)(2,1)S(1)}) custom-call(s32[1,1]{1,0:T(1,128)} %bitcast.8.len_ref, bf16[8,256]{1,0:T(8,128)(2,1)S(1)} %get-tuple-element.33.refs_0_, ...), custom_call_target="tpu_custom_call" | custom-call | flops 32000000000 | bytes 40000000 | tf_op jit(solution)/shard_map/attention/attend/pallas_call | solution.py:244
  26.1 0.2 collective-permute-start.4
  26.3 1.7 %collective-permute-start.5 = (bf16[8,256]{1,0:T(8,128)(2,1)S(1)}, bf16[8,256]{1,0:T(8,128)(2,1)S(1)}, u32[]{:S(2)}, u32[]{:S(2)}) collective-permute-start(bf16[8,256]{1,0:T(8,128)(2,1)S(1)} %get-tuple-element.40), channel_id=1, source_target_pairs={{0,2},{1,3},{2,0},{3,1},{4,6},{5,7},{6,4},{7,5},{8,10},{9,11},{10,... | collective-permute-start | bytes 12296 | tf_op jit(solution)/shard_map/attention/ppermute | solution.py:320
  28.0 0.1 collective-permute-start.6
  28.1 0.0 copy-done
  28.1 0.0 copy-done.1
  28.1 0.0 copy-start.7
  28.1 2.0 %early.1 = (f32[32,1024]{1,0:T(8,128)S(1)}, bf16[1024,512]{1,0:T(8,128)(2,1)S(1)}) custom-call(bf16[8,256]{1,0:T(8,128)(2,1)S(1)} %get-tuple-element.38.after_ref.refs_0_, bf16[32,256]{1,0:T(8,128)(2,1)S(1)} %bitcast.10, s32[4,8,64]{2,1,0:T(8,128)S(1)} %copy-done.1, bf16[2048,256]{1,0:T(8,128)(2,1)} %bitcast.14, bf16[1792,1024]{1,0:T(8,128)(2,1)} %refs_6_.3, ...), custom_call_target="tpu_custom_call" | custom-call | flops 1000000000 | bytes 1000000 | tf_op jit(solution)/shard_map/attention/early/pallas_call | solution.py:181
  30.2 0.0 copy-done.7
  30.2 0.0 collective-permute-done.4.refs_1_
  30.2 0.0 collective-permute-done.5.refs_2_
  30.2 0.8 %collective-permute-done.6.refs_3_ = bf16[8,256]{1,0:T(8,128)(2,1)S(1)} collective-permute-done((bf16[8,256]{1,0:T(8,128)(2,1)S(1)}, bf16[8,256]{1,0:T(8,128)(2,1)S(1)}, u32[]{:S(2)}, u32[]{:S(2)}) %collective-permute-start.6) | collective-permute-done | bytes 4128 | tf_op jit(solution)/shard_map/attention/ppermute | solution.py:320
  31.0 0.0 all-to-all-done.1.ret_ref
  31.0 2.5 %score.1 = f32[4,8]{1,0:T(4,128)} custom-call(s32[1]{0:T(128)} %bitcast.me_ref, bf16[32,16,128]{2,1,0:T(8,128)(2,1)S(1)} %all-to-all-done.1.ret_ref, bf16[8,256]{1,0:T(8,128)(2,1)S(1)} %get-tuple-element.38.after_ref.refs_0_, bf16[8,256]{1,0:T(8,128)(2,1)S(1)} %collective-permute-done.4.refs_1_, bf16[8,256]{1,0:T(8,128)(2,1)S(1)} %collective-permute-done.5.refs_2_, ...), custom_call_target="tpu_custom_call" | custom-call | tf_op jit(solution)/shard_map/scoring/score/pallas_call | solution.py:300
  (1 shorter events, 0.0 us)
Async XLA Ops:
  0.0 16.3 %collective-permute-start = (bf16[8192,128]{1,0:T(8,128)(2,1)}, bf16[8192,128]{1,0:T(8,128)(2,1)}, u32[]{:S(2)}, u32[]{:S(2)}) collective-permute-start(bf16[8192,128]{1,0:T(8,128)(2,1)} %bitcast.11), channel_id=1, source_target_pairs={{0,1},{1,0},{2,3},{3,2},{4,5},{5,4},{6,7},{7,6},{8,9},{9,8},{10,11... | collective-permute-start | bytes 6291464 | tf_op jit(solution)/shard_map/sending/ppermute | solution.py:332
  0.5 15.9 %copy-start.2 = (bf16[1,8192,128]{2,1,0:T(8,128)(2,1)S(1)}, bf16[1,8192,128]{2,1,0:T(8,128)(2,1)}, u32[]{:S(2)}) copy-start(bf16[1,8192,128]{2,1,0:T(8,128)(2,1)} %param.20) | copy-start | bytes 6291460
  2.2 14.1 %all-to-all-start = ((s32[32,1,64]{2,1,0:T(1,128)}), s32[32,1,64]{2,1,0:T(1,128)S(1)}, u32[]{:S(2)}, u32[]{:S(2)}) async-start(s32[32,1,64]{2,1,0:T(1,128)} %get-tuple-element.26), calls=%async_computation | async-start | bytes 32768 | tf_op jit(solution)/shard_map/sending/all_to_all | solution.py:335
  9.2 10.9 %collective-permute-start.1 = (bf16[8,256]{1,0:T(8,128)(2,1)S(1)}, bf16[8,256]{1,0:T(8,128)(2,1)S(1)}, u32[]{:S(2)}, u32[]{:S(2)}) collective-permute-start(bf16[8,256]{1,0:T(8,128)(2,1)S(1)} %get-tuple-element.29), channel_id=1, source_target_pairs={{0,1},{1,0},{2,3},{3,2},{4,5},{5,4},{6,7},{7,6},{8,9},{9,8},{10,11... | collective-permute-start | bytes 12296 | tf_op jit(solution)/shard_map/sending/ppermute | solution.py:320
  9.5 10.6 %collective-permute-start.2 = (bf16[8,256]{1,0:T(8,128)(2,1)S(1)}, bf16[8,256]{1,0:T(8,128)(2,1)S(1)}, u32[]{:S(2)}, u32[]{:S(2)}) collective-permute-start(bf16[8,256]{1,0:T(8,128)(2,1)S(1)} %get-tuple-element.30), channel_id=1, source_target_pairs={{0,2},{1,3},{2,0},{3,1},{4,6},{5,7},{6,4},{7,5},{8,10},{9,11},{10,... | collective-permute-start | bytes 12296 | tf_op jit(solution)/shard_map/sending/ppermute | solution.py:320
  11.2 8.9 %collective-permute-start.3 = (bf16[8,256]{1,0:T(8,128)(2,1)S(1)}, bf16[8,256]{1,0:T(8,128)(2,1)S(1)}, u32[]{:S(2)}, u32[]{:S(2)}) collective-permute-start(bf16[8,256]{1,0:T(8,128)(2,1)S(1)} %get-tuple-element.31), channel_id=1, source_target_pairs={{0,3},{1,2},{2,1},{3,0},{4,7},{5,6},{6,5},{7,4},{8,11},{9,10},{10,... | collective-permute-start | bytes 12296 | tf_op jit(solution)/shard_map/sending/ppermute | solution.py:320
  16.3 6.4 %copy-start.3 = (bf16[256,128]{1,0:T(8,128)(2,1)S(1)}, bf16[256,128]{1,0:T(8,128)(2,1)}, u32[]{:S(2)}) copy-start(bf16[256,128]{1,0:T(8,128)(2,1)} %refs_5_.1) | copy-start | bytes 196612
  16.4 6.4 %copy-start.4 = (bf16[256,128]{1,0:T(8,128)(2,1)S(1)}, bf16[256,128]{1,0:T(8,128)(2,1)}, u32[]{:S(2)}) copy-start(bf16[256,128]{1,0:T(8,128)(2,1)} %refs_6_.2) | copy-start | bytes 196612
  16.4 6.4 %copy-start.5 = (bf16[256,128]{1,0:T(8,128)(2,1)S(1)}, bf16[256,128]{1,0:T(8,128)(2,1)}, u32[]{:S(2)}) copy-start(bf16[256,128]{1,0:T(8,128)(2,1)} %refs_7_.1) | copy-start | bytes 196612
  16.4 6.4 %copy-start.6 = (bf16[128]{0:T(256)(128)(2,1)S(1)}, bf16[128]{0:T(256)(128)(2,1)}, u32[]{:S(2)}) copy-start(bf16[128]{0:T(256)(128)(2,1)} %param.25) | copy-start | bytes 772
  20.1 10.9 %all-to-all-start.1 = ((bf16[32,16,128]{2,1,0:T(8,128)(2,1)}), bf16[32,16,128]{2,1,0:T(8,128)(2,1)S(1)}, u32[]{:S(2)}, u32[]{:S(2)}) async-start(bf16[32,16,128]{2,1,0:T(8,128)(2,1)} %get-tuple-element.32), calls=%async_computation.1 | async-start | bytes 262144 | tf_op jit(solution)/shard_map/pooling/all_to_all | solution.py:339
  22.8 5.3 %copy-start = (bf16[4,8,256]{2,1,0:T(8,128)(2,1)S(1)}, bf16[4,8,256]{2,1,0:T(8,128)(2,1)}, u32[]{:S(2)}) copy-start(bf16[4,8,256]{2,1,0:T(8,128)(2,1)} %param.17) | copy-start | bytes 49156
  22.8 5.3 %copy-start.1 = (s32[4,8,64]{2,1,0:T(8,128)S(1)}, s32[4,8,64]{2,1,0:T(8,128)}, u32[]{:S(2)}) copy-start(s32[4,8,64]{2,1,0:T(8,128)} %leaf_ids_ref.1) | copy-start | bytes 24580
  26.1 4.0 %collective-permute-start.4 = (bf16[8,256]{1,0:T(8,128)(2,1)S(1)}, bf16[8,256]{1,0:T(8,128)(2,1)S(1)}, u32[]{:S(2)}, u32[]{:S(2)}) collective-permute-start(bf16[8,256]{1,0:T(8,128)(2,1)S(1)} %get-tuple-element.39), channel_id=1, source_target_pairs={{0,1},{1,0},{2,3},{3,2},{4,5},{5,4},{6,7},{7,6},{8,9},{9,8},{10,11... | collective-permute-start | bytes 12296 | tf_op jit(solution)/shard_map/attention/ppermute | solution.py:320
  26.3 3.9 %collective-permute-start.5 = (bf16[8,256]{1,0:T(8,128)(2,1)S(1)}, bf16[8,256]{1,0:T(8,128)(2,1)S(1)}, u32[]{:S(2)}, u32[]{:S(2)}) collective-permute-start(bf16[8,256]{1,0:T(8,128)(2,1)S(1)} %get-tuple-element.40), channel_id=1, source_target_pairs={{0,2},{1,3},{2,0},{3,1},{4,6},{5,7},{6,4},{7,5},{8,10},{9,11},{10,... | collective-permute-start | bytes 12296 | tf_op jit(solution)/shard_map/attention/ppermute | solution.py:320
  28.0 3.0 %collective-permute-start.6 = (bf16[8,256]{1,0:T(8,128)(2,1)S(1)}, bf16[8,256]{1,0:T(8,128)(2,1)S(1)}, u32[]{:S(2)}, u32[]{:S(2)}) collective-permute-start(bf16[8,256]{1,0:T(8,128)(2,1)S(1)} %get-tuple-element.41), channel_id=1, source_target_pairs={{0,3},{1,2},{2,1},{3,0},{4,7},{5,6},{6,5},{7,4},{8,11},{9,10},{10,... | collective-permute-start | bytes 12296 | tf_op jit(solution)/shard_map/attention/ppermute | solution.py:320
  28.1 2.1 %copy-start.7 = (bf16[256]{0:T(256)(128)(2,1)S(1)}, bf16[256]{0:T(256)(128)(2,1)}, u32[]{:S(2)}) copy-start(bf16[256]{0:T(256)(128)(2,1)} %param.29) | copy-start | bytes 1540

commit v7 on v6

--- a/solution.py
+++ b/solution.py
@@ -39,8 +39,8 @@
         ids = by_table[:, core * half : (core + 1) * half]
         near = ids - piece * piece_rows
         far = ids - (piece - core + 1 - core) * piece_rows
-        row = jnp.where((far >= 0) & (far < piece_rows), far + piece_rows, 2 * piece_rows)
-        row = jnp.where((near >= 0) & (near < piece_rows), near, row)
+        row = jnp.where((far >= 0) & (far < piece_rows), far, 2 * piece_rows)
+        row = jnp.where((near >= 0) & (near < piece_rows), near + piece_rows, row)
         for t in range(tables):
             ids_ref[t * SPLIT + piece] = row[t : t + 1, :]
     target_f[...] = target_ref[...].astype(jnp.float32)
@@ -88,34 +88,34 @@
                 sums[k * step + at, n : n + 1, :] = total
         return carry
 
-    lax.fori_loop(0, step, one_step, 0)
+    lax.fori_loop(0, step, one_step, 0, unroll=2)
 
 
 CHUNKS = 8
 
 
-def pool_kernel(bag_size, ids_ref, table_ref, far_hbm, history_hbm, out_ref, history_ref, *refs):
+def pool_kernel(bag_size, ids_ref, far_ref, own_hbm, history_hbm, out_ref, history_ref, *refs):
     scalars = refs[:GROUPS]
-    rows_f, far_ref, sums, id_sems, far_sems, sem = refs[GROUPS:]
+    rows_f, own_ref, sums, id_sems, own_sems, sem = refs[GROUPS:]
     step = ids_ref.shape[0] // GROUPS
-    piece_rows, width = table_ref.shape
+    piece_rows, width = far_ref.shape
     chunk = piece_rows // CHUNKS
     copies = [
         pltpu.make_async_copy(ids_ref.at[pl.ds(k * step, step)], scalar, id_sems.at[k]) for k, scalar in enumerate(scalars)
     ]
     arrivals = [
-        pltpu.make_async_copy(far_hbm.at[pl.ds(k * chunk, chunk)], far_ref.at[pl.ds(k * chunk, chunk)], far_sems.at[k])
+        pltpu.make_async_copy(own_hbm.at[pl.ds(k * chunk, chunk)], own_ref.at[pl.ds(k * chunk, chunk)], own_sems.at[k])
         for k in range(CHUNKS)
     ]
     fetch = pltpu.make_async_copy(history_hbm, history_ref, sem)
     for copy in (*copies, *arrivals):
         copy.start()
-    rows_f[:piece_rows, :] = table_ref[...].astype(jnp.float32)
+    rows_f[:piece_rows, :] = far_ref[...].astype(jnp.float32)
     rows_f[2 * piece_rows :, :] = jnp.zeros((8, width), jnp.float32)
     for k, arrival in enumerate(arrivals):
         arrival.wait()
         at = piece_rows + k * chunk
-        rows_f[at : at + chunk, :] = far_ref[k * chunk : (k + 1) * chunk, :].astype(jnp.float32)
+        rows_f[at : at + chunk, :] = own_ref[k * chunk : (k + 1) * chunk, :].astype(jnp.float32)
     fetch.start()
     for copy in copies:
         copy.wait()
@@ -124,7 +124,7 @@
     fetch.wait()
 
 
-def pool(ids, table, far_table, history, bag_size):
+def pool(ids, far_table, table, history, bag_size):
     sources, _, lanes = ids.shape
     piece_rows, width = table.shape
     shape = (sources, lanes // bag_size, width)
@@ -145,7 +145,7 @@
         compiler_params=pltpu.CompilerParams(vmem_limit_bytes=24 << 20),
         cost_estimate=pl.CostEstimate(flops=3 * 10**10, bytes_accessed=4 * 10**7, transcendentals=0),
         name="pool",
-    )(ids, table, *in_hbm(far_table, history))
+    )(ids, far_table, *in_hbm(table, history))
 
 
 def early_kernel(
@@ -334,7 +334,7 @@
         queries = swap(blocks)
         incoming = lax.all_to_all(outgoing, ALL, split_axis=0, concat_axis=0, tiled=True)
     with jax.named_scope("pooling"):
-        pair_sums, events = pool(incoming, table_piece[0], far_table, history[0], bag_ids.shape[3])
+        pair_sums, events = pool(incoming, far_table, table_piece[0], history[0], bag_ids.shape[3])
         pair_sums, queries = lax.optimization_barrier((pair_sums, queries))
         returned = lax.all_to_all(pair_sums, ALL, split_axis=0, concat_axis=0, tiled=True)
     with jax.named_scope("attention"):

time: 33.8 us -> 33.6 us (level)
  no operation moved by 1% of the time
where the time goes in v7:
time: 33.6 us; the launch traced here: 33.3 us
  starting transfers between devices  14 us (42%)
  Pallas kernels  13.1 us (39%)
  waiting for transfers between devices  5.35 us (16%)
  between operations  0.82 us (2%)
    all_to_all x1, starting transfers between devices, on_device(): lax.all_to_all(outgoing, ALL, split_axis=0, concat_axis=0, tiled=True)  6.97 us
    all_to_all x1, waiting for transfers between devices, on_device(): lax.all_to_all(outgoing, ALL, split_axis=0, concat_axis=0, tiled=True)  4.49 us
    ppermute x6, starting transfers between devices, swap(): lax.ppermute(blocks[k], 'cand', [(i, i ^ k) for i in range(size)])  3.96 us
    pallas_call x1, Pallas kernels, pool(): pl.pallas_call(functools.partial(pool_kernel, bag_size), out_shape=[jax.S...  3.66 us
    pallas_call x1, Pallas kernels, attend(): pl.pallas_call(functools.partial(attend_kernel, parts, 8, min(256, events...  3.34 us
    all_to_all x1, starting transfers between devices, on_device(): lax.all_to_all(pair_sums, ALL, split_axis=0, concat_axis=0, tiled=True)  2.58 us
    pallas_call x1, Pallas kernels, score(): pl.pallas_call(functools.partial(score_kernel, parts), out_shape=jax.Shap...  2.45 us
    pallas_call x1, Pallas kernels, early_part(): pl.pallas_call(early_kernel, out_shape=[jax.ShapeDtypeStruct((rows, hidde...  2.05 us
  transfers between devices with their start and end apart: 9, of which 2 were waited for; matrix products, arithmetic and copies ran while one was open for 0% of the time, Pallas kernels for 32%

profile of v7, /device:TPU:0, one launch (start us, length us, event | category | flops | bytes accessed | tf_op | source)
XLA Modules:
  0.0 33.3 jit_solution(14721536328524419526)
XLA Ops:
  0.0 0.5 %collective-permute-start = (bf16[8192,128]{1,0:T(8,128)(2,1)}, bf16[8192,128]{1,0:T(8,128)(2,1)S(1)}, u32[]{:S(2)}, u32[]{:S(2)}) collective-permute-start(bf16[8192,128]{1,0:T(8,128)(2,1)} %bitcast.13), channel_id=1, source_target_pairs={{0,1},{1,0},{2,3},{3,2},{4,5},{5,4},{6,7},{7,6},{8,9},{9,8},{10,11... | collective-permute-start | bytes 6291464 | tf_op jit(solution)/shard_map/sending/ppermute | solution.py:332
  0.5 1.6 %prepare.1 = (s32[32,1,64]{2,1,0:T(1,128)}, bf16[8,256]{1,0:T(8,128)(2,1)S(1)}, bf16[8,256]{1,0:T(8,128)(2,1)S(1)}, bf16[8,256]{1,0:T(8,128)(2,1)S(1)}, bf16[8,256]{1,0:T(8,128)(2,1)S(1)}) custom-call(s32[1]{0:T(128)} %bitcast.me_ref, s32[4,8,4,8]{3,2,1,0:T(4,128)} %bitcast.16, bf16[32,256]{1,0:T(8,128)(2,1)} %bitcast.9), custom_call_target="tpu_custom_call" | custom-call | flops 30000001024 | bytes 40000000 | tf_op jit(solution)/shard_map/sending/prepare/pallas_call | solution.py:56
  2.1 7.0 %all-to-all-start = ((s32[32,1,64]{2,1,0:T(1,128)}), s32[32,1,64]{2,1,0:T(1,128)S(1)}, u32[]{:S(2)}, u32[]{:S(2)}) async-start(s32[32,1,64]{2,1,0:T(1,128)} %get-tuple-element.26), calls=%async_computation | async-start | bytes 32768 | tf_op jit(solution)/shard_map/sending/all_to_all | solution.py:335
  9.0 0.3 collective-permute-start.1
  9.4 1.7 %collective-permute-start.2 = (bf16[8,256]{1,0:T(8,128)(2,1)S(1)}, bf16[8,256]{1,0:T(8,128)(2,1)S(1)}, u32[]{:S(2)}, u32[]{:S(2)}) collective-permute-start(bf16[8,256]{1,0:T(8,128)(2,1)S(1)} %get-tuple-element.30), channel_id=1, source_target_pairs={{0,2},{1,3},{2,0},{3,1},{4,6},{5,7},{6,4},{7,5},{8,10},{9,11},{10,... | collective-permute-start | bytes 12296 | tf_op jit(solution)/shard_map/sending/ppermute | solution.py:320
  11.0 0.0 collective-permute-start.3
  11.7 4.5 %all-to-all-done.ids_ref = s32[32,1,64]{2,1,0:T(1,128)S(1)} async-done(((s32[32,1,64]{2,1,0:T(1,128)}), s32[32,1,64]{2,1,0:T(1,128)S(1)}, u32[]{:S(2)}, u32[]{:S(2)}) %all-to-all-start) | async-done | bytes 8224 | tf_op jit(solution)/shard_map/sending/all_to_all | solution.py:335
  16.2 0.0 collective-permute-done.far_ref
  16.2 0.0 copy-start.2
  16.2 0.0 copy-start.3
  16.2 0.0 copy-start.4
  16.2 0.0 copy-start.5
  16.2 3.7 %pool.1 = (bf16[32,16,128]{2,1,0:T(8,128)(2,1)}, bf16[1024,256]{1,0:T(8,128)(2,1)S(1)}) custom-call(s32[32,1,64]{2,1,0:T(1,128)S(1)} %all-to-all-done.ids_ref, bf16[8192,128]{1,0:T(8,128)(2,1)S(1)} %collective-permute-done.far_ref, bf16[8192,128]{1,0:T(8,128)(2,1)} %bitcast.14, bf16[1024,256]{1,0:T(8,128)(2,1)} %bitcast.15), custom_call_target="tpu_custom_call" | custom-call | flops 30000001024 | bytes 40000000 | tf_op jit(solution)/shard_map/pooling/pool/pallas_call | solution.py:131
  19.9 0.0 collective-permute-done.1.refs_1_
  19.9 0.0 collective-permute-done.2.refs_2_
  19.9 0.0 collective-permute-done.3.refs_3_
  19.9 2.6 %all-to-all-start.1 = ((bf16[32,16,128]{2,1,0:T(8,128)(2,1)}), bf16[32,16,128]{2,1,0:T(8,128)(2,1)S(1)}, u32[]{:S(2)}, u32[]{:S(2)}) async-start(bf16[32,16,128]{2,1,0:T(8,128)(2,1)} %get-tuple-element.32), calls=%async_computation.1 | async-start | bytes 262144 | tf_op jit(solution)/shard_map/pooling/all_to_all | solution.py:339
  22.5 0.0 copy-done.2
  22.5 0.0 copy-done.3
  22.5 0.0 copy-done.4
  22.5 0.0 copy-done.5
  22.5 0.0 copy-start
  22.6 0.0 copy-start.1
  22.6 3.3 %attend.1 = (bf16[8,256]{1,0:T(8,128)(2,1)S(1)}, bf16[8,256]{1,0:T(8,128)(2,1)S(1)}, bf16[8,256]{1,0:T(8,128)(2,1)S(1)}, bf16[8,256]{1,0:T(8,128)(2,1)S(1)}, bf16[1024,1024]{1,0:T(8,128)(2,1)S(1)}) custom-call(s32[1,1]{1,0:T(1,128)} %bitcast.8.len_ref, bf16[8,256]{1,0:T(8,128)(2,1)S(1)} %get-tuple-element.33.refs_0_, ...), custom_call_target="tpu_custom_call" | custom-call | flops 32000000000 | bytes 40000000 | tf_op jit(solution)/shard_map/attention/attend/pallas_call | solution.py:244
  25.9 0.2 collective-permute-start.4
  26.1 1.7 %collective-permute-start.5 = (bf16[8,256]{1,0:T(8,128)(2,1)S(1)}, bf16[8,256]{1,0:T(8,128)(2,1)S(1)}, u32[]{:S(2)}, u32[]{:S(2)}) collective-permute-start(bf16[8,256]{1,0:T(8,128)(2,1)S(1)} %get-tuple-element.40), channel_id=1, source_target_pairs={{0,2},{1,3},{2,0},{3,1},{4,6},{5,7},{6,4},{7,5},{8,10},{9,11},{10,... | collective-permute-start | bytes 12296 | tf_op jit(solution)/shard_map/attention/ppermute | solution.py:320
  27.8 0.1 collective-permute-start.6
  27.9 0.0 copy-done
  27.9 0.0 copy-done.1
  27.9 0.0 copy-start.6
  27.9 2.0 %early.1 = (f32[32,1024]{1,0:T(8,128)S(1)}, bf16[1024,512]{1,0:T(8,128)(2,1)S(1)}) custom-call(bf16[8,256]{1,0:T(8,128)(2,1)S(1)} %get-tuple-element.38.after_ref.refs_0_, bf16[32,256]{1,0:T(8,128)(2,1)S(1)} %bitcast.10, s32[4,8,64]{2,1,0:T(8,128)S(1)} %copy-done.1, bf16[2048,256]{1,0:T(8,128)(2,1)} %bitcast.12, bf16[1792,1024]{1,0:T(8,128)(2,1)} %refs_6_.3, ...), custom_call_target="tpu_custom_call" | custom-call | flops 1000000000 | bytes 1000000 | tf_op jit(solution)/shard_map/attention/early/pallas_call | solution.py:181
  29.9 0.0 copy-done.6
  30.0 0.0 collective-permute-done.4.refs_1_
  30.0 0.0 collective-permute-done.5.refs_2_
  30.0 0.8 %collective-permute-done.6.refs_3_ = bf16[8,256]{1,0:T(8,128)(2,1)S(1)} collective-permute-done((bf16[8,256]{1,0:T(8,128)(2,1)S(1)}, bf16[8,256]{1,0:T(8,128)(2,1)S(1)}, u32[]{:S(2)}, u32[]{:S(2)}) %collective-permute-start.6) | collective-permute-done | bytes 4128 | tf_op jit(solution)/shard_map/attention/ppermute | solution.py:320
  30.8 0.0 all-to-all-done.1.ret_ref
  30.8 2.5 %score.1 = f32[4,8]{1,0:T(4,128)} custom-call(s32[1]{0:T(128)} %bitcast.me_ref, bf16[32,16,128]{2,1,0:T(8,128)(2,1)S(1)} %all-to-all-done.1.ret_ref, bf16[8,256]{1,0:T(8,128)(2,1)S(1)} %get-tuple-element.38.after_ref.refs_0_, bf16[8,256]{1,0:T(8,128)(2,1)S(1)} %collective-permute-done.4.refs_1_, bf16[8,256]{1,0:T(8,128)(2,1)S(1)} %collective-permute-done.5.refs_2_, ...), custom_call_target="tpu_custom_call" | custom-call | tf_op jit(solution)/shard_map/scoring/score/pallas_call | solution.py:300
  (1 shorter events, 0.0 us)
Async XLA Ops:
  0.0 16.2 %collective-permute-start = (bf16[8192,128]{1,0:T(8,128)(2,1)}, bf16[8192,128]{1,0:T(8,128)(2,1)S(1)}, u32[]{:S(2)}, u32[]{:S(2)}) collective-permute-start(bf16[8192,128]{1,0:T(8,128)(2,1)} %bitcast.13), channel_id=1, source_target_pairs={{0,1},{1,0},{2,3},{3,2},{4,5},{5,4},{6,7},{7,6},{8,9},{9,8},{10,11... | collective-permute-start | bytes 6291464 | tf_op jit(solution)/shard_map/sending/ppermute | solution.py:332
  2.1 14.1 %all-to-all-start = ((s32[32,1,64]{2,1,0:T(1,128)}), s32[32,1,64]{2,1,0:T(1,128)S(1)}, u32[]{:S(2)}, u32[]{:S(2)}) async-start(s32[32,1,64]{2,1,0:T(1,128)} %get-tuple-element.26), calls=%async_computation | async-start | bytes 32768 | tf_op jit(solution)/shard_map/sending/all_to_all | solution.py:335
  9.0 10.8 %collective-permute-start.1 = (bf16[8,256]{1,0:T(8,128)(2,1)S(1)}, bf16[8,256]{1,0:T(8,128)(2,1)S(1)}, u32[]{:S(2)}, u32[]{:S(2)}) collective-permute-start(bf16[8,256]{1,0:T(8,128)(2,1)S(1)} %get-tuple-element.29), channel_id=1, source_target_pairs={{0,1},{1,0},{2,3},{3,2},{4,5},{5,4},{6,7},{7,6},{8,9},{9,8},{10,11... | collective-permute-start | bytes 12296 | tf_op jit(solution)/shard_map/sending/ppermute | solution.py:320
  9.4 10.5 %collective-permute-start.2 = (bf16[8,256]{1,0:T(8,128)(2,1)S(1)}, bf16[8,256]{1,0:T(8,128)(2,1)S(1)}, u32[]{:S(2)}, u32[]{:S(2)}) collective-permute-start(bf16[8,256]{1,0:T(8,128)(2,1)S(1)} %get-tuple-element.30), channel_id=1, source_target_pairs={{0,2},{1,3},{2,0},{3,1},{4,6},{5,7},{6,4},{7,5},{8,10},{9,11},{10,... | collective-permute-start | bytes 12296 | tf_op jit(solution)/shard_map/sending/ppermute | solution.py:320
  11.0 8.9 %collective-permute-start.3 = (bf16[8,256]{1,0:T(8,128)(2,1)S(1)}, bf16[8,256]{1,0:T(8,128)(2,1)S(1)}, u32[]{:S(2)}, u32[]{:S(2)}) collective-permute-start(bf16[8,256]{1,0:T(8,128)(2,1)S(1)} %get-tuple-element.31), channel_id=1, source_target_pairs={{0,3},{1,2},{2,1},{3,0},{4,7},{5,6},{6,5},{7,4},{8,11},{9,10},{10,... | collective-permute-start | bytes 12296 | tf_op jit(solution)/shard_map/sending/ppermute | solution.py:320
  16.2 6.3 %copy-start.2 = (bf16[256,128]{1,0:T(8,128)(2,1)S(1)}, bf16[256,128]{1,0:T(8,128)(2,1)}, u32[]{:S(2)}) copy-start(bf16[256,128]{1,0:T(8,128)(2,1)} %refs_5_.1) | copy-start | bytes 196612
  16.2 6.3 %copy-start.3 = (bf16[256,128]{1,0:T(8,128)(2,1)S(1)}, bf16[256,128]{1,0:T(8,128)(2,1)}, u32[]{:S(2)}) copy-start(bf16[256,128]{1,0:T(8,128)(2,1)} %refs_6_.2) | copy-start | bytes 196612
  16.2 6.3 %copy-start.4 = (bf16[256,128]{1,0:T(8,128)(2,1)S(1)}, bf16[256,128]{1,0:T(8,128)(2,1)}, u32[]{:S(2)}) copy-start(bf16[256,128]{1,0:T(8,128)(2,1)} %refs_7_.1) | copy-start | bytes 196612
  16.2 6.3 %copy-start.5 = (bf16[128]{0:T(256)(128)(2,1)S(1)}, bf16[128]{0:T(256)(128)(2,1)}, u32[]{:S(2)}) copy-start(bf16[128]{0:T(256)(128)(2,1)} %param.25) | copy-start | bytes 772
  19.9 10.9 %all-to-all-start.1 = ((bf16[32,16,128]{2,1,0:T(8,128)(2,1)}), bf16[32,16,128]{2,1,0:T(8,128)(2,1)S(1)}, u32[]{:S(2)}, u32[]{:S(2)}) async-start(bf16[32,16,128]{2,1,0:T(8,128)(2,1)} %get-tuple-element.32), calls=%async_computation.1 | async-start | bytes 262144 | tf_op jit(solution)/shard_map/pooling/all_to_all | solution.py:339
  22.5 5.3 %copy-start = (bf16[4,8,256]{2,1,0:T(8,128)(2,1)S(1)}, bf16[4,8,256]{2,1,0:T(8,128)(2,1)}, u32[]{:S(2)}) copy-start(bf16[4,8,256]{2,1,0:T(8,128)(2,1)} %param.17) | copy-start | bytes 49156
  22.6 5.3 %copy-start.1 = (s32[4,8,64]{2,1,0:T(8,128)S(1)}, s32[4,8,64]{2,1,0:T(8,128)}, u32[]{:S(2)}) copy-start(s32[4,8,64]{2,1,0:T(8,128)} %leaf_ids_ref.1) | copy-start | bytes 24580
  25.9 4.0 %collective-permute-start.4 = (bf16[8,256]{1,0:T(8,128)(2,1)S(1)}, bf16[8,256]{1,0:T(8,128)(2,1)S(1)}, u32[]{:S(2)}, u32[]{:S(2)}) collective-permute-start(bf16[8,256]{1,0:T(8,128)(2,1)S(1)} %get-tuple-element.39), channel_id=1, source_target_pairs={{0,1},{1,0},{2,3},{3,2},{4,5},{5,4},{6,7},{7,6},{8,9},{9,8},{10,11... | collective-permute-start | bytes 12296 | tf_op jit(solution)/shard_map/attention/ppermute | solution.py:320
  26.1 3.9 %collective-permute-start.5 = (bf16[8,256]{1,0:T(8,128)(2,1)S(1)}, bf16[8,256]{1,0:T(8,128)(2,1)S(1)}, u32[]{:S(2)}, u32[]{:S(2)}) collective-permute-start(bf16[8,256]{1,0:T(8,128)(2,1)S(1)} %get-tuple-element.40), channel_id=1, source_target_pairs={{0,2},{1,3},{2,0},{3,1},{4,6},{5,7},{6,4},{7,5},{8,10},{9,11},{10,... | collective-permute-start | bytes 12296 | tf_op jit(solution)/shard_map/attention/ppermute | solution.py:320
  27.8 3.0 %collective-permute-start.6 = (bf16[8,256]{1,0:T(8,128)(2,1)S(1)}, bf16[8,256]{1,0:T(8,128)(2,1)S(1)}, u32[]{:S(2)}, u32[]{:S(2)}) collective-permute-start(bf16[8,256]{1,0:T(8,128)(2,1)S(1)} %get-tuple-element.41), channel_id=1, source_target_pairs={{0,3},{1,2},{2,1},{3,0},{4,7},{5,6},{6,5},{7,4},{8,11},{9,10},{10,... | collective-permute-start | bytes 12296 | tf_op jit(solution)/shard_map/attention/ppermute | solution.py:320
  27.9 2.1 %copy-start.6 = (bf16[256]{0:T(256)(128)(2,1)S(1)}, bf16[256]{0:T(256)(128)(2,1)}, u32[]{:S(2)}) copy-start(bf16[256]{0:T(256)(128)(2,1)} %param.29) | copy-start | bytes 1540

commit v8 on v7

--- a/solution.py
+++ b/solution.py
@@ -26,7 +26,8 @@
     requests, per, bag_size, tables = bag_hbm.shape
     block_refs = refs[:requests]
     bag_ref, target_ref, target_f, sems = refs[requests:]
-    copies = [pltpu.make_async_copy(bag_hbm, bag_ref, sems.at[0]), pltpu.make_async_copy(target_hbm, target_ref, sems.at[1])]
+    copies = [pltpu.make_async_copy(bag_hbm.at[r], bag_ref.at[r], sems.at[r]) for r in range(requests)]
+    copies.append(pltpu.make_async_copy(target_hbm, target_ref, sems.at[requests]))
     for copy in copies:
         copy.start()
     for copy in copies:
@@ -63,7 +64,7 @@
             pltpu.VMEM((requests, per, bag_size, tables), jnp.int32),
             pltpu.VMEM((requests * per, width), target.dtype),
             pltpu.VMEM((requests * per, width), jnp.float32),
-            pltpu.SemaphoreType.DMA((2,)),
+            pltpu.SemaphoreType.DMA((requests + 1,)),
         ],
         compiler_params=pltpu.CompilerParams(vmem_limit_bytes=8 << 20),
         cost_estimate=pl.CostEstimate(flops=3 * 10**10, bytes_accessed=4 * 10**7, transcendentals=0),
@@ -88,7 +89,7 @@
                 sums[k * step + at, n : n + 1, :] = total
         return carry
 
-    lax.fori_loop(0, step, one_step, 0, unroll=2)
+    lax.fori_loop(0, step, one_step, 0, unroll=4)
 
 
 CHUNKS = 8

time: 33.6 us -> 33.6 us (level)
  no operation moved by 1% of the time
where the time goes in v8:
time: 33.6 us; the launch traced here: 33.2 us
  starting transfers between devices  14 us (42%)
  Pallas kernels  13.1 us (39%)
  waiting for transfers between devices  5.35 us (16%)
  between operations  0.82 us (2%)
    all_to_all x1, starting transfers between devices, on_device(): lax.all_to_all(outgoing, ALL, split_axis=0, concat_axis=0, tiled=True)  6.97 us
    all_to_all x1, waiting for transfers between devices, on_device(): lax.all_to_all(outgoing, ALL, split_axis=0, concat_axis=0, tiled=True)  4.49 us
    ppermute x6, starting transfers between devices, swap(): lax.ppermute(blocks[k], 'cand', [(i, i ^ k) for i in range(size)])  3.96 us
    pallas_call x1, Pallas kernels, pool(): pl.pallas_call(functools.partial(pool_kernel, bag_size), out_shape=[jax.S...  3.64 us
    pallas_call x1, Pallas kernels, attend(): pl.pallas_call(functools.partial(attend_kernel, parts, 8, min(256, events...  3.34 us
    all_to_all x1, starting transfers between devices, on_device(): lax.all_to_all(pair_sums, ALL, split_axis=0, concat_axis=0, tiled=True)  2.58 us
    pallas_call x1, Pallas kernels, score(): pl.pallas_call(functools.partial(score_kernel, parts), out_shape=jax.Shap...  2.45 us
    pallas_call x1, Pallas kernels, early_part(): pl.pallas_call(early_kernel, out_shape=[jax.ShapeDtypeStruct((rows, hidde...  2.05 us
  transfers between devices with their start and end apart: 9, of which 2 were waited for; matrix products, arithmetic and copies ran while one was open for 0% of the time, Pallas kernels for 32%

profile of v8, /device:TPU:0, one launch (start us, length us, event | category | flops | bytes accessed | tf_op | source)
XLA Modules:
  0.0 33.2 jit_solution(9220209418824915518)
XLA Ops:
  0.0 0.5 %collective-permute-start = (bf16[8192,128]{1,0:T(8,128)(2,1)}, bf16[8192,128]{1,0:T(8,128)(2,1)S(1)}, u32[]{:S(2)}, u32[]{:S(2)}) collective-permute-start(bf16[8192,128]{1,0:T(8,128)(2,1)} %bitcast.13), channel_id=1, source_target_pairs={{0,1},{1,0},{2,3},{3,2},{4,5},{5,4},{6,7},{7,6},{8,9},{9,8},{10,11... | collective-permute-start | bytes 6291464 | tf_op jit(solution)/shard_map/sending/ppermute | solution.py:333
  0.5 1.6 %prepare.1 = (s32[32,1,64]{2,1,0:T(1,128)}, bf16[8,256]{1,0:T(8,128)(2,1)S(1)}, bf16[8,256]{1,0:T(8,128)(2,1)S(1)}, bf16[8,256]{1,0:T(8,128)(2,1)S(1)}, bf16[8,256]{1,0:T(8,128)(2,1)S(1)}) custom-call(s32[1]{0:T(128)} %bitcast.me_ref, s32[4,8,4,8]{3,2,1,0:T(4,128)} %bitcast.16, bf16[32,256]{1,0:T(8,128)(2,1)} %bitcast.9), custom_call_target="tpu_custom_call" | custom-call | flops 30000001024 | bytes 40000000 | tf_op jit(solution)/shard_map/sending/prepare/pallas_call | solution.py:57
  2.0 7.0 %all-to-all-start = ((s32[32,1,64]{2,1,0:T(1,128)}), s32[32,1,64]{2,1,0:T(1,128)S(1)}, u32[]{:S(2)}, u32[]{:S(2)}) async-start(s32[32,1,64]{2,1,0:T(1,128)} %get-tuple-element.26), calls=%async_computation | async-start | bytes 32768 | tf_op jit(solution)/shard_map/sending/all_to_all | solution.py:336
  9.0 0.3 collective-permute-start.1
  9.3 1.7 %collective-permute-start.2 = (bf16[8,256]{1,0:T(8,128)(2,1)S(1)}, bf16[8,256]{1,0:T(8,128)(2,1)S(1)}, u32[]{:S(2)}, u32[]{:S(2)}) collective-permute-start(bf16[8,256]{1,0:T(8,128)(2,1)S(1)} %get-tuple-element.30), channel_id=1, source_target_pairs={{0,2},{1,3},{2,0},{3,1},{4,6},{5,7},{6,4},{7,5},{8,10},{9,11},{10,... | collective-permute-start | bytes 12296 | tf_op jit(solution)/shard_map/sending/ppermute | solution.py:321
  11.0 0.0 collective-permute-start.3
  11.7 4.5 %all-to-all-done.ids_ref = s32[32,1,64]{2,1,0:T(1,128)S(1)} async-done(((s32[32,1,64]{2,1,0:T(1,128)}), s32[32,1,64]{2,1,0:T(1,128)S(1)}, u32[]{:S(2)}, u32[]{:S(2)}) %all-to-all-start) | async-done | bytes 8224 | tf_op jit(solution)/shard_map/sending/all_to_all | solution.py:336
  16.2 0.0 collective-permute-done.far_ref
  16.2 0.0 copy-start.2
  16.2 0.0 copy-start.3
  16.2 0.0 copy-start.4
  16.2 0.0 copy-start.5
  16.2 3.6 %pool.1 = (bf16[32,16,128]{2,1,0:T(8,128)(2,1)}, bf16[1024,256]{1,0:T(8,128)(2,1)S(1)}) custom-call(s32[32,1,64]{2,1,0:T(1,128)S(1)} %all-to-all-done.ids_ref, bf16[8192,128]{1,0:T(8,128)(2,1)S(1)} %collective-permute-done.far_ref, bf16[8192,128]{1,0:T(8,128)(2,1)} %bitcast.14, bf16[1024,256]{1,0:T(8,128)(2,1)} %bitcast.15), custom_call_target="tpu_custom_call" | custom-call | flops 30000001024 | bytes 40000000 | tf_op jit(solution)/shard_map/pooling/pool/pallas_call | solution.py:132
  19.8 0.0 collective-permute-done.1.refs_1_
  19.9 0.0 collective-permute-done.2.refs_2_
  19.9 0.0 collective-permute-done.3.refs_3_
  19.9 2.6 %all-to-all-start.1 = ((bf16[32,16,128]{2,1,0:T(8,128)(2,1)}), bf16[32,16,128]{2,1,0:T(8,128)(2,1)S(1)}, u32[]{:S(2)}, u32[]{:S(2)}) async-start(bf16[32,16,128]{2,1,0:T(8,128)(2,1)} %get-tuple-element.32), calls=%async_computation.1 | async-start | bytes 262144 | tf_op jit(solution)/shard_map/pooling/all_to_all | solution.py:340
  22.5 0.0 copy-done.2
  22.5 0.0 copy-done.3
  22.5 0.0 copy-done.4
  22.5 0.0 copy-done.5
  22.5 0.0 copy-start
  22.5 0.0 copy-start.1
  22.5 3.3 %attend.1 = (bf16[8,256]{1,0:T(8,128)(2,1)S(1)}, bf16[8,256]{1,0:T(8,128)(2,1)S(1)}, bf16[8,256]{1,0:T(8,128)(2,1)S(1)}, bf16[8,256]{1,0:T(8,128)(2,1)S(1)}, bf16[1024,1024]{1,0:T(8,128)(2,1)S(1)}) custom-call(s32[1,1]{1,0:T(1,128)} %bitcast.8.len_ref, bf16[8,256]{1,0:T(8,128)(2,1)S(1)} %get-tuple-element.33.refs_0_, ...), custom_call_target="tpu_custom_call" | custom-call | flops 32000000000 | bytes 40000000 | tf_op jit(solution)/shard_map/attention/attend/pallas_call | solution.py:245
  25.9 0.2 collective-permute-start.4
  26.0 1.7 %collective-permute-start.5 = (bf16[8,256]{1,0:T(8,128)(2,1)S(1)}, bf16[8,256]{1,0:T(8,128)(2,1)S(1)}, u32[]{:S(2)}, u32[]{:S(2)}) collective-permute-start(bf16[8,256]{1,0:T(8,128)(2,1)S(1)} %get-tuple-element.40), channel_id=1, source_target_pairs={{0,2},{1,3},{2,0},{3,1},{4,6},{5,7},{6,4},{7,5},{8,10},{9,11},{10,... | collective-permute-start | bytes 12296 | tf_op jit(solution)/shard_map/attention/ppermute | solution.py:321
  27.7 0.1 collective-permute-start.6
  27.8 0.0 copy-done
  27.8 0.0 copy-done.1
  27.8 0.0 copy-start.6
  27.8 2.0 %early.1 = (f32[32,1024]{1,0:T(8,128)S(1)}, bf16[1024,512]{1,0:T(8,128)(2,1)S(1)}) custom-call(bf16[8,256]{1,0:T(8,128)(2,1)S(1)} %get-tuple-element.38.after_ref.refs_0_, bf16[32,256]{1,0:T(8,128)(2,1)S(1)} %bitcast.10, s32[4,8,64]{2,1,0:T(8,128)S(1)} %copy-done.1, bf16[2048,256]{1,0:T(8,128)(2,1)} %bitcast.12, bf16[1792,1024]{1,0:T(8,128)(2,1)} %refs_6_.3, ...), custom_call_target="tpu_custom_call" | custom-call | flops 1000000000 | bytes 1000000 | tf_op jit(solution)/shard_map/attention/early/pallas_call | solution.py:182
  29.9 0.0 copy-done.6
  29.9 0.0 collective-permute-done.4.refs_1_
  29.9 0.0 collective-permute-done.5.refs_2_
  29.9 0.8 %collective-permute-done.6.refs_3_ = bf16[8,256]{1,0:T(8,128)(2,1)S(1)} collective-permute-done((bf16[8,256]{1,0:T(8,128)(2,1)S(1)}, bf16[8,256]{1,0:T(8,128)(2,1)S(1)}, u32[]{:S(2)}, u32[]{:S(2)}) %collective-permute-start.6) | collective-permute-done | bytes 4128 | tf_op jit(solution)/shard_map/attention/ppermute | solution.py:321
  30.8 0.0 all-to-all-done.1.ret_ref
  30.8 2.5 %score.1 = f32[4,8]{1,0:T(4,128)} custom-call(s32[1]{0:T(128)} %bitcast.me_ref, bf16[32,16,128]{2,1,0:T(8,128)(2,1)S(1)} %all-to-all-done.1.ret_ref, bf16[8,256]{1,0:T(8,128)(2,1)S(1)} %get-tuple-element.38.after_ref.refs_0_, bf16[8,256]{1,0:T(8,128)(2,1)S(1)} %collective-permute-done.4.refs_1_, bf16[8,256]{1,0:T(8,128)(2,1)S(1)} %collective-permute-done.5.refs_2_, ...), custom_call_target="tpu_custom_call" | custom-call | tf_op jit(solution)/shard_map/scoring/score/pallas_call | solution.py:301
  (1 shorter events, 0.0 us)
Async XLA Ops:
  0.0 16.2 %collective-permute-start = (bf16[8192,128]{1,0:T(8,128)(2,1)}, bf16[8192,128]{1,0:T(8,128)(2,1)S(1)}, u32[]{:S(2)}, u32[]{:S(2)}) collective-permute-start(bf16[8192,128]{1,0:T(8,128)(2,1)} %bitcast.13), channel_id=1, source_target_pairs={{0,1},{1,0},{2,3},{3,2},{4,5},{5,4},{6,7},{7,6},{8,9},{9,8},{10,11... | collective-permute-start | bytes 6291464 | tf_op jit(solution)/shard_map/sending/ppermute | solution.py:333
  2.0 14.1 %all-to-all-start = ((s32[32,1,64]{2,1,0:T(1,128)}), s32[32,1,64]{2,1,0:T(1,128)S(1)}, u32[]{:S(2)}, u32[]{:S(2)}) async-start(s32[32,1,64]{2,1,0:T(1,128)} %get-tuple-element.26), calls=%async_computation | async-start | bytes 32768 | tf_op jit(solution)/shard_map/sending/all_to_all | solution.py:336
  9.0 10.8 %collective-permute-start.1 = (bf16[8,256]{1,0:T(8,128)(2,1)S(1)}, bf16[8,256]{1,0:T(8,128)(2,1)S(1)}, u32[]{:S(2)}, u32[]{:S(2)}) collective-permute-start(bf16[8,256]{1,0:T(8,128)(2,1)S(1)} %get-tuple-element.29), channel_id=1, source_target_pairs={{0,1},{1,0},{2,3},{3,2},{4,5},{5,4},{6,7},{7,6},{8,9},{9,8},{10,11... | collective-permute-start | bytes 12296 | tf_op jit(solution)/shard_map/sending/ppermute | solution.py:321
  9.3 10.5 %collective-permute-start.2 = (bf16[8,256]{1,0:T(8,128)(2,1)S(1)}, bf16[8,256]{1,0:T(8,128)(2,1)S(1)}, u32[]{:S(2)}, u32[]{:S(2)}) collective-permute-start(bf16[8,256]{1,0:T(8,128)(2,1)S(1)} %get-tuple-element.30), channel_id=1, source_target_pairs={{0,2},{1,3},{2,0},{3,1},{4,6},{5,7},{6,4},{7,5},{8,10},{9,11},{10,... | collective-permute-start | bytes 12296 | tf_op jit(solution)/shard_map/sending/ppermute | solution.py:321
  11.0 8.9 %collective-permute-start.3 = (bf16[8,256]{1,0:T(8,128)(2,1)S(1)}, bf16[8,256]{1,0:T(8,128)(2,1)S(1)}, u32[]{:S(2)}, u32[]{:S(2)}) collective-permute-start(bf16[8,256]{1,0:T(8,128)(2,1)S(1)} %get-tuple-element.31), channel_id=1, source_target_pairs={{0,3},{1,2},{2,1},{3,0},{4,7},{5,6},{6,5},{7,4},{8,11},{9,10},{10,... | collective-permute-start | bytes 12296 | tf_op jit(solution)/shard_map/sending/ppermute | solution.py:321
  16.2 6.3 %copy-start.2 = (bf16[256,128]{1,0:T(8,128)(2,1)S(1)}, bf16[256,128]{1,0:T(8,128)(2,1)}, u32[]{:S(2)}) copy-start(bf16[256,128]{1,0:T(8,128)(2,1)} %refs_5_.1) | copy-start | bytes 196612
  16.2 6.3 %copy-start.3 = (bf16[256,128]{1,0:T(8,128)(2,1)S(1)}, bf16[256,128]{1,0:T(8,128)(2,1)}, u32[]{:S(2)}) copy-start(bf16[256,128]{1,0:T(8,128)(2,1)} %refs_6_.2) | copy-start | bytes 196612
  16.2 6.3 %copy-start.4 = (bf16[256,128]{1,0:T(8,128)(2,1)S(1)}, bf16[256,128]{1,0:T(8,128)(2,1)}, u32[]{:S(2)}) copy-start(bf16[256,128]{1,0:T(8,128)(2,1)} %refs_7_.1) | copy-start | bytes 196612
  16.2 6.3 %copy-start.5 = (bf16[128]{0:T(256)(128)(2,1)S(1)}, bf16[128]{0:T(256)(128)(2,1)}, u32[]{:S(2)}) copy-start(bf16[128]{0:T(256)(128)(2,1)} %param.25) | copy-start | bytes 772
  19.9 10.9 %all-to-all-start.1 = ((bf16[32,16,128]{2,1,0:T(8,128)(2,1)}), bf16[32,16,128]{2,1,0:T(8,128)(2,1)S(1)}, u32[]{:S(2)}, u32[]{:S(2)}) async-start(bf16[32,16,128]{2,1,0:T(8,128)(2,1)} %get-tuple-element.32), calls=%async_computation.1 | async-start | bytes 262144 | tf_op jit(solution)/shard_map/pooling/all_to_all | solution.py:340
  22.5 5.3 %copy-start = (bf16[4,8,256]{2,1,0:T(8,128)(2,1)S(1)}, bf16[4,8,256]{2,1,0:T(8,128)(2,1)}, u32[]{:S(2)}) copy-start(bf16[4,8,256]{2,1,0:T(8,128)(2,1)} %param.17) | copy-start | bytes 49156
  22.5 5.3 %copy-start.1 = (s32[4,8,64]{2,1,0:T(8,128)S(1)}, s32[4,8,64]{2,1,0:T(8,128)}, u32[]{:S(2)}) copy-start(s32[4,8,64]{2,1,0:T(8,128)} %leaf_ids_ref.1) | copy-start | bytes 24580
  25.9 4.0 %collective-permute-start.4 = (bf16[8,256]{1,0:T(8,128)(2,1)S(1)}, bf16[8,256]{1,0:T(8,128)(2,1)S(1)}, u32[]{:S(2)}, u32[]{:S(2)}) collective-permute-start(bf16[8,256]{1,0:T(8,128)(2,1)S(1)} %get-tuple-element.39), channel_id=1, source_target_pairs={{0,1},{1,0},{2,3},{3,2},{4,5},{5,4},{6,7},{7,6},{8,9},{9,8},{10,11... | collective-permute-start | bytes 12296 | tf_op jit(solution)/shard_map/attention/ppermute | solution.py:321
  26.0 3.9 %collective-permute-start.5 = (bf16[8,256]{1,0:T(8,128)(2,1)S(1)}, bf16[8,256]{1,0:T(8,128)(2,1)S(1)}, u32[]{:S(2)}, u32[]{:S(2)}) collective-permute-start(bf16[8,256]{1,0:T(8,128)(2,1)S(1)} %get-tuple-element.40), channel_id=1, source_target_pairs={{0,2},{1,3},{2,0},{3,1},{4,6},{5,7},{6,4},{7,5},{8,10},{9,11},{10,... | collective-permute-start | bytes 12296 | tf_op jit(solution)/shard_map/attention/ppermute | solution.py:321
  27.7 3.0 %collective-permute-start.6 = (bf16[8,256]{1,0:T(8,128)(2,1)S(1)}, bf16[8,256]{1,0:T(8,128)(2,1)S(1)}, u32[]{:S(2)}, u32[]{:S(2)}) collective-permute-start(bf16[8,256]{1,0:T(8,128)(2,1)S(1)} %get-tuple-element.41), channel_id=1, source_target_pairs={{0,3},{1,2},{2,1},{3,0},{4,7},{5,6},{6,5},{7,4},{8,11},{9,10},{10,... | collective-permute-start | bytes 12296 | tf_op jit(solution)/shard_map/attention/ppermute | solution.py:321
  27.8 2.1 %copy-start.6 = (bf16[256]{0:T(256)(128)(2,1)S(1)}, bf16[256]{0:T(256)(128)(2,1)}, u32[]{:S(2)}) copy-start(bf16[256]{0:T(256)(128)(2,1)} %param.29) | copy-start | bytes 1540
